TPU v7x, 32 devices: a whole 2x2x4 slice. The times are simulated.
32 devices in a mesh: dp: 8 (over z, y), expert: 4 (over x, core).
Axes of the slice: x: 2, y: 2, z: 4, core: 2. Of those that a mesh axis runs over, the one named last changes fastest.
Arguments:
- tokens: bfloat16 [16384, 1024], P(('dp', 'expert')), may hold values from -6 to 6
- cotangent: bfloat16 [16384, 1024], P(('dp', 'expert')), may hold values from -6 to 6
- gain_one: float32 [1024], replicated, may hold values from 0.25 to 1.75
- w_query: bfloat16 [1024, 1024], P('dp'), may hold values from -0.1875 to 0.1875
- w_key: bfloat16 [1024, 1024], P('dp'), may hold values from -0.1875 to 0.1875
- w_value: bfloat16 [1024, 1024], P('dp'), may hold values from -0.1875 to 0.1875
- w_out: bfloat16 [1024, 1024], P('dp'), may hold values from -1.5 to 1.5
- rel_table: float32 [32, 16], replicated, may hold values from -4 to 4
- gain_two: float32 [1024], replicated, may hold values from 0.25 to 1.75
- w_router: bfloat16 [1024, 4], replicated, may hold values from -0.125 to 0.125
- w_gate: bfloat16 [4, 1024, 2816], P(None, 'dp'), may hold values from -0.1875 to 0.1875
- w_up: bfloat16 [4, 1024, 2816], P(None, 'dp'), may hold values from -0.1875 to 0.1875
- w_down: bfloat16 [4, 2816, 1024], P(None, 'dp'), may hold values from -0.4375 to 0.4375
- expert_ids: int32 [16384, 2], P(('dp', 'expert')), may hold values from 0 to 3, as said below
- slot_index: int32 [16384, 2], P(('dp', 'expert')), may hold values from 0 to 1279, as said below
- slot_kept: int32 [16384, 2], P(('dp', 'expert')), may hold values from 0 to 1, as said below
- seq_bucket: int32 [32], P(('dp', 'expert')), may hold values 0 or 1
Outputs:
- block_out: bfloat16 [16384, 1024], P(('dp', 'expert'))
- input_grad: float32 [16384, 1024], P(('dp', 'expert'))
- gain_one_grad: float32 [1024], replicated
- query_grad: float32 [1024, 1024], P('dp')
- key_grad: float32 [1024, 1024], P('dp')
- value_grad: float32 [1024, 1024], P('dp')
- out_grad: float32 [1024, 1024], P('dp')
- table_grad: float32 [32, 16], replicated
- gain_two_grad: float32 [1024], replicated
- router_grad: float32 [1024, 4], replicated
- gate_grad: float32 [4, 1024, 2816], P(None, 'dp')
- up_grad: float32 [4, 1024, 2816], P(None, 'dp')
- down_grad: float32 [4, 2816, 1024], P(None, 'dp')
Inputs may be any that keep to these rules, and one draw needn't show every extreme that they name: `expert_ids`: each token names two different experts. `slot_index`: A kept pair of a token on the device at index d of expert has a slot s with d * 80 <= s % 320 < (d + 1) * 80; within one dp index no two kept pairs share an expert and a slot; a dropped pair has slot 0. `slot_kept`: 1 where the pair holds its slot, 0 where it is dropped.
All inputs are finite; a program needn't handle non-finite values. No bound on the sum of `seq_bucket` on one device may be relied on, other than what follows from the above.
Results may differ from a plain program's by a relative error of at most 0.017.
Values may be sent and summed in bfloat16 or wider, within the bound.
No kernel may reach another device: no remote copies, remote signals or barrier semaphores. Data moves between devices by JAX's collectives and lax.ppermute only.
A program may use at most 704 MiB of HBM per device.

v0:
```python
import math

import jax
import jax.numpy as jnp
import numpy as np
from jax import lax
from jax.sharding import PartitionSpec as P

D = 1024
H = 16
HEAD = 64
EXPERTS = 4
BUCKETS = 32
LONG = 512
SHORT = 128


EPSILON = 1e-06


def bucket_table(length):
    offsets = np.arange(-(length - 1), length)
    distance = np.abs(offsets)
    half_count = BUCKETS // 2
    exact_count = half_count // 2
    widened = np.maximum(distance, 1)
    far_bucket = exact_count + np.floor(
        np.log(widened / exact_count) / np.log(128.0 / exact_count) * (half_count - exact_count)
    ).astype(np.int32)
    far_bucket = np.minimum(far_bucket, half_count - 1)
    inside = np.where(distance < exact_count, distance, far_bucket)
    return (np.where(offsets > 0, half_count, 0) + inside).astype(np.int32)


def position_index(length):
    places = np.arange(length)
    return bucket_table(length)[places[None, :] - places[:, None] + length - 1]


def make_bias(rel_table):
    return jnp.transpose(rel_table[position_index(LONG)], (2, 0, 1))


def block_masks(flags):
    groups = jnp.arange(LONG, dtype=jnp.int32) // SHORT
    same_seq = groups[:, None] == groups[None, :]
    return jnp.logical_or(same_seq[None], (flags == 0)[:, None, None])


def matmul(left, right):
    return jnp.dot(left, right, preferred_element_type=jnp.float32)


def attention_weights(w_query, w_key, w_value, w_out):
    return (
        lax.all_gather(w_query, "dp", axis=0, tiled=True),
        lax.all_gather(w_key, "dp", axis=0, tiled=True),
        lax.all_gather(w_value, "dp", axis=0, tiled=True),
        lax.all_gather(w_out, "dp", axis=0, tiled=True),
    )


def send_owners(values):
    return lax.all_to_all(values, "expert", split_axis=0, concat_axis=0, tiled=True)


def send_tokens(values):
    return lax.all_to_all(values, "expert", split_axis=0, concat_axis=0, tiled=True)


def gather_slots(values):
    return lax.all_gather(values, "dp", axis=0, tiled=True)


def slot_sum(term_fn, rows):
    return lax.psum_scatter(
        term_fn(jnp.int32(0), lax.axis_size("dp") * rows), "dp", scatter_dimension=0, tiled=True
    )


def norm_backward(grad_rows, row_data, inverse, gain_vec):
    scaled = grad_rows * gain_vec
    inner_mean = jnp.mean(scaled * row_data, -1, keepdims=True)
    grad_input = inverse * scaled - row_data * inverse * inverse * inverse * inner_mean
    return (grad_input, jnp.sum(grad_rows * row_data * inverse, 0))


def body(
    tokens,
    cotangent,
    gain_one,
    w_query,
    w_key,
    w_value,
    w_out,
    rel_table,
    gain_two,
    w_router,
    w_gate,
    w_up,
    w_down,
    expert_ids,
    slot_index,
    slot_kept,
    seq_bucket,
):
    tok_count = tokens.shape[0]
    blocks = tok_count // LONG
    score_scale = 1.0 / math.sqrt(HEAD)
    head_shape = (blocks, LONG, H, HEAD)
    score_bias = make_bias(rel_table)
    allowed = block_masks(seq_bucket)
    row_one = tokens.astype(jnp.float32)
    inv_one = lax.rsqrt(jnp.mean(row_one * row_one, -1, keepdims=True) + EPSILON)
    normed = (row_one * inv_one * gain_one).astype(jnp.bfloat16)
    full_query, full_key, full_value, full_out = attention_weights(w_query, w_key, w_value, w_out)
    query_rows = matmul(normed, full_query).astype(jnp.bfloat16).reshape(head_shape)
    key_rows = matmul(normed, full_key).astype(jnp.bfloat16).reshape(head_shape)
    value_rows = matmul(normed, full_value).astype(jnp.bfloat16).reshape(head_shape)

    def scores_of(query_block, key_block, allowed_block):
        scores = jnp.einsum(
            "qhd,khd->hqk", query_block, key_block, preferred_element_type=jnp.float32
        )
        scores = scores * score_scale + score_bias
        return jnp.where(allowed_block[None], scores, -1e30)

    def attend_forward(inputs):
        query_block, key_block, value_block, allowed_block = inputs
        scores = scores_of(query_block, key_block, allowed_block)
        highest = jnp.max(scores, -1, keepdims=True)
        log_total = highest + jnp.log(jnp.sum(jnp.exp(scores - highest), -1, keepdims=True))
        weights = jnp.exp(scores - log_total).astype(jnp.bfloat16)
        context_block = jnp.einsum(
            "hqk,khd->qhd", weights, value_block, preferred_element_type=jnp.float32
        )
        return (context_block.astype(jnp.bfloat16), log_total)

    context, log_totals = lax.map(attend_forward, (query_rows, key_rows, value_rows, allowed))
    context = context.reshape(tok_count, D)
    mid_rows = row_one + matmul(context, full_out)
    inv_two = lax.rsqrt(jnp.mean(mid_rows * mid_rows, -1, keepdims=True) + EPSILON)
    normed_two = (mid_rows * inv_two * gain_two).astype(jnp.bfloat16)
    logits = matmul(normed_two, w_router)
    raised = jnp.exp(logits - jnp.max(logits, -1, keepdims=True))
    router = raised / jnp.sum(raised, -1, keepdims=True)
    chosen = (expert_ids[:, :, None] == jnp.arange(EXPERTS, dtype=jnp.int32)).astype(jnp.float32)
    kept_pair = slot_kept.astype(jnp.float32)
    gate_vals = jnp.sum(chosen * router[:, None, :], -1) * kept_pair
    device = lax.axis_index("expert")
    owner_count = lax.axis_size("expert")
    slot_quota = 5 * tok_count // (2 * EXPERTS * owner_count)
    slot_span = owner_count * slot_quota
    slot_room = owner_count * EXPERTS * slot_quota
    pair_count = 2 * tok_count
    local_slot = (
        (slot_index // slot_span * EXPERTS + expert_ids) * slot_quota
        + slot_index % slot_span
        - device * slot_quota
    )
    target = jnp.where(slot_kept == 1, local_slot, slot_room).reshape(-1)
    pair_of_slot = (
        jnp.full((slot_room + 1,), pair_count, jnp.int32)
        .at[target]
        .set(jnp.arange(pair_count, dtype=jnp.int32))[:slot_room]
    )
    token_of_slot = jnp.where(pair_of_slot < pair_count, pair_of_slot // 2, tok_count)
    zero_row = jnp.zeros((1, D), jnp.bfloat16)
    outgoing = jnp.concatenate([normed_two, zero_row], 0)[token_of_slot].reshape(
        owner_count, EXPERTS * slot_quota, D
    )
    slot_rows = send_owners(outgoing).reshape(owner_count, EXPERTS, slot_quota, D)
    results = []
    gate_slice, up_slice = (
        lax.all_to_all(w_gate, "dp", split_axis=2, concat_axis=1, tiled=True),
        lax.all_to_all(w_up, "dp", split_axis=2, concat_axis=1, tiled=True),
    )
    group_rows = gather_slots(slot_rows)
    group_total = group_rows.shape[0] * slot_quota
    for expert_num in range(EXPERTS):
        rows_all = group_rows[:, expert_num].reshape(group_total, D)
        hidden_part = (
            jax.nn.gelu(matmul(rows_all, gate_slice[expert_num]))
            * matmul(rows_all, up_slice[expert_num])
        ).astype(jnp.bfloat16)
        down_part = w_down[expert_num]

        def down_term(start, count):
            return matmul(hidden_part, down_part)

        summed = slot_sum(down_term, slot_span)
        results.append(summed.astype(jnp.bfloat16).reshape(owner_count, slot_quota, D))
    returned = send_tokens(jnp.stack(results, 1).reshape(owner_count, EXPERTS * slot_quota, D))
    pair_values = (
        jnp.concatenate([returned.reshape(slot_room, D), zero_row], 0)[target]
        .reshape(tok_count, 2, D)
        .astype(jnp.float32)
    )
    block_out = (mid_rows + jnp.sum(pair_values * gate_vals[:, :, None], 1)).astype(jnp.bfloat16)
    grad_final = cotangent.astype(jnp.float32)
    grad_pairs = (grad_final[:, None, :] * gate_vals[:, :, None]).astype(jnp.bfloat16)
    grad_gates = jnp.sum(grad_final[:, None, :] * pair_values, -1) * kept_pair
    grad_router = jnp.sum(chosen * grad_gates[:, :, None], 1)
    grad_logits = (
        router * (grad_router - jnp.sum(router * grad_router, -1, keepdims=True))
    ).astype(jnp.bfloat16)
    router_local = matmul(normed_two.T, grad_logits)
    grad_normed_two = matmul(grad_logits, w_router.T)
    pair_rows = jnp.concatenate([grad_pairs.reshape(pair_count, D), zero_row], 0)[pair_of_slot]
    slot_grads = send_owners(pair_rows.reshape(owner_count, EXPERTS * slot_quota, D))
    slot_grads = slot_grads.reshape(owner_count, EXPERTS, slot_quota, D)
    back_rows = []
    group_grads = gather_slots(slot_grads)
    gate_parts = []
    up_parts = []
    down_parts = []
    for expert_num in range(EXPERTS):
        rows_all = group_rows[:, expert_num].reshape(group_total, D)
        grads_all = group_grads[:, expert_num].reshape(group_total, D)
        gate_here = gate_slice[expert_num]
        up_here = up_slice[expert_num]
        lifted = matmul(rows_all, up_here)
        activated, gelu_back = jax.vjp(jax.nn.gelu, matmul(rows_all, gate_here))
        hidden_part = (activated * lifted).astype(jnp.bfloat16)
        grad_hidden = matmul(grads_all, w_down[expert_num].T)
        grad_pre = gelu_back(grad_hidden * lifted)[0].astype(jnp.bfloat16)
        grad_lift = (grad_hidden * activated).astype(jnp.bfloat16)
        gate_parts.append(matmul(rows_all.T, grad_pre))
        up_parts.append(matmul(rows_all.T, grad_lift))
        down_parts.append(matmul(hidden_part.T, grads_all))

        def input_term(start, count):
            return matmul(grad_pre, gate_here.T) + matmul(grad_lift, up_here.T)

        summed = slot_sum(input_term, slot_span)
        back_rows.append(summed.astype(jnp.bfloat16).reshape(owner_count, slot_quota, D))
    sums = (
        lax.psum(jnp.stack(gate_parts, 0).astype(jnp.bfloat16), "expert").astype(jnp.float32),
        lax.psum(jnp.stack(up_parts, 0).astype(jnp.bfloat16), "expert").astype(jnp.float32),
        lax.psum(jnp.stack(down_parts, 0).astype(jnp.bfloat16), "expert").astype(jnp.float32),
    )
    gate_out, up_out = (
        lax.all_to_all(
            sums[0].astype(jnp.bfloat16), "dp", split_axis=1, concat_axis=2, tiled=True
        ).astype(jnp.float32),
        lax.all_to_all(
            sums[1].astype(jnp.bfloat16), "dp", split_axis=1, concat_axis=2, tiled=True
        ).astype(jnp.float32),
    )
    down_out = sums[2]
    returned_grads = send_tokens(
        jnp.stack(back_rows, 1).reshape(owner_count, EXPERTS * slot_quota, D)
    )
    routed_grads = jnp.concatenate([returned_grads.reshape(slot_room, D), zero_row], 0)[
        target
    ].reshape(tok_count, 2, D)
    grad_normed_two = grad_normed_two + jnp.sum(routed_grads.astype(jnp.float32), 1)
    grad_mid_norm, gain_two_local = norm_backward(grad_normed_two, mid_rows, inv_two, gain_two)
    grad_mid = grad_final + grad_mid_norm
    back_query, back_key, back_value, back_out = attention_weights(w_query, w_key, w_value, w_out)
    grad_branch = grad_mid.astype(jnp.bfloat16)
    out_local = matmul(context.T, grad_branch)
    grad_context = matmul(grad_branch, back_out.T).astype(jnp.bfloat16).reshape(head_shape)

    def attend_backward(bias_total, inputs):
        query_block, key_block, value_block, allowed_block, log_total, grad_block = inputs
        prob_rows = jnp.exp(scores_of(query_block, key_block, allowed_block) - log_total)
        weights = prob_rows.astype(jnp.bfloat16)
        grad_probs = jnp.einsum(
            "qhd,khd->hqk", grad_block, value_block, preferred_element_type=jnp.float32
        )
        grad_scores = prob_rows * (grad_probs - jnp.sum(prob_rows * grad_probs, -1, keepdims=True))
        grad_scores = grad_scores.astype(jnp.bfloat16)
        grad_value = jnp.einsum(
            "hqk,qhd->khd", weights, grad_block, preferred_element_type=jnp.float32
        )
        grad_query = (
            jnp.einsum("hqk,khd->qhd", grad_scores, key_block, preferred_element_type=jnp.float32)
            * score_scale
        )
        grad_key = (
            jnp.einsum("hqk,qhd->khd", grad_scores, query_block, preferred_element_type=jnp.float32)
            * score_scale
        )
        outputs = (
            grad_query.astype(jnp.bfloat16),
            grad_key.astype(jnp.bfloat16),
            grad_value.astype(jnp.bfloat16),
        )
        return (bias_total + grad_scores.astype(jnp.float32), outputs)

    bias_start = jnp.zeros((H, LONG, LONG), jnp.float32)
    bias_total, attn_grads = lax.scan(
        attend_backward,
        bias_start,
        (query_rows, key_rows, value_rows, allowed, log_totals, grad_context),
    )
    grad_query = attn_grads[0].reshape(tok_count, D)
    grad_key = attn_grads[1].reshape(tok_count, D)
    grad_value = attn_grads[2].reshape(tok_count, D)
    grad_normed = (
        matmul(grad_query, back_query.T)
        + matmul(grad_key, back_key.T)
        + matmul(grad_value, back_value.T)
    )
    grad_row_one, gain_one_local = norm_backward(grad_normed, row_one, inv_one, gain_one)
    input_grad = grad_mid + grad_row_one
    table_local = jax.vjp(make_bias, rel_table)[1](bias_total)[0]
    shares = (
        lax.psum_scatter(
            matmul(normed.T, grad_query), ("dp", "expert"), scatter_dimension=0, tiled=True
        ),
        lax.psum_scatter(
            matmul(normed.T, grad_key), ("dp", "expert"), scatter_dimension=0, tiled=True
        ),
        lax.psum_scatter(
            matmul(normed.T, grad_value), ("dp", "expert"), scatter_dimension=0, tiled=True
        ),
        lax.psum_scatter(out_local, ("dp", "expert"), scatter_dimension=0, tiled=True),
    )
    query_grad, key_grad, value_grad, out_grad = (
        lax.all_gather(shares[0].astype(jnp.bfloat16), "expert", axis=0, tiled=True).astype(
            jnp.float32
        ),
        lax.all_gather(shares[1].astype(jnp.bfloat16), "expert", axis=0, tiled=True).astype(
            jnp.float32
        ),
        lax.all_gather(shares[2].astype(jnp.bfloat16), "expert", axis=0, tiled=True).astype(
            jnp.float32
        ),
        lax.all_gather(shares[3].astype(jnp.bfloat16), "expert", axis=0, tiled=True).astype(
            jnp.float32
        ),
    )
    gain_one_grad, gain_two_grad, router_grad, table_grad = lax.psum(
        (gain_one_local, gain_two_local, router_local, table_local), ("dp", "expert")
    )
    return (
        block_out,
        input_grad,
        gain_one_grad,
        query_grad,
        key_grad,
        value_grad,
        out_grad,
        table_grad,
        gain_two_grad,
        router_grad,
        gate_out,
        up_out,
        down_out,
    )


def solution(mesh):
    placed = (
        P(("dp", "expert"), None),
        P(("dp", "expert"), None),
        P(),
        P("dp", None),
        P("dp", None),
        P("dp", None),
        P("dp", None),
        P(),
        P(),
        P(),
        P(None, "dp", None),
        P(None, "dp", None),
        P(None, "dp", None),
        P(("dp", "expert"), None),
        P(("dp", "expert"), None),
        P(("dp", "expert"), None),
        P(("dp", "expert")),
    )
    return jax.shard_map(
        body,
        mesh=mesh,
        in_specs=placed,
        out_specs=(
            P(("dp", "expert"), None),
            P(("dp", "expert"), None),
            P(),
            P("dp", None),
            P("dp", None),
            P("dp", None),
            P("dp", None),
            P(),
            P(),
            P(),
            P(None, "dp", None),
            P(None, "dp", None),
            P(None, "dp", None),
        ),
        check_vma=False,
    )
```

profile of v0, /device:TPU:0, one launch (start us, length us, event | category | flops | bytes accessed | tf_op | source)
XLA Modules:
  0.0 5701.5 jit_solution(16896603929180266955)
XLA Ops:
  21.6 860.0 %gather_fusion = f32[262144,16]{1,0:T(8,128)} fusion(f32[32,16]{1,0:T(8,128)S(1)} %copy.238, s32[262144]{0:T(1024)S(1)} %broadcast_clamp_fusion), kind=kCustom, calls=%fused_computation | custom fusion | bytes 34603008 | tf_op jit(solution)/shard_map/gather | solution.py:41
  881.7 72.7 %copy.240 = f32[512,512,16]{0,1,2:T(8,128)} copy(f32[512,512,16]{2,1,0:T(8,128)} %bitcast.4) | data formatting | bytes 33554432 | tf_op jit(solution)/shard_map/gather | solution.py:41
  970.6 16.4 fusion.162
  1014.7 36.6 all_to_all.68
  1070.3 36.1 all_to_all.69
  1122.5 79.4 %all-to-all-done.1 = bf16[4,128,2816]{1,0,2:T(4,128)(2,1)S(1)} async-done(((bf16[4,128,2816]{1,0,2:T(4,128)(2,1)}), bf16[4,128,2816]{1,0,2:T(4,128)(2,1)S(1)}, u32[]{:S(2)}, u32[]{:S(2)}) %all-to-all-start.1) | async-done | bytes 2883616 | tf_op jit(solution)/shard_map/all_to_all | solution.py:175
  1203.4 12.2 all-to-all-start.2
  1220.4 82.1 %all-to-all-done.2 = bf16[4,128,2816]{1,0,2:T(4,128)(2,1)S(1)} async-done(((bf16[4,128,2816]{1,0,2:T(4,128)(2,1)}), bf16[4,128,2816]{1,0,2:T(4,128)(2,1)S(1)}, u32[]{:S(2)}, u32[]{:S(2)}) %all-to-all-start.2) | async-done | bytes 2883616 | tf_op jit(solution)/shard_map/all_to_all | solution.py:176
  1304.2 212.0 %all-gather.15.cloned.1.call-done = bf16[32,4,80,1024]{3,2,1,0:T(8,128)(2,1)} async-done(((bf16[4,4,80,1024]{3,2,1,0:T(8,128)(2,1)}), bf16[32,4,80,1024]{3,2,1,0:T(8,128)(2,1)}) %all-gather.15.cloned.1.call-update) | async-done | bytes 20971536 | tf_op jit(solution)/shard_map/all_gather | solution.py:72
  1516.2 14.9 fusion.165
  1539.0 380.4 %all-gather.17.cloned.1.call-done = bf16[32,4,80,1024]{3,2,1,0:T(8,128)(2,1)} async-done(((bf16[4,4,80,1024]{3,2,1,0:T(8,128)(2,1)}), bf16[32,4,80,1024]{3,2,1,0:T(8,128)(2,1)}) %all-gather.17.cloned.1.call-update) | async-done | bytes 20971536 | tf_op jit(solution)/shard_map/all_gather | solution.py:72
  1919.4 15.7 fusion.164
  2088.3 40.9 reduce-scatter.23.cloned.1.call-done
  2130.7 179.4 %reduce-scatter.25.cloned.1.call-done = f32[320,1024]{1,0:T(8,128)} async-done(((f32[2560,1024]{1,0:T(8,128)}), f32[320,1024]{1,0:T(8,128)}) %reduce-scatter.25.cloned.1.call-update) | async-done | bytes 1310736 | tf_op jit(solution)/shard_map/reduce_scatter | solution.py:76
  2311.4 179.4 %reduce-scatter.21.cloned.1.call-done = f32[320,1024]{1,0:T(8,128)} async-done(((f32[2560,1024]{1,0:T(8,128)}), f32[320,1024]{1,0:T(8,128)}) %reduce-scatter.21.cloned.1.call-update) | async-done | bytes 1310736 | tf_op jit(solution)/shard_map/reduce_scatter | solution.py:76
  2492.2 179.2 %reduce-scatter.27.cloned.1.call-done = f32[320,1024]{1,0:T(8,128)} async-done(((f32[2560,1024]{1,0:T(8,128)}), f32[320,1024]{1,0:T(8,128)}) %reduce-scatter.27.cloned.1.call-update) | async-done | bytes 1310736 | tf_op jit(solution)/shard_map/reduce_scatter | solution.py:76
  2694.0 158.2 %reduce-scatter.17.cloned.1.call-done = f32[320,1024]{1,0:T(8,128)} async-done(((f32[2560,1024]{1,0:T(8,128)}), f32[320,1024]{1,0:T(8,128)}) %reduce-scatter.17.cloned.1.call-update) | async-done | bytes 1310736 | tf_op jit(solution)/shard_map/reduce_scatter | solution.py:76
  2853.6 179.2 %reduce-scatter.13.cloned.1.call-done = f32[320,1024]{1,0:T(8,128)} async-done(((f32[2560,1024]{1,0:T(8,128)}), f32[320,1024]{1,0:T(8,128)}) %reduce-scatter.13.cloned.1.call-update) | async-done | bytes 1310736 | tf_op jit(solution)/shard_map/reduce_scatter | solution.py:76
  3035.1 178.4 %reduce-scatter.19.cloned.1.call-done = f32[320,1024]{1,0:T(8,128)} async-done(((f32[2560,1024]{1,0:T(8,128)}), f32[320,1024]{1,0:T(8,128)}) %reduce-scatter.19.cloned.1.call-update) | async-done | bytes 1310736 | tf_op jit(solution)/shard_map/reduce_scatter | solution.py:76
  3215.8 178.4 %reduce-scatter.15.cloned.1.call-done = f32[320,1024]{1,0:T(8,128)} async-done(((f32[2560,1024]{1,0:T(8,128)}), f32[320,1024]{1,0:T(8,128)}) %reduce-scatter.15.cloned.1.call-update) | async-done | bytes 1310736 | tf_op jit(solution)/shard_map/reduce_scatter | solution.py:76
  3423.2 30.7 all-to-all-done.3
  3467.0 10.7 multiply_reduce_fusion.1
  3501.8 9.0 fusion.54
  3514.5 10.7 multiply_reduce_fusion
  3525.2 13.9 multiply_convert_fusion
  3547.1 36.1 all-reduce.8.cloned.1.call-done
  3600.4 73.4 %all-to-all-done.6 = bf16[4,1024,352]{2,0,1:T(4,128)(2,1)} async-done(((bf16[4,1024,352]{2,0,1:T(4,128)(2,1)}), bf16[4,1024,352]{2,0,1:T(4,128)(2,1)}, u32[]{:S(2)}, u32[]{:S(2)}) %all-to-all-start.6) | async-done | bytes 2883616 | tf_op jit(solution)/shard_map/all_to_all | solution.py:243
  3716.0 45.0 all-to-all-done.7
  3780.6 24.0 fusion.7
  3804.6 62.1 %copy.289 = f32[512,512,16]{2,1,0:T(8,128)} copy(f32[512,512,16]{0,1,2:T(8,128)} %fusion.7) | data formatting | bytes 33554432 | tf_op jit(solution)/shard_map/while/body/eval_jaxpr/convert_element_type | solution.py:290
  3866.7 1746.1 %scatter_custom_fusion.1 = f32[32,16]{1,0:T(8,128)S(1)} fusion(s32[262144]{0:T(1024)} %constant.174, f32[262144,16]{1,0:T(8,128)} %bitcast.66, f32[]{:T(128)} %constant.132.clone.1), kind=kCustom, calls=%fused_computation.228 | custom fusion | flops 4194304 | bytes 2560 | tf_op jit(solution)/shard_map/transpose(jvp())/scatter-add | solution.py:41
  5621.3 38.0 all-reduce.4
  (482 shorter events, 493.6 us)
Async XLA Ops:
  7.2 1053.5 %copy-start = (bf16[1024,4]{0,1:T(4,128)(2,1)S(1)}, bf16[1024,4]{0,1:T(4,128)(2,1)}, u32[]{:S(2)}) copy-start(bf16[1024,4]{0,1:T(4,128)(2,1)} %param.30) | copy-start | bytes 24580
  7.2 947.5 %all-gather.9.cloned.1.call-start = ((), (), s32[]{:S(2)}) async-start(), calls=%async_computation.21 | async-start | bytes 2359296 | tf_op jit(solution)/shard_map/all_gather | solution.py:56
  7.9 950.3 %all-gather.11.cloned.1.call-start = ((), (), s32[]{:S(2)}) async-start(), calls=%async_computation.22 | async-start | bytes 2359296 | tf_op jit(solution)/shard_map/all_gather | solution.py:57
  8.7 955.4 %all-gather.7.cloned.1.call-start = ((), (), s32[]{:S(2)}) async-start(), calls=%async_computation.20 | async-start | bytes 2359296 | tf_op jit(solution)/shard_map/all_gather | solution.py:58
  9.4 995.3 %all-gather.13.cloned.1.call-start = ((), (), s32[]{:S(2)}) async-start(), calls=%async_computation.23 | async-start | bytes 2359296 | tf_op jit(solution)/shard_map/all_gather | solution.py:59
  10.0 1506.2 %all-gather.15.cloned.1.call-start = ((), (), s32[]{:S(2)}) async-start(), calls=%async_computation.24 | async-start | bytes 23592960 | tf_op jit(solution)/shard_map/all_gather | solution.py:72
  1051.3 868.0 %all-gather.17.cloned.1.call-start = ((), (), s32[]{:S(2)}) async-start(), calls=%async_computation.29 | async-start | bytes 23592960 | tf_op jit(solution)/shard_map/all_gather | solution.py:72
  1110.1 91.8 %all-to-all-start.1 = ((bf16[4,128,2816]{1,0,2:T(4,128)(2,1)}), bf16[4,128,2816]{1,0,2:T(4,128)(2,1)S(1)}, u32[]{:S(2)}, u32[]{:S(2)}) async-start(bf16[4,128,2816]{1,0,2:T(4,128)(2,1)} %copy.243), calls=%async_computation.1 | async-start | bytes 5767168 | tf_op jit(solution)/shard_map/all_to_all | solution.py:175
  1203.4 99.0 %all-to-all-start.2 = ((bf16[4,128,2816]{1,0,2:T(4,128)(2,1)}), bf16[4,128,2816]{1,0,2:T(4,128)(2,1)S(1)}, u32[]{:S(2)}, u32[]{:S(2)}) async-start(bf16[4,128,2816]{1,0,2:T(4,128)(2,1)} %copy.246), calls=%async_computation.2 | async-start | bytes 5767168 | tf_op jit(solution)/shard_map/all_to_all | solution.py:176
  1215.6 913.6 %reduce-scatter.23.cloned.1.call-start = ((), (), s32[]{:S(2)}) async-start(), calls=%async_computation.31 | async-start | bytes 11796480 | tf_op jit(solution)/shard_map/reduce_scatter | solution.py:76
  1951.2 358.8 %reduce-scatter.25.cloned.1.call-start = ((), (), s32[]{:S(2)}) async-start(), calls=%async_computation.32 | async-start | bytes 11796480 | tf_op jit(solution)/shard_map/reduce_scatter | solution.py:76
  1975.4 515.4 %reduce-scatter.21.cloned.1.call-start = ((), (), s32[]{:S(2)}) async-start(), calls=%async_computation.30 | async-start | bytes 11796480 | tf_op jit(solution)/shard_map/reduce_scatter | solution.py:76
  1999.6 671.9 %reduce-scatter.27.cloned.1.call-start = ((), (), s32[]{:S(2)}) async-start(), calls=%async_computation.33 | async-start | bytes 11796480 | tf_op jit(solution)/shard_map/reduce_scatter | solution.py:76
  2025.3 826.8 %reduce-scatter.17.cloned.1.call-start = ((), (), s32[]{:S(2)}) async-start(), calls=%async_computation.27 | async-start | bytes 11796480 | tf_op jit(solution)/shard_map/reduce_scatter | solution.py:76
  2034.1 998.7 %reduce-scatter.13.cloned.1.call-start = ((), (), s32[]{:S(2)}) async-start(), calls=%async_computation.25 | async-start | bytes 11796480 | tf_op jit(solution)/shard_map/reduce_scatter | solution.py:76
  2042.8 1170.7 %reduce-scatter.19.cloned.1.call-start = ((), (), s32[]{:S(2)}) async-start(), calls=%async_computation.28 | async-start | bytes 11796480 | tf_op jit(solution)/shard_map/reduce_scatter | solution.py:76
  2051.4 1342.8 %reduce-scatter.15.cloned.1.call-start = ((), (), s32[]{:S(2)}) async-start(), calls=%async_computation.26 | async-start | bytes 11796480 | tf_op jit(solution)/shard_map/reduce_scatter | solution.py:76
  2674.7 724.0 %all-to-all-start.5 = ((bf16[4,320,1024]{2,1,0:T(8,128)(2,1)}), bf16[4,320,1024]{2,1,0:T(8,128)(2,1)S(1)}, u32[]{:S(2)}, u32[]{:S(2)}) async-start(bf16[4,320,1024]{2,1,0:T(8,128)(2,1)} %bitcast.332), calls=%async_computation.13 | async-start | bytes 5242880 | tf_op jit(solution)/shard_map/all_to_all | solution.py:68
  3398.7 55.2 all-to-all-start.3
  3403.3 179.9 %all-reduce.8.cloned.1.call-start = ((), (), s32[]{:S(2)}) async-start(), calls=%async_computation.38 | async-start | bytes 17301504 | tf_op jit(solution)/shard_map/psum | solution.py:238
  3408.5 2255.1 %reduce-scatter.35.cloned.1.call-start = ((), (), s32[]{:S(2)}) async-start(), calls=%async_computation.37 | async-start | bytes 4325376 | tf_op jit(solution)/shard_map/reduce_scatter | solution.py:319
  3496.5 2175.3 %reduce-scatter.33.cloned.1.call-start = ((), (), s32[]{:S(2)}) async-start(), calls=%async_computation.36 | async-start | bytes 4325376 | tf_op jit(solution)/shard_map/reduce_scatter | solution.py:316
  3514.4 2165.1 %reduce-scatter.29.cloned.1.call-start = ((), (), s32[]{:S(2)}) async-start(), calls=%async_computation.34 | async-start | bytes 4325376 | tf_op jit(solution)/shard_map/reduce_scatter | solution.py:310
  3588.9 84.8 %all-to-all-start.6 = ((bf16[4,1024,352]{2,0,1:T(4,128)(2,1)}), bf16[4,1024,352]{2,0,1:T(4,128)(2,1)}, u32[]{:S(2)}, u32[]{:S(2)}) async-start(bf16[4,1024,352]{2,0,1:T(4,128)(2,1)} %copy.273), calls=%async_computation.18 | async-start | bytes 6291456 | tf_op jit(solution)/shard_map/all_to_all | solution.py:243
  3673.7 87.3 %all-to-all-start.7 = ((bf16[4,1024,352]{2,0,1:T(4,128)(2,1)}), bf16[4,1024,352]{2,0,1:T(4,128)(2,1)}, u32[]{:S(2)}, u32[]{:S(2)}) async-start(bf16[4,1024,352]{2,0,1:T(4,128)(2,1)} %copy.276), calls=%async_computation.19 | async-start | bytes 6291456 | tf_op jit(solution)/shard_map/all_to_all | solution.py:246
  3681.5 2005.6 %reduce-scatter.31.cloned.1.call-start = ((), (), s32[]{:S(2)}) async-start(), calls=%async_computation.35 | async-start | bytes 4325376 | tf_op jit(solution)/shard_map/reduce_scatter | solution.py:313
  3804.6 1808.2 %copy-start.9 = (bf16[512,1024]{1,0:T(8,128)(2,1)S(1)}, bf16[512,1024]{1,0:T(8,128)(2,1)}, u32[]{:S(2)}) copy-start(bf16[512,1024]{1,0:T(8,128)(2,1)} %copy-done.8) | copy-start | bytes 3145732
  3804.6 1808.2 %copy-start.69 = (f32[512,4]{0,1:T(4,128)S(1)}, f32[512,4]{0,1:T(4,128)}, u32[]{:S(2)}) copy-start(f32[512,4]{0,1:T(4,128)} %copy-done.67) | copy-start | bytes 24580
  3804.6 1808.2 %copy-start.71 = (f32[512,4]{0,1:T(4,128)S(1)}, f32[512,4]{0,1:T(4,128)}, u32[]{:S(2)}) copy-start(f32[512,4]{0,1:T(4,128)} %copy-done.70) | copy-start | bytes 24580
  3804.6 1808.2 %copy-start.74 = (f32[512]{0:T(512)S(1)}, f32[512]{0:T(512)}, u32[]{:S(2)}) copy-start(f32[512]{0:T(512)} %copy-done.72) | copy-start | bytes 6148
  3804.6 1808.2 %copy-start.77 = (f32[512]{0:T(512)S(1)}, f32[512]{0:T(512)}, u32[]{:S(2)}) copy-start(f32[512]{0:T(512)} %copy-done.75) | copy-start | bytes 6148
  3804.6 1808.2 %copy-start.90 = (f32[512]{0:T(512)S(1)}, f32[512]{0:T(512)}, u32[]{:S(2)}) copy-start(f32[512]{0:T(512)} %copy-done.89) | copy-start | bytes 6148
  (122 other events, 1256.1 us)
Sparse Core Ops, SparseCore 0:
  10.2 51.9 all-gather.8
  64.3 47.7 all-gather.10
  114.2 47.7 all-gather.6
  164.0 47.7 all-gather.12
  1051.5 464.6 all-gather.14
  1517.6 401.7 all-gather.16
  1951.3 177.8 reduce-scatter.22
  2132.8 177.1 reduce-scatter.24
  2313.6 177.1 reduce-scatter.20
  2494.2 177.1 reduce-scatter.26
  2675.0 177.1 reduce-scatter.16
  2855.6 177.1 reduce-scatter.12
  3036.4 177.0 reduce-scatter.18
  3217.0 177.1 reduce-scatter.14
  3408.7 174.4 all-reduce.7
  3585.3 159.6 reduce-scatter.34
  3747.1 171.0 reduce-scatter.32
  3920.4 136.8 reduce-scatter.28
  4059.6 136.6 reduce-scatter.30
where the time goes:
time: 5710 us; the launch traced here: 5700 us
  waiting for transfers between devices  2220 us (39%)
  other arithmetic  1870 us (33%)
  local copies, waits for them, and re-layouts  1160 us (20%)
  matrix products  261 us (5%)
  blocking collectives  135 us (2%)
    scatter-add x1, other arithmetic, make_bias(): return jnp.transpose(rel_table[position_index(LONG)], (2, 0, 1))  1750 us
    reduce_scatter x8, waiting for transfers between devices, slot_sum(): lax.psum_scatter(term_fn(jnp.int32(0), lax.axis_size('dp') * rows), 'dp',...  1270 us
    gather x2, local copies, waits for them, and re-layouts, make_bias(): return jnp.transpose(rel_table[position_index(LONG)], (2, 0, 1))  933 us
    all_gather x2, waiting for transfers between devices, gather_slots(): return lax.all_gather(values, 'dp', axis=0, tiled=True)  592 us
    dot_general x51, matrix products, matmul(): return jnp.dot(left, right, preferred_element_type=jnp.float32)  209 us
  transfers between devices with their start and end apart: 25, of which 16 were waited for; matrix products, arithmetic and copies ran while one was open for 57% of the time, Pallas kernels for 0%

commit v1 on v0

v1 whole, which is shorter than its diff:
```python
import math

import jax
import jax.numpy as jnp
import numpy as np
from jax import lax
from jax.experimental import pallas as pl
from jax.experimental.pallas import tpu as pltpu
from jax.sharding import PartitionSpec as P

D = 1024
H = 16
HEAD = 64
EXPERTS = 4
BUCKETS = 32
LONG = 512
SHORT = 128
PAIR = 2 * HEAD
TILES = LONG // SHORT
EPSILON = 1e-06
FF_TILE = 256
LAY_TILE = 512
MIB = 1024 * 1024
MASKED = -1e30


def bucket_of(offsets):
    distance = np.abs(offsets)
    half_count = BUCKETS // 2
    exact_count = half_count // 2
    widened = np.maximum(distance, 1)
    far_bucket = exact_count + np.floor(
        np.log(widened / exact_count) / np.log(128.0 / exact_count) * (half_count - exact_count)
    ).astype(np.int32)
    far_bucket = np.minimum(far_bucket, half_count - 1)
    inside = np.where(distance < exact_count, distance, far_bucket)
    return (np.where(offsets > 0, half_count, 0) + inside).astype(np.int32)


def near_buckets():
    places = np.arange(SHORT)
    inside = places[:, None] - places[None, :]
    return np.stack([bucket_of(SHORT * step + inside) for step in (-1, 0, 1)]).reshape(-1)


def near_onehot():
    buckets = jnp.asarray(near_buckets().astype(np.int8)).astype(jnp.int32)
    return (jnp.arange(BUCKETS, dtype=jnp.int32)[:, None] == buckets[None, :]).astype(jnp.float32)


FAR_BEFORE = BUCKETS // 2 - 1
FAR_AFTER = BUCKETS - 1


def ring_order(count):
    cols = 4 if count >= 16 else 2
    rows = count // cols
    cycle = [(0, col) for col in range(cols)]
    for row in range(1, rows):
        span = range(cols - 1, 0, -1) if row % 2 else range(1, cols)
        cycle += [(row, col) for col in span]
    cycle += [(row, 0) for row in range(rows - 1, 0, -1)]
    return [row * cols + col for row, col in cycle]


def ring_tables(count):
    ring = ring_order(count)
    ahead = [(ring[i], ring[(i + 1) % count]) for i in range(count)]
    behind = [(there, here) for here, there in ahead]
    place = {index: i for i, index in enumerate(ring)}
    seats = np.asarray(
        [[ring[(place[g] + d) % count] for d in range(count)] for g in range(count)], np.int32
    )
    return ahead, behind, seats


def after(value, *others):
    return lax.optimization_barrier((value, *others))[0]


def matmul(left, right):
    return jnp.dot(left, right, preferred_element_type=jnp.float32)


def dot_dims(left, right, left_dim, right_dim):
    return lax.dot_general(
        left, right, (((left_dim,), (right_dim,)), ((), ())), preferred_element_type=jnp.float32
    )


def tie(values, others):
    values = tuple(values)
    return lax.optimization_barrier(values + tuple(others))[: len(values)]


def pick(array, index, axis=0):
    return lax.dynamic_index_in_dim(array, index, axis, keepdims=False, allow_negative_indices=False)


def lay_kernel(places, spots_ref, *refs):
    *piece_refs, out_ref = refs
    for piece_ref, place in zip(piece_refs, places):
        index = place(spots_ref)
        out_ref[index] = piece_ref[: index[-1].size]


def lay_together(spots, pieces, shape, places, tile, start=0):
    lead = (0,) * (len(shape) - 1)
    first = start // tile
    return pl.pallas_call(
        lambda *refs: lay_kernel(places, *refs),
        grid_spec=pltpu.PrefetchScalarGridSpec(
            num_scalar_prefetch=1,
            grid=(shape[-1] // tile,),
            in_specs=[
                pl.BlockSpec((piece.shape[0], tile), lambda i, spots: (0, i + first))
                for piece in pieces
            ],
            out_specs=pl.BlockSpec((*shape[:-1], tile), lambda i, spots: (*lead, i)),
        ),
        out_shape=jax.ShapeDtypeStruct(shape, jnp.bfloat16),
        compiler_params=pltpu.CompilerParams(vmem_limit_bytes=16 * MIB),
        cost_estimate=pl.CostEstimate(
            flops=0, bytes_accessed=4 * math.prod(shape), transcendentals=0
        ),
    )(spots, *pieces)


class RingGather:
    def __init__(self, block, seat):
        self.count = lax.axis_size("dp")
        self.ahead, self.behind, _ = ring_tables(self.count)
        self.seat, self.rows, self.taken = seat, block.shape[0], 0
        self.low = self.high = block
        self.mid = min((self.rows // 2 + 15) // 16 * 16, self.rows)
        self.pieces = [(block, 0, 0)]

    def arrived(self):
        return (self.low, self.high)

    def step(self, *others):
        half = self.count // 2
        if self.taken >= half:
            return
        if self.taken == 0:
            self.sent = (low,) = tie((self.low,), others)
            high = low
        else:
            self.sent = low, high = tie((self.low, self.high), others)
        self.taken += 1
        last = self.taken == half
        low, high = (low[: self.mid], high[self.mid :]) if last else (low, high)
        self.low = lax.ppermute(low, "dp", self.ahead)
        self.high = lax.ppermute(high, "dp", self.behind)
        self.pieces += [
            (self.low, (half if last else -self.taken) % self.count, 0),
            (self.high, self.taken, self.mid if last else 0),
        ]

    def finish(self, *others):
        while self.taken < self.count // 2:
            self.step()
        columns = self.pieces[0][0].shape[1]
        places = []
        for piece, step, start in self.pieces:

            def place(spots, step=step, start=start, rows=piece.shape[0]):
                return (spots[step], pl.ds(start, rows))

            places.append(place)
        out = lay_together(
            after(self.seat, *others),
            [piece for piece, _, _ in self.pieces],
            (self.count, self.rows, columns),
            places,
            columns // 2,
        )
        return out.reshape(-1, columns)


def ring_sum_kernel(received, outs, *refs):
    own_refs, received_refs = refs[:outs], refs[outs:-outs]
    side = pl.program_id(0)
    for out in range(outs):
        total = own_refs[out][...].astype(jnp.float32)
        for received_ref, (target, only) in zip(received_refs, received):
            if target == out:
                more = received_ref[...].astype(jnp.float32)
                total = total + (more if only is None else jnp.where(side == only, more, 0.0))
        refs[out - outs][...] = total.astype(jnp.bfloat16)


class RingSum:
    def __init__(self, parts, seat, entry=None):
        self.count = lax.axis_size("dp")
        self.ahead, self.behind, _ = ring_tables(self.count)
        self.seat, self.parts, self.entry, self.taken = seat, parts, entry, 0
        if entry is None:
            self.shape = (parts.shape[1], parts.shape[2] // 2)
        else:
            self.shape = (D // self.count, parts.shape[2])
        self.low = self.high = None

    def own(self, step, side=0):
        step = step % self.count
        if self.entry is None:
            return self.parts, pl.BlockSpec(
                (None, *self.shape), lambda i, seat: (seat[step], 0, i + side)
            )
        first = self.entry + side
        return self.parts, pl.BlockSpec(
            (None, *self.shape), lambda i, seat: (first + i, seat[step], 0)
        )

    def call(self, own, received, operands, others=(), halves=2, joined=False):
        moved = 2 * halves * math.prod(self.shape)

        def block(item):
            if item.shape[0] == 1:
                return pl.BlockSpec((None, *self.shape), lambda i, seat: (0, 0, 0))
            return pl.BlockSpec((None, *self.shape), lambda i, seat: (i, 0, 0))

        if joined:
            out_spec = pl.BlockSpec(self.shape, lambda i, seat: (0, i))
            out_shape = (self.shape[0], halves * self.shape[1])
        else:
            out_spec = pl.BlockSpec((None, *self.shape), lambda i, seat: (i, 0, 0))
            out_shape = (halves, *self.shape)
        return pl.pallas_call(
            lambda seat_ref, *refs: ring_sum_kernel(received, len(own), *refs),
            grid_spec=pltpu.PrefetchScalarGridSpec(
                num_scalar_prefetch=1,
                grid=(halves,),
                in_specs=[spec for _, spec in own] + [block(item) for item in operands],
                out_specs=[out_spec] * len(own),
            ),
            out_shape=[jax.ShapeDtypeStruct(out_shape, jnp.bfloat16)] * len(own),
            compiler_params=pltpu.CompilerParams(
                vmem_limit_bytes=(16 if self.entry is None else 40) * MIB
            ),
            cost_estimate=pl.CostEstimate(
                flops=2 * moved,
                bytes_accessed=moved * (len(operands) + 2 * len(own)),
                transcendentals=0,
            ),
        )(after(self.seat, *others), *(part for part, _ in own), *operands)

    def arrived(self):
        return (self.low, self.high)

    def received(self, targets):
        single = self.taken == 1
        return [(targets[0], 0 if single else None), (targets[1], 1 if single else None)]

    def step(self, *others):
        half = self.count // 2
        if self.taken >= half:
            return
        distance = half - self.taken
        if self.taken:
            received, operands = self.received((0, 1)), tie(self.arrived(), others)
            sent = self.call(self.following, received, operands)
        else:
            own = (self.own(distance), self.own(-distance, 1))
            sent = self.call(own, [], (), others, 1)
        self.low = lax.ppermute(sent[0], "dp", self.ahead)
        self.high = lax.ppermute(sent[1], "dp", self.behind)
        self.taken += 1
        distance -= 1
        steps = (distance, -distance) if distance else (0,)
        self.following = [self.own(step) for step in steps]
        self.sent = tuple(sent)

    def finish(self, *others, joined=False):
        while self.taken < self.count // 2:
            self.step()
        received, operands = self.received((0, 0)), tie(self.arrived(), others)
        return self.call(self.following, received, operands, joined=joined)[0]


def swap(value, bit):
    count = lax.axis_size("expert")
    return lax.ppermute(value, "expert", [(i, i ^ bit) for i in range(count)])


class Exchange:
    def __init__(self, own, near, far):
        self.own, self.count, self.rows = own, lax.axis_size("expert"), own.shape[0]
        self.near, self.last = swap(near, 1), None
        if self.count == 4:
            self.far = swap(far, 2)
        else:
            blocks = far.reshape(-1, self.rows, far.shape[1])
            self.far = [swap(block, bit + 2) for bit, block in enumerate(blocks)]

    def forward(self, *others):
        if self.count == 4:
            self.last = swap(after(self.far, *others)[self.rows :], 1)
        return self

    def arrived(self):
        return (self.near, self.last) if self.count == 4 else tuple(self.far)

    def together(self, seat, *others):
        if self.count == 4:
            pieces = [self.own, self.near, self.far, self.last]
        else:
            pieces = [self.own, self.near, *self.far]
        places = [
            lambda spots, d=d: (pl.ds(d * self.rows, self.rows),) for d in range(len(pieces))
        ]
        shape = (self.count * self.rows, self.own.shape[1])
        return lay_together(after(seat, *others), pieces, shape, places, LAY_TILE)


class Spread:
    def __init__(self, value):
        self.bit = lax.axis_size("expert") // 2
        self.held = {0: (value, None)}
        self.hop()

    @classmethod
    def pair(cls, both):
        spreads = cls(both[0]), cls(both[1])
        for lead, spread in enumerate(spreads):
            spread.held[0] = (both, lead)
        return spreads

    @classmethod
    def hop_own(cls, first, second, both, *others):
        swapped = swap(after(both, *others), 1)
        for lead, spread in enumerate((first, second)):
            spread.held[1] = (swapped, lead)
            spread.own_last = (swapped,)

    def hop(self, *others):
        if not self.bit:
            return
        keys = [key for key in self.held if key ^ self.bit not in self.held]
        items = [self.held[key] for key in keys]
        items = tie((item if lead is None else item[lead] for item, lead in items), others)
        fresh = {key ^ self.bit: swap(item, self.bit) for key, item in zip(keys, items)}
        self.last = tuple(fresh.values())
        self.held.update({key: (item, None) for key, item in fresh.items()})
        self.bit //= 2

    def arrived(self):
        return self.last

    def outputs(self, device, *others):
        while self.bit:
            self.hop()
        keys = sorted(self.held)
        shares = len(keys) // EXPERTS
        rows, columns = self.held[0][0].shape[-2:]
        tile = columns // 2

        def spec(lead):
            if lead is None:
                return pl.BlockSpec((rows, tile), lambda i, spots: (0, i))
            return pl.BlockSpec((None, rows, tile), lambda i, spots: (lead, 0, i))

        def kernel(spots_ref, *refs):
            *block_refs, out_ref = refs
            for first in range(0, len(keys), shares):
                total = block_refs[first][...].astype(jnp.float32)
                for block_ref in block_refs[first + 1 : first + shares]:
                    total = total + block_ref[...].astype(jnp.float32)
                out_ref[spots_ref[first]] = total

        spots = jnp.stack([device ^ key if shares == 1 else lax.div(device ^ key, shares) for key in keys])
        return pl.pallas_call(
            kernel,
            grid_spec=pltpu.PrefetchScalarGridSpec(
                num_scalar_prefetch=1,
                grid=(2,),
                in_specs=[spec(self.held[key][1]) for key in keys],
                out_specs=pl.BlockSpec((EXPERTS, rows, tile), lambda i, spots: (0, 0, i)),
            ),
            out_shape=jax.ShapeDtypeStruct((EXPERTS, rows, columns), jnp.float32),
            compiler_params=pltpu.CompilerParams(vmem_limit_bytes=24 * MIB),
            cost_estimate=pl.CostEstimate(
                flops=0, bytes_accessed=6 * EXPERTS * rows * columns, transcendentals=0
            ),
        )(after(spots, *others), *(self.held[key][0] for key in keys))


class SumAll:
    def __init__(self, parts):
        self.shapes = [part.shape for part in parts]
        self.flat = jnp.concatenate([part.reshape(-1, 128) for part in parts], 0)
        self.hops = []
        for axis in ("expert", "dp"):
            bit, count = 1, lax.axis_size(axis)
            while bit < count:
                self.hops.append((axis, [(i, i ^ bit) for i in range(count)]))
                bit *= 2
        over_x = self.hops.pop(1)
        self.hops.append(over_x)

    def hop(self, *others):
        if not self.hops:
            return self.flat
        axis, pairs = self.hops.pop(0)
        flat = after(self.flat, *others)
        self.flat = flat + lax.ppermute(flat, axis, pairs)
        return self.flat

    def finish(self, *others):
        while self.hops:
            self.hop(*others)
        sums, start = [], 0
        for shape in self.shapes:
            rows = math.prod(shape) // 128
            sums.append(self.flat[start : start + rows].reshape(shape))
            start += rows
        return sums


def norm_backward(grad_rows, row_data, inverse, gain_vec):
    scaled = grad_rows * gain_vec
    inner_mean = jnp.mean(scaled * row_data, -1, keepdims=True)
    grad_input = inverse * scaled - row_data * inverse * inverse * inverse * inner_mean
    return (grad_input, jnp.sum(grad_rows * row_data * inverse, 0))


def other_head_zeroed(rows_t, head):
    own = rows_t[head * HEAD : (head + 1) * HEAD]
    rest = jnp.zeros_like(own)
    return jnp.concatenate([own, rest] if head == 0 else [rest, own], 0)


def tile_biases(bias_ref, far_ref, pair, head, penalty):
    near = {
        -1: bias_ref[head, 0] + penalty,
        0: bias_ref[head, 1],
        1: bias_ref[head, 2] + penalty,
    }
    before = far_ref[0, 2 * pair + head] + penalty
    later = far_ref[1, 2 * pair + head] + penalty
    return lambda step: near[step] if abs(step) < 2 else (before if step < 0 else later)


def transposed(rows):
    return rows.astype(jnp.float32).T


def attend_forward_kernel(
    flag_ref, far_ref, q_ref, k_ref, v_ref, bias_ref, ctx_ref, lse_ref
):
    block, pair = pl.program_id(0), pl.program_id(1)
    penalty = jnp.where(flag_ref[block] == 0, 0.0, MASKED).astype(jnp.float32)
    query_t = (transposed(q_ref[...]) * (1.0 / math.sqrt(HEAD))).astype(jnp.bfloat16)
    value_t = transposed(v_ref[...]).astype(jnp.bfloat16)
    key_rows = k_ref[...]
    parts = []
    for head in range(2):
        bias = tile_biases(bias_ref, far_ref, pair, head, penalty)
        scores = dot_dims(key_rows, other_head_zeroed(query_t, head), 1, 0)
        value_head = value_t[head * HEAD : (head + 1) * HEAD]
        pieces = []
        for col in range(TILES):
            cols = slice(col * SHORT, (col + 1) * SHORT)
            panel = jnp.concatenate(
                [
                    scores[row * SHORT : (row + 1) * SHORT, cols] + bias(row - col)
                    for row in range(TILES)
                ],
                0,
            )
            highest = jnp.max(panel, 0, keepdims=True)
            raised = jnp.exp(panel - highest)
            total = jnp.sum(raised, 0, keepdims=True)
            piece = matmul(value_head, raised.astype(jnp.bfloat16))
            pieces.append(piece / total)
            lse_ref[0, 0, head : head + 1, cols] = highest + jnp.log(total)
        parts.append(pieces)
    for col in range(TILES):
        joined = jnp.concatenate([parts[0][col], parts[1][col]], 0)
        ctx_ref[col * SHORT : (col + 1) * SHORT, :] = joined.T.astype(jnp.bfloat16)


def attend_forward(qkv, flags, far, bias):
    tok_count = qkv.shape[0]
    blocks = tok_count // LONG
    pairs = H // 2

    def column(first):
        return pl.BlockSpec((LONG, PAIR), lambda b, p, flag: (b, first + p))

    return pl.pallas_call(
        attend_forward_kernel,
        grid_spec=pltpu.PrefetchScalarGridSpec(
            num_scalar_prefetch=1,
            grid=(blocks, pairs),
            in_specs=[
                pl.BlockSpec(memory_space=pltpu.SMEM),
                column(0),
                column(pairs),
                column(2 * pairs),
                pl.BlockSpec((2, 3, SHORT, SHORT), lambda b, p, flag: (p, 0, 0, 0)),
            ],
            out_specs=[
                column(0),
                pl.BlockSpec((1, 1, 2, LONG), lambda b, p, flag: (b, p, 0, 0)),
            ],
        ),
        out_shape=[
            jax.ShapeDtypeStruct((tok_count, D), jnp.bfloat16),
            jax.ShapeDtypeStruct((blocks, pairs, 2, LONG), jnp.float32),
        ],
        compiler_params=pltpu.CompilerParams(vmem_limit_bytes=16 * MIB),
        cost_estimate=pl.CostEstimate(
            flops=8 * H * LONG * LONG * HEAD * blocks,
            bytes_accessed=8 * tok_count * D + 12 * H * SHORT * SHORT,
            transcendentals=H * LONG * LONG * blocks,
        ),
    )(flags, far, qkv, qkv, qkv, bias)


def attend_backward_kernel(
    flag_ref,
    far_ref,
    q_ref,
    k_ref,
    v_ref,
    grad_ref,
    lse_ref,
    bias_ref,
    dq_ref,
    dk_ref,
    dv_ref,
    near_ref,
    away_ref,
    weight_scr,
    score_scr,
):
    pair, block = pl.program_id(0), pl.program_id(1)
    penalty = jnp.where(flag_ref[block] == 0, 0.0, MASKED).astype(jnp.float32)
    scaled = (q_ref[...].astype(jnp.float32) * (1.0 / math.sqrt(HEAD))).astype(jnp.bfloat16)
    query_t = transposed(scaled).astype(jnp.bfloat16)
    grad_t = transposed(grad_ref[...]).astype(jnp.bfloat16)
    key_t = transposed(k_ref[...]).astype(jnp.bfloat16)
    key_rows, value_rows, grad_rows = k_ref[...], v_ref[...], grad_ref[...]

    @pl.when(block == 0)
    def _():
        near_ref[...] = jnp.zeros_like(near_ref)
        away_ref[...] = jnp.zeros_like(away_ref)

    query_parts, key_parts, value_parts = [], [], []
    for head in range(2):
        bias = tile_biases(bias_ref, far_ref, pair, head, penalty)
        scores = dot_dims(key_rows, other_head_zeroed(query_t, head), 1, 0)
        grad_probs = dot_dims(value_rows, other_head_zeroed(grad_t, head), 1, 0)
        key_head = key_t[head * HEAD : (head + 1) * HEAD]
        near = {-1: None, 0: None, 1: None}
        away = [None, None]
        for col in range(TILES):
            cols = slice(col * SHORT, (col + 1) * SHORT)
            total = lse_ref[0, 0, head : head + 1, cols]
            probs = jnp.exp(
                jnp.concatenate(
                    [
                        scores[row * SHORT : (row + 1) * SHORT, cols] + bias(row - col)
                        for row in range(TILES)
                    ],
                    0,
                )
                - total
            )
            panel = grad_probs[:, cols]
            inner = jnp.sum(probs * panel, 0, keepdims=True)
            grad_scores = (probs * (panel - inner)).astype(jnp.bfloat16)
            weight_scr[:, cols] = probs.astype(jnp.bfloat16)
            score_scr[:, cols] = grad_scores
            rounded = grad_scores.astype(jnp.float32)
            for row in range(TILES):
                tile = rounded[row * SHORT : (row + 1) * SHORT]
                step = row - col
                if abs(step) < 2:
                    near[step] = tile if near[step] is None else near[step] + tile
                else:
                    side = 0 if step < 0 else 1
                    tile = jnp.sum(tile, 0, keepdims=True)
                    away[side] = tile if away[side] is None else away[side] + tile
        for step in (-1, 0, 1):
            near_ref[head, step + 1] += near[step]
        for side in range(2):
            away_ref[0, head, side : side + 1, :] += away[side]
        query_parts.append(matmul(key_head, score_scr[...]))
        key_parts.append(matmul(score_scr[...], scaled))
        value_parts.append(matmul(weight_scr[...], grad_rows))
    lane = lax.broadcasted_iota(jnp.int32, (LONG, PAIR), 1)
    dk_ref[...] = jnp.where(lane < HEAD, key_parts[0], key_parts[1]).astype(jnp.bfloat16)
    dv_ref[...] = jnp.where(lane < HEAD, value_parts[0], value_parts[1]).astype(jnp.bfloat16)
    joined = jnp.concatenate(query_parts, 0) * (1.0 / math.sqrt(HEAD))
    dq_ref[...] = joined.T.astype(jnp.bfloat16)


def attend_backward(qkv, grad_context, lse, flags, far, bias):
    tok_count = qkv.shape[0]
    blocks = tok_count // LONG
    pairs = H // 2

    def column(first):
        return pl.BlockSpec((LONG, PAIR), lambda p, b, flag: (b, first + p))

    rows = jax.ShapeDtypeStruct((tok_count, D), jnp.bfloat16)
    return pl.pallas_call(
        attend_backward_kernel,
        grid_spec=pltpu.PrefetchScalarGridSpec(
            num_scalar_prefetch=1,
            grid=(pairs, blocks),
            in_specs=[
                pl.BlockSpec(memory_space=pltpu.SMEM),
                column(0),
                column(pairs),
                column(2 * pairs),
                column(0),
                pl.BlockSpec((1, 1, 2, LONG), lambda p, b, flag: (b, p, 0, 0)),
                pl.BlockSpec((2, 3, SHORT, SHORT), lambda p, b, flag: (p, 0, 0, 0)),
            ],
            out_specs=[
                column(0),
                column(0),
                column(0),
                pl.BlockSpec((2, 3, SHORT, SHORT), lambda p, b, flag: (p, 0, 0, 0)),
                pl.BlockSpec((1, 2, 2, SHORT), lambda p, b, flag: (p, 0, 0, 0)),
            ],
            scratch_shapes=[
                pltpu.VMEM((LONG, LONG), jnp.bfloat16),
                pltpu.VMEM((LONG, LONG), jnp.bfloat16),
            ],
        ),
        out_shape=[
            rows,
            rows,
            rows,
            jax.ShapeDtypeStruct((H, 3, SHORT, SHORT), jnp.float32),
            jax.ShapeDtypeStruct((pairs, 2, 2, SHORT), jnp.float32),
        ],
        compiler_params=pltpu.CompilerParams(vmem_limit_bytes=24 * MIB),
        cost_estimate=pl.CostEstimate(
            flops=20 * H * LONG * LONG * HEAD * blocks,
            bytes_accessed=16 * tok_count * D + 24 * H * SHORT * SHORT,
            transcendentals=H * LONG * LONG * blocks,
        ),
    )(flags, far, qkv, qkv, qkv, grad_context, lse, bias)


ROW_TILE = 256
GELU_SCALE = math.sqrt(2.0 / math.pi)
GELU_CUBE = 0.044715


def row_tiles(rows):
    return [slice(start, min(start + ROW_TILE, rows)) for start in range(0, rows, ROW_TILE)]


def gate_kernel(rows_ref, weight_ref, act_ref, slope_ref):
    for part in row_tiles(rows_ref.shape[0]):
        pre = matmul(rows_ref[part, :], weight_ref[...])
        square = pre * pre
        angle = jnp.tanh(pre * (GELU_SCALE + (GELU_SCALE * GELU_CUBE) * square))
        half = 0.5 + 0.5 * angle
        act_ref[part, :] = (pre * half).astype(jnp.bfloat16)
        bend = (0.5 * GELU_SCALE) + (1.5 * GELU_SCALE * GELU_CUBE) * square
        slope_ref[part, :] = (half + pre * (1.0 - angle * angle) * bend).astype(jnp.bfloat16)


def up_kernel(rows_ref, weight_ref, act_ref, slope_ref, grads_ref, hid_ref, lift_ref, down_ref):
    for part in row_tiles(rows_ref.shape[0]):
        lift = matmul(rows_ref[part, :], weight_ref[...])
        hid_ref[part, :] = (act_ref[part, :].astype(jnp.float32) * lift).astype(jnp.bfloat16)
        lift_ref[part, :] = (slope_ref[part, :].astype(jnp.float32) * lift).astype(jnp.bfloat16)
    down_ref[...] = dot_dims(hid_ref[...], grads_ref[...], 0, 0).astype(jnp.bfloat16)


def hidden_back_kernel(grads_ref, down_ref, lift_ref, act_ref, rows_t_ref, out_ref):
    for part in row_tiles(grads_ref.shape[0]):
        back = dot_dims(grads_ref[part, :], down_ref[...], 1, 1)
        out_ref[0, part, :] = (back * lift_ref[part, :].astype(jnp.float32)).astype(jnp.bfloat16)
        out_ref[1, part, :] = (back * act_ref[part, :].astype(jnp.float32)).astype(jnp.bfloat16)
    rows = rows_t_ref.shape[0]
    for part in row_tiles(rows):
        out_ref[2, part, :] = matmul(rows_t_ref[part, :], out_ref[0]).astype(jnp.bfloat16)
        out_ref[3, part, :] = matmul(rows_t_ref[part, :], out_ref[1]).astype(jnp.bfloat16)
    rest = jnp.zeros((2, out_ref.shape[1] - rows, out_ref.shape[2]), jnp.bfloat16)
    out_ref[2:, rows:, :] = rest


def rows_back_kernel(pre_ref, up_ref, gate_w_ref, up_w_ref, *out_refs):
    total = dot_dims(pre_ref[...], gate_w_ref[...], 1, 1) + dot_dims(up_ref[...], up_w_ref[...], 1, 1)
    start = 0
    for out_ref in out_refs:
        rows = out_ref.shape[0]
        out_ref[...] = total[start : start + rows].astype(jnp.bfloat16)
        start += rows


def kernel_call(kernel, operands, in_specs, out_specs, out_shape, steps, flops, vmem):
    moved = sum(2 * math.prod(item.shape) for item in (*operands, *out_shape))
    return pl.pallas_call(
        kernel,
        grid=(steps,),
        in_specs=in_specs,
        out_specs=out_specs,
        out_shape=[jax.ShapeDtypeStruct(item.shape, jnp.bfloat16) for item in out_shape],
        compiler_params=pltpu.CompilerParams(vmem_limit_bytes=vmem * MIB),
        cost_estimate=pl.CostEstimate(flops=flops, bytes_accessed=moved, transcendentals=0),
    )(*operands)


def width_tiles(width):
    return pl.cdiv(width, FF_TILE)


def whole_spec(shape, buffers=2):
    return pl.BlockSpec(shape, lambda i: (0, 0), pipeline_mode=pl.Buffered(buffers))


def gate_forward(rows, weight):
    count, width = rows.shape[0], weight.shape[1]
    tile = pl.BlockSpec((count, FF_TILE), lambda i: (0, i))
    shape = jax.ShapeDtypeStruct((count, width), jnp.bfloat16)
    return kernel_call(
        gate_kernel,
        (rows, weight),
        [whole_spec(rows.shape), pl.BlockSpec((D, FF_TILE), lambda i: (0, i))],
        [tile, tile],
        [shape, shape],
        width_tiles(width),
        2 * count * D * width,
        59,
    )


def up_forward(rows, weight, act, slope, grads):
    count, width = rows.shape[0], weight.shape[1]
    tile = pl.BlockSpec((count, FF_TILE), lambda i: (0, i))
    shape = jax.ShapeDtypeStruct((count, width), jnp.bfloat16)
    return kernel_call(
        up_kernel,
        (rows, weight, act, slope, grads),
        [
            whole_spec(rows.shape),
            pl.BlockSpec((D, FF_TILE), lambda i: (0, i)),
            tile,
            tile,
            whole_spec(grads.shape),
        ],
        [tile, tile, pl.BlockSpec((FF_TILE, D), lambda i: (i, 0))],
        [shape, shape, jax.ShapeDtypeStruct((width, D), jnp.bfloat16)],
        width_tiles(width),
        4 * count * D * width,
        59,
    )


def hidden_back(grads, weight, lift, act, rows_t):
    count, width = lift.shape
    tile = pl.BlockSpec((count, FF_TILE), lambda i: (0, i))
    return kernel_call(
        hidden_back_kernel,
        (grads, weight, lift, act, rows_t),
        [
            whole_spec(grads.shape),
            pl.BlockSpec((FF_TILE, D), lambda i: (i, 0)),
            tile,
            tile,
            whole_spec(rows_t.shape),
        ],
        [pl.BlockSpec((4, count, FF_TILE), lambda i: (0, 0, i))],
        [jax.ShapeDtypeStruct((4, count, width), jnp.bfloat16)],
        width_tiles(width),
        6 * count * D * width,
        59,
    )[0]


def rows_back(hidden_grads, gate_weight, up_weight, splits):
    _, count, width = hidden_grads.shape
    weight_tile = pl.BlockSpec((ROW_TILE, width), lambda i: (i, 0))

    def entry(number):
        return pl.BlockSpec(
            (None, count, width), lambda i: (number, 0, 0), pipeline_mode=pl.Buffered(1)
        )

    return kernel_call(
        rows_back_kernel,
        (hidden_grads, hidden_grads, gate_weight, up_weight),
        [entry(0), entry(1), weight_tile, weight_tile],
        [pl.BlockSpec((rows, ROW_TILE), lambda i: (0, i)) for rows in splits],
        [jax.ShapeDtypeStruct((rows, D), jnp.bfloat16) for rows in splits],
        D // ROW_TILE,
        4 * count * D * width,
        59,
    )


def table_sums(near, away):
    near_part = lax.dot_general(
        near_onehot(),
        near.reshape(H, -1),
        (((1,), (1,)), ((), ())),
        precision=lax.Precision.HIGHEST,
        preferred_element_type=jnp.float32,
    )
    far_part = jnp.sum(away, -1).reshape(H, 2)
    sides = np.zeros((BUCKETS, 2), np.float32)
    sides[FAR_BEFORE, 0] = sides[FAR_AFTER, 1] = 1.0
    return near_part + jnp.sum(sides[:, None, :] * far_part[None], -1)


def body(
    tokens,
    cotangent,
    gain_one,
    w_query,
    w_key,
    w_value,
    w_out,
    rel_table,
    gain_two,
    w_router,
    w_gate,
    w_up,
    w_down,
    expert_ids,
    slot_index,
    slot_kept,
    seq_bucket,
):
    tok_count = tokens.shape[0]
    dp_count = lax.axis_size("dp")
    owner_count = lax.axis_size("expert")
    shares = owner_count // EXPERTS
    group = lax.axis_index("dp")
    device = lax.axis_index("expert")
    expert = device if shares == 1 else lax.div(device, shares)
    core = device & 1
    seat = pick(jnp.asarray(ring_tables(dp_count)[2]), group)

    half_rows = w_query.shape[0] // 2

    def own_half(weight):
        return lax.dynamic_slice_in_dim(
            weight, core * half_rows, half_rows, 0, allow_negative_indices=False
        )

    slot_quota = 5 * tok_count // (2 * EXPERTS * owner_count)
    slot_span = owner_count * slot_quota
    owners_each = owner_count // shares
    block_rows = owners_each * slot_quota
    slot_room = owner_count * block_rows

    def routes(ids, slots, kept):
        owner = slots // slot_span
        dest = ids * shares + owner // owners_each
        local_slot = (
            (dest ^ device) * block_rows
            + (owner % owners_each) * slot_quota
            + slots % slot_span
            - device * slot_quota
        )
        target = jnp.where(kept == 1, local_slot, slot_room)
        room = jnp.arange(slot_room, dtype=jnp.int32)
        from_slot = [
            (target[:, k : k + 1] == room[None, :]).astype(jnp.bfloat16) for k in range(2)
        ]
        to_slot = jnp.logical_or(
            target[:, 0][None, :] == room[:, None], target[:, 1][None, :] == room[:, None]
        ).astype(jnp.bfloat16)
        return from_slot, to_slot

    def parts_of(rows):
        return rows[:block_rows], rows[block_rows : 2 * block_rows], rows[2 * block_rows :]

    def outgoing(rows, to_slot):
        return [matmul(part, rows).astype(jnp.bfloat16) for part in reversed(parts_of(to_slot))][::-1]

    def route(rows):
        logits = matmul(rows, w_router)
        raised = jnp.exp(logits - jnp.max(logits, -1, keepdims=True))
        return raised / jnp.sum(raised, -1, keepdims=True)

    weight_ring = RingGather(
        jnp.concatenate([own_half(weight) for weight in (w_query, w_key, w_value, w_out)], 1), seat
    )
    weight_ring.step()
    row_one = tokens.astype(jnp.float32)
    inv_one = lax.rsqrt(jnp.mean(row_one * row_one, -1, keepdims=True) + EPSILON)
    normed = (row_one * inv_one * gain_one).astype(jnp.bfloat16)
    theirs = [swap(weight_ring.pieces[0][0], 1)]

    def weight_step(*others):
        if weight_ring.taken < dp_count // 2:
            weight_ring.step(*others)
            theirs.extend(swap(piece, 1) for piece in weight_ring.sent)

    weight_step(inv_one)
    ids, slots, kept = tie((expert_ids, slot_index, slot_kept), weight_ring.sent)
    from_slot, to_slot = routes(ids, slots, kept)
    weight_step(to_slot, theirs[0])
    cots, table = tie((cotangent, rel_table), weight_ring.sent)
    cot_blocks = outgoing(cots, to_slot)
    bias = lax.dot_general(
        after(table, *cot_blocks),
        near_onehot(),
        (((0,), (0,)), ((), ())),
        precision=lax.Precision.HIGHEST,
        preferred_element_type=jnp.float32,
    ).reshape(H, 3, SHORT, SHORT)
    far = jnp.stack([rel_table[FAR_BEFORE], rel_table[FAR_AFTER]])
    weight_step(bias, *theirs[1:3])
    while weight_ring.taken < dp_count // 2:
        weight_step()
    gate_ring = RingGather(pick(w_gate, expert), seat)
    gate_ring.step(*weight_ring.sent)
    theirs.extend(swap(piece, 1) for piece in weight_ring.arrived())
    places = []
    for side in range(2):
        for piece, step, start in weight_ring.pieces:

            def place(spots, step=step, side=side, start=start, rows=piece.shape[0]):
                return (spots[step], spots[dp_count + side], pl.ds(start, rows))

            places.append(place)
    spots = jnp.concatenate([seat, jnp.stack([core, 1 - core])])
    pieces = [piece for piece, _, _ in weight_ring.pieces] + theirs
    full_qkv = lay_together(spots, pieces, (dp_count, 2, half_rows, 3 * D), places, LAY_TILE)
    full_out = lay_together(spots, pieces, (dp_count, 2, half_rows, D), places, LAY_TILE, 3 * D)
    full_qkv, full_out = full_qkv.reshape(D, 3 * D), full_out.reshape(D, D)
    up_own, down_own = tie((pick(w_up, expert), pick(w_down, expert)), (full_qkv,))
    up_ring = RingGather(up_own, seat)
    down_ring = RingGather(down_own, seat)

    gate_ring.step(full_qkv, up_own, down_own)
    (normed_now,) = tie((normed,), gate_ring.sent)
    qkv = matmul(normed_now, full_qkv).astype(jnp.bfloat16)
    context, lse = attend_forward(qkv, seq_bucket, far, bias)
    (context,) = tie((context,), gate_ring.arrived())
    gate_ring.step(context)
    (context,) = tie((context,), gate_ring.sent)
    mid_rows = row_one + matmul(context, full_out)
    inv_two = lax.rsqrt(jnp.mean(mid_rows * mid_rows, -1, keepdims=True) + EPSILON)
    normed_two = (mid_rows * inv_two * gain_two).astype(jnp.bfloat16)
    row_blocks = outgoing(normed_two, to_slot)
    row_exchange = Exchange(*row_blocks)
    gate_ring.step(*row_blocks)
    up_ring.step(*gate_ring.sent)
    gate_full = gate_ring.finish(*up_ring.sent)
    router = route(after(normed_two, gate_full))
    chosen = (ids[:, :, None] == jnp.arange(EXPERTS, dtype=jnp.int32)).astype(jnp.float32)
    kept_pair = kept.astype(jnp.float32)
    gate_vals = jnp.sum(chosen * router[:, None, :], -1) * kept_pair
    up_ring.step(gate_vals)

    slot_rows = row_exchange.forward(*up_ring.sent).together(seat)
    cot_exchange = Exchange(*tie(cot_blocks, (slot_rows,)))
    down_ring.step(slot_rows)
    (gate_now,) = tie((gate_full,), (*down_ring.sent, cot_exchange.near))
    act, slope = gate_forward(slot_rows, gate_now)
    act, slope = tie((act, slope), up_ring.arrived())
    up_ring.step(act)
    (rows_now,) = tie((slot_rows,), up_ring.sent)
    slot_gate = lax.dynamic_index_in_dim(
        route(rows_now), expert, 1, allow_negative_indices=False
    )
    slot_rows_t = rows_now.T
    cot_exchange.forward(slot_gate, slot_rows_t, *up_ring.arrived())
    slot_cots = cot_exchange.together(seat)
    slot_grads = (slot_gate * slot_cots.astype(jnp.float32)).astype(jnp.bfloat16)
    up_ring.step(slot_gate, slot_rows_t)
    down_ring.step(*up_ring.arrived())
    up_full = up_ring.finish(*down_ring.sent, slot_grads)
    down_ring.step(up_full, slot_grads)
    (up_full,) = tie((up_full,), down_ring.sent)
    hidden, lift_slope, down_parts = up_forward(slot_rows, up_full, act, slope, slot_grads)
    hidden, lift_slope = tie((hidden, lift_slope), down_ring.arrived())
    down_ring.step(hidden)
    down_sum = RingSum(down_parts.reshape(dp_count, -1, D), seat)
    down_sum.step(*down_ring.sent)
    down_full = down_ring.finish(*down_sum.sent)

    expert_rows = matmul(hidden, down_full).astype(jnp.bfloat16)
    expert_blocks = tie(parts_of(expert_rows), down_sum.arrived())
    returned = Exchange(*expert_blocks)
    down_sum.step(expert_rows)
    (back_grads,) = tie((slot_grads,), down_sum.sent)
    hidden_grads = hidden_back(back_grads, down_full, lift_slope, act, slot_rows_t)
    (hidden_grads,) = tie(
        (hidden_grads,),
        (*down_sum.arrived(), returned.near, *(returned.arrived() if owner_count > 4 else (returned.far,))),
    )
    returned.forward(hidden_grads)
    gate_up_sum = RingSum(hidden_grads, seat, 2)
    gate_up_sum.step(hidden_grads)
    down_sum.step(*gate_up_sum.sent, *returned.arrived())
    (hidden_now,) = tie((hidden_grads,), (*down_sum.sent, *gate_up_sum.sent))
    splits = (block_rows, block_rows, slot_room - 2 * block_rows)
    grad_rows = rows_back(hidden_now, gate_full, up_full, splits)
    returned_grads = Exchange(*grad_rows)
    gate_up_sum.step(*grad_rows)

    returned = returned.together(seat, *gate_up_sum.sent, *down_sum.arrived())
    pair_values = [matmul(picks, returned) for picks in from_slot]
    block_out = (
        mid_rows + pair_values[0] * gate_vals[:, 0:1] + pair_values[1] * gate_vals[:, 1:2]
    ).astype(jnp.bfloat16)
    grad_final = cotangent.astype(jnp.float32)
    grad_gates = (
        jnp.stack([jnp.sum(grad_final * values, -1) for values in pair_values], 1) * kept_pair
    )
    grad_router = jnp.sum(chosen * grad_gates[:, :, None], 1)
    grad_logits = (
        router * (grad_router - jnp.sum(router * grad_router, -1, keepdims=True))
    ).astype(jnp.bfloat16)
    returned_grads.forward(grad_logits, *gate_up_sum.arrived())
    gate_up_sum.step(grad_logits)
    returned_grads = returned_grads.together(seat, *gate_up_sum.sent)
    grad_normed_two = matmul(grad_logits, w_router.T) + matmul(
        from_slot[0] + from_slot[1], returned_grads
    )
    grad_mid_norm, gain_two_local = norm_backward(grad_normed_two, mid_rows, inv_two, gain_two)
    grad_mid = grad_final + grad_mid_norm

    grad_branch = grad_mid.astype(jnp.bfloat16)
    grad_context = dot_dims(grad_branch, full_out, 1, 1).astype(jnp.bfloat16)

    def core_parts(local):
        split = local.reshape(dp_count, 2, half_rows, -1)
        return pick(split, core, 1), pick(split, 1 - core, 1)

    out_mine, out_other = core_parts(dot_dims(context, grad_branch, 0, 0).astype(jnp.bfloat16))
    (grad_context,) = tie((grad_context,), (out_mine, out_other))
    grad_query, grad_key, grad_value, near, away = attend_backward(
        qkv, grad_context, lse, seq_bucket, far, bias
    )
    down_sum.step(grad_query)
    out_other = swap(after(out_other, grad_query), 1)
    qkv_grads = jnp.concatenate([grad_query, grad_key, grad_value], 1)
    qkv_mine, qkv_other = core_parts(dot_dims(normed, qkv_grads, 0, 0).astype(jnp.bfloat16))
    gate_up_sum.step(qkv_other, qkv_mine, *down_sum.arrived())
    down_share = down_sum.finish(*gate_up_sum.sent, joined=True)
    qkv_other = swap(after(qkv_other, *gate_up_sum.sent), 1)
    down_blocks = Spread(after(down_share, *gate_up_sum.sent))
    qkv_mine, out_mine = tie((qkv_mine, out_mine), gate_up_sum.sent)
    weight_parts = jnp.concatenate(
        [
            (mine.astype(jnp.float32) + other.astype(jnp.float32)).astype(jnp.bfloat16)
            for mine, other in ((qkv_mine, qkv_other), (out_mine, out_other))
        ],
        2,
    )
    weight_sum = RingSum(weight_parts, seat)
    near, away = tie((near, away), gate_up_sum.sent)
    table_local = table_sums(near, away)
    weight_sum.step(weight_parts, table_local, *down_blocks.arrived())
    (late_grads,) = tie((qkv_grads,), weight_sum.sent)
    grad_normed = dot_dims(late_grads, full_qkv, 1, 1)
    grad_row_one, gain_one_local = norm_backward(grad_normed, row_one, inv_one, gain_one)
    input_grad = grad_mid + grad_row_one
    down_blocks.hop(*weight_sum.sent)

    gate_up_share = gate_up_sum.finish(input_grad)
    gate_blocks, up_blocks = Spread.pair(gate_up_share)
    weight_sum.step(gate_up_share, *down_blocks.arrived())
    (late_rows,) = tie((normed_two,), weight_sum.sent)
    small = SumAll((gain_one_local, table_local, gain_two_local, matmul(late_rows.T, grad_logits)))
    weight_sum.step(small.hop(*weight_sum.sent), *gate_blocks.arrived())
    Spread.hop_own(gate_blocks, up_blocks, gate_up_share, *weight_sum.sent)
    weight_sum.step(small.hop(*weight_sum.sent), *up_blocks.arrived(), *up_blocks.own_last)
    gate_blocks.hop(*weight_sum.sent)
    up_blocks.hop(*weight_sum.sent)
    down_out = down_blocks.outputs(device, *weight_sum.sent)
    rounded = weight_sum.finish(
        down_out, small.hop(*weight_sum.sent), *gate_blocks.arrived(), *up_blocks.arrived()
    )
    gate_out = gate_blocks.outputs(device, rounded, small.hop(rounded))
    up_out = up_blocks.outputs(device, gate_out)
    bit = owner_count // 2
    while bit > 1:
        arriving = after(swap(rounded, bit), gate_out, up_out)
        share = rounded.astype(jnp.float32) + arriving.astype(jnp.float32)
        rounded = share.astype(jnp.bfloat16)
        bit //= 2
    other = swap(rounded, 1)
    small.hop(rounded)
    gain_one_grad, table_grad, gain_two_grad, router_grad = small.finish()
    weight_grads = jnp.concatenate(
        [jnp.where(core == 0, rounded, other), jnp.where(core == 0, other, rounded)], 1
    ).astype(jnp.float32)
    query_grad, key_grad, value_grad, out_grad = (
        weight_grads[i // 2, :, i % 2 * D : (i % 2 + 1) * D] for i in range(4)
    )
    return (
        block_out,
        input_grad,
        gain_one_grad,
        query_grad,
        key_grad,
        value_grad,
        out_grad,
        table_grad,
        gain_two_grad,
        router_grad,
        gate_out,
        up_out,
        down_out,
    )


def solution(mesh):
    placed = (
        P(("dp", "expert"), None),
        P(("dp", "expert"), None),
        P(),
        P("dp", None),
        P("dp", None),
        P("dp", None),
        P("dp", None),
        P(),
        P(),
        P(),
        P(None, "dp", None),
        P(None, "dp", None),
        P(None, "dp", None),
        P(("dp", "expert"), None),
        P(("dp", "expert"), None),
        P(("dp", "expert"), None),
        P(("dp", "expert")),
    )
    return jax.shard_map(
        body,
        mesh=mesh,
        in_specs=placed,
        out_specs=(
            P(("dp", "expert"), None),
            P(("dp", "expert"), None),
            P(),
            P("dp", None),
            P("dp", None),
            P("dp", None),
            P("dp", None),
            P(),
            P(),
            P(),
            P(None, "dp", None),
            P(None, "dp", None),
            P(None, "dp", None),
        ),
        check_vma=False,
    )
```

time: 5710 us -> 581 us (0.10)
  waiting for transfers between devices: 2220 us -> 174 us
  other arithmetic: 1870 us -> 15 us
  local copies, waits for them, and re-layouts: 1160 us -> 59.4 us
  matrix products: 261 us -> 49 us
  Pallas kernels: 0 us -> 192 us
  blocking collectives: 135 us -> 0 us
    scatter-add x1 -> x0, other arithmetic: 1750 us -> none  [make_bias(): return jnp.transpose(rel_table[position_index(LONG)], (2, 0, 1))]
    reduce_scatter x12 -> x0, waiting for transfers between devices: 1270 us -> none  [the longest x8 1270 us: slot_sum(): lax.psum_scatter(term_fn(jnp.int32(0), lax.axis_size('dp') * rows), 'dp',...]
    gather x6 -> x0, local copies, waits for them, and re-layouts: 954 us -> none  [the longest x2 933 us: make_bias(): return jnp.transpose(rel_table[position_index(LONG)], (2, 0, 1))]
    all_gather x6 -> x0, waiting for transfers between devices: 592 us -> none  [the longest x2 592 us: gather_slots(): return lax.all_gather(values, 'dp', axis=0, tiled=True)]
    all_to_all x6 -> x0, waiting for transfers between devices: 311 us -> none  [the longest x1 82.1 us: body(): lax.all_to_all(w_up, 'dp', split_axis=2, concat_axis=1, tiled=True)]
    pallas_call x0 -> x33, Pallas kernels: none -> 192 us  [the longest x4 94.5 us: kernel_call(): pl.pallas_call(kernel, grid=(steps,), in_specs=in_specs, out_specs=out_sp...]
    dot_general x51 -> x16, matrix products: 209 us -> 30.4 us  [matmul(): return jnp.dot(left, right, preferred_element_type=jnp.float32)]
    ppermute x0 -> x94, waiting for transfers between devices: none -> 174 us  [the longest x16 71.9 us: step(): self.low = lax.ppermute(low, 'dp', self.ahead)]
  transfers between devices with their start and end apart: 25 -> 94, of which waited for: 16 -> 43; matrix products, arithmetic and copies ran while one was open for 57% -> 17% of each run, Pallas kernels for 0% -> 32%
where the time goes in v1:
time: 581 us; the launch traced here: 570 us
  Pallas kernels  192 us (33%)
  waiting for transfers between devices  174 us (30%)
  starting transfers between devices  76.7 us (13%)
  local copies, waits for them, and re-layouts  59.4 us (10%)
  matrix products  49 us (8%)
  other arithmetic  15 us (3%)
    pallas_call x4, Pallas kernels, kernel_call(): pl.pallas_call(kernel, grid=(steps,), in_specs=in_specs, out_specs=out_sp...  94.5 us
    ppermute x16, waiting for transfers between devices, step(): self.low = lax.ppermute(low, 'dp', self.ahead)  71.9 us
    ppermute x33, waiting for transfers between devices, swap(): return lax.ppermute(value, 'expert', [(i, i ^ bit) for i in range(count)])  40 us
    dot_general x16, matrix products, matmul(): return jnp.dot(left, right, preferred_element_type=jnp.float32)  30.4 us
    pallas_call x15, Pallas kernels, call(): pl.pallas_call(lambda seat_ref, *refs: ring_sum_kernel(received, len(own)...  29.4 us
    unnamed x201, local copies, waits for them, and re-layouts  26.8 us
    ppermute x5, waiting for transfers between devices, hop(): self.flat = flat + lax.ppermute(flat, axis, pairs)  25.8 us
    pallas_call x1, Pallas kernels, attend_backward(): pl.pallas_call(attend_backward_kernel, grid_spec=pltpu.PrefetchScalarGrid...  21.6 us
  transfers between devices with their start and end apart: 94, of which 43 were waited for; matrix products, arithmetic and copies ran while one was open for 17% of the time, Pallas kernels for 32%

profile of v1, /device:TPU:0, one launch (start us, length us, event | category | flops | bytes accessed | tf_op | source)
XLA Modules:
  0.0 569.8 jit_solution(14990470267970343539)
XLA Ops:
  10.8 7.2 %collective-permute-done.refs_2_ = bf16[64,4096]{1,0:T(8,128)(2,1)} collective-permute-done((bf16[64,4096]{1,0:T(8,128)(2,1)S(1)}, bf16[64,4096]{1,0:T(8,128)(2,1)}, u32[]{:S(2)}, u32[]{:S(2)}) %collective-permute-start) | collective-permute-done | bytes 524320 | tf_op jit(solution)/shard_map/ppermute | solution.py:153
  22.4 9.8 %collective-permute-done.2.refs_4_ = bf16[64,4096]{1,0:T(8,128)(2,1)} collective-permute-done((bf16[64,4096]{1,0:T(8,128)(2,1)}, bf16[64,4096]{1,0:T(8,128)(2,1)}, u32[]{:S(2)}, u32[]{:S(2)}) %collective-permute-start.2) | collective-permute-done | bytes 524320 | tf_op jit(solution)/shard_map/ppermute | solution.py:153
  68.6 4.7 shard_map.300
  83.6 12.3 %shard_map.301 = (bf16[512,1024]{1,0:T(8,128)(2,1)S(1)}, f32[1,8,2,512]{3,2,1,0:T(2,128)S(1)}) custom-call(s32[1]{0:T(128)S(6)} %copy.107.flag_ref, f32[2,16]{1,0:T(2,128)S(1)} %pad_maximum_fusion.3.far_ref, bf16[512,3072]{1,0:T(8,128)(2,1)S(1)} %convolution_convert_fusion.1.q_ref.k_ref.v_ref, ...), custom_call_target="tpu_custom_call" | custom-call | flops 2147483648 | bytes 7340032 | tf_op jit(solution)/shard_map/pallas_call | solution.py:491
  104.6 8.0 %collective-permute-done.23.refs_6_ = bf16[128,2816]{1,0:T(8,128)(2,1)S(1)} collective-permute-done((bf16[128,2816]{1,0:T(8,128)(2,1)S(1)}, bf16[128,2816]{1,0:T(8,128)(2,1)S(1)}, u32[]{:S(2)}, u32[]{:S(2)}) %collective-permute-start.23) | collective-permute-done | bytes 720928 | tf_op jit(solution)/shard_map/ppermute | solution.py:153
  115.5 7.8 %collective-permute-done.27.refs_8_ = bf16[64,2816]{1,0:T(8,128)(2,1)S(1)} collective-permute-done((bf16[64,2816]{1,0:T(8,128)(2,1)S(1)}, bf16[64,2816]{1,0:T(8,128)(2,1)S(1)}, u32[]{:S(2)}, u32[]{:S(2)}) %collective-permute-start.27) | collective-permute-done | bytes 360480 | tf_op jit(solution)/shard_map/ppermute | solution.py:153
  129.9 6.4 %collective-permute-done.25.refs_2_ = bf16[128,2816]{1,0:T(8,128)(2,1)S(1)} collective-permute-done((bf16[128,2816]{1,0:T(8,128)(2,1)S(1)}, bf16[128,2816]{1,0:T(8,128)(2,1)S(1)}, u32[]{:S(2)}, u32[]{:S(2)}) %collective-permute-start.25) | collective-permute-done | bytes 720928 | tf_op jit(solution)/shard_map/ppermute | solution.py:153
  147.9 18.9 %shard_map.305 = (bf16[1280,2816]{1,0:T(8,128)(2,1)}, bf16[1280,2816]{1,0:T(8,128)(2,1)}) custom-call(bf16[1280,1024]{1,0:T(8,128)(2,1)} %copy-done.8, bf16[1024,2816]{1,0:T(8,128)(2,1)} %bitcast.120), custom_call_target="tpu_custom_call" | custom-call | flops 7381975040 | bytes 22806528 | tf_op jit(solution)/shard_map/pallas_call | solution.py:704
  172.5 4.2 collective-permute-done.33.refs_3_
  176.6 14.2 %collective-permute-done.34.refs_6_ = bf16[128,2816]{1,0:T(8,128)(2,1)} collective-permute-done((bf16[128,2816]{1,0:T(8,128)(2,1)}, bf16[128,2816]{1,0:T(8,128)(2,1)}, u32[]{:S(2)}, u32[]{:S(2)}) %collective-permute-start.34) | collective-permute-done | bytes 720928 | tf_op jit(solution)/shard_map/ppermute | solution.py:153
  196.3 7.7 %collective-permute-done.39.refs_8_ = bf16[64,2816]{1,0:T(8,128)(2,1)S(1)} collective-permute-done((bf16[64,2816]{1,0:T(8,128)(2,1)S(1)}, bf16[64,2816]{1,0:T(8,128)(2,1)S(1)}, u32[]{:S(2)}, u32[]{:S(2)}) %collective-permute-start.39) | collective-permute-done | bytes 360480 | tf_op jit(solution)/shard_map/ppermute | solution.py:153
  217.0 6.0 %collective-permute-done.41.refs_4_ = bf16[352,1024]{1,0:T(8,128)(2,1)S(1)} collective-permute-done((bf16[352,1024]{1,0:T(8,128)(2,1)}, bf16[352,1024]{1,0:T(8,128)(2,1)S(1)}, u32[]{:S(2)}, u32[]{:S(2)}) %collective-permute-start.41) | collective-permute-done | bytes 720928 | tf_op jit(solution)/shard_map/ppermute | solution.py:153
  226.5 22.1 %shard_map.308 = (bf16[1280,2816]{1,0:T(8,128)(2,1)}, bf16[1280,2816]{1,0:T(8,128)(2,1)}, bf16[2816,1024]{1,0:T(8,128)(2,1)}) custom-call(bf16[1280,1024]{1,0:T(8,128)(2,1)} %copy-done.8, bf16[1024,2816]{1,0:T(8,128)(2,1)} %bitcast.122, bf16[1280,2816]{1,0:T(8,128)(2,1)} %get-tuple-element.203.act_ref, bf16[1280,2816]{1,0:T(8,128)(2,1)} %get-tuple-element.218.slope_ref, ...), custom_call_target="tpu_custom_call" | custom-call | flops 14763950080 | bytes 45613056 | tf_op jit(solution)/shard_map/pallas_call | solution.py:704
  264.1 7.8 %convolution_convert_fusion.2 = bf16[1280,1024]{1,0:T(8,128)(2,1)S(1)} fusion(bf16[1280,2816]{1,0:T(8,128)(2,1)S(1)} %bitcast.152, bf16[2816,1024]{1,0:T(8,128)(2,1)S(1)} %bitcast.130), kind=kOutput, calls=%fused_computation.13 | convolution fusion | flops 7383285760 | bytes 15597568 | tf_op jit(solution)/shard_map/dot_general | solution.py:82
  279.3 30.9 %shard_map.312.refs_0_.refs_1_.pre_ref.up_ref = bf16[4,1280,2816]{2,1,0:T(8,128)(2,1)} custom-call(bf16[1280,1024]{1,0:T(8,128)(2,1)} %multiply_convert_fusion.grads_ref, bf16[2816,1024]{1,0:T(8,128)(2,1)} %bitcast.131, bf16[1280,2816]{1,0:T(8,128)(2,1)} %get-tuple-element.234.lift_ref, bf16[1280,2816]{1,0:T(8,128)(2,1)} %get-tuple-element.203.act_ref, ...), custom_call_target="tpu_custom_call" | custom-call | flops 22145925120 | bytes 54263808 | tf_op jit(solution)/shard_map/pallas_call | solution.py:704
  320.1 22.6 %shard_map.315 = (bf16[320,1024]{1,0:T(8,128)(2,1)}, bf16[320,1024]{1,0:T(8,128)(2,1)}, bf16[640,1024]{1,0:T(8,128)(2,1)}) custom-call(bf16[4,1280,2816]{2,1,0:T(8,128)(2,1)} %shard_map.312.refs_0_.refs_1_.pre_ref.up_ref, bf16[4,1280,2816]{2,1,0:T(8,128)(2,1)} %shard_map.312.refs_0_.refs_1_.pre_ref.up_ref, bf16[1024,2816]{1,0:T(8,128)(2,1)} %bitcast.121, ...), custom_call_target="tpu_custom_call" | custom-call | flops 14763950080 | bytes 71827456 | tf_op jit(solution)/shard_map/pallas_call | solution.py:704
  355.7 16.9 %collective-permute-done.61.refs_3_ = bf16[640,1024]{1,0:T(8,128)(2,1)S(1)} collective-permute-done((bf16[640,1024]{1,0:T(8,128)(2,1)}, bf16[640,1024]{1,0:T(8,128)(2,1)S(1)}, u32[]{:S(2)}, u32[]{:S(2)}) %collective-permute-start.61) | collective-permute-done | bytes 1310752 | tf_op jit(solution)/shard_map/ppermute | solution.py:283
  372.6 7.5 %collective-permute-done.58.refs_2_ = bf16[2,128,2816]{2,1,0:T(8,128)(2,1)S(1)} collective-permute-done((bf16[2,128,2816]{2,1,0:T(8,128)(2,1)S(1)}, bf16[2,128,2816]{2,1,0:T(8,128)(2,1)S(1)}, u32[]{:S(2)}, u32[]{:S(2)}) %collective-permute-start.58) | collective-permute-done | bytes 1441824 | tf_op jit(solution)/shard_map/ppermute | solution.py:266
  398.1 21.6 %shard_map.320 = (bf16[512,1024]{1,0:T(8,128)(2,1)S(1)}, bf16[512,1024]{1,0:T(8,128)(2,1)S(1)}, bf16[512,1024]{1,0:T(8,128)(2,1)S(1)}, f32[16,3,128,128]{3,2,1,0:T(8,128)S(1)}, f32[8,2,2,128]{3,2,1,0:T(2,128)S(1)}) custom-call(s32[1]{0:T(128)S(6)} %copy.107.flag_ref, f32[2,16]{1,0:T(2,128)S(1)} %pad_maximum_fusion.3.far_ref, ...), custom_call_target="tpu_custom_call" | custom-call | flops 5368709120 | bytes 14680064 | tf_op jit(solution)/shard_map/pallas_call | solution.py:610
  425.7 5.4 convolution_convert_fusion
  431.2 6.2 %dynamic-slice_bitcast_fusion = (bf16[8,64,3072]{2,1,0:T(8,128)(2,1)}, bf16[8,64,3072]{2,1,0:T(8,128)(2,1)}) fusion(bf16[8,2,64,3072]{3,2,1,0:T(8,128)(2,1)} %bitcast.135, s32[]{:T(128)} %sub.55, s32[]{:T(128)} %and.21), kind=kLoop, calls=%fused_computation.16 | loop fusion | bytes 12582920 | tf_op jit(solution)/shard_map/jit(dynamic_index_in_dim)/squeeze | solution.py:97
  441.8 3.8 shard_map.322
  451.7 4.4 fusion.32
  461.9 5.9 %collective-permute-done.69.refs_2_ = bf16[352,1024]{1,0:T(8,128)(2,1)} collective-permute-done((bf16[352,1024]{1,0:T(8,128)(2,1)}, bf16[352,1024]{1,0:T(8,128)(2,1)}, u32[]{:S(2)}, u32[]{:S(2)}) %collective-permute-start.69) | collective-permute-done | bytes 720928 | tf_op jit(solution)/shard_map/ppermute | solution.py:283
  470.8 3.9 fusion.23
  476.7 4.3 collective-permute-done.72.refs_1_
  496.3 7.8 %collective-permute-done.79.refs_2_ = bf16[128,2816]{1,0:T(8,128)(2,1)} collective-permute-done((bf16[128,2816]{1,0:T(8,128)(2,1)}, bf16[128,2816]{1,0:T(8,128)(2,1)}, u32[]{:S(2)}, u32[]{:S(2)}) %collective-permute-start.79) | collective-permute-done | bytes 720928 | tf_op jit(solution)/shard_map/ppermute | solution.py:283
  511.5 12.3 %collective-permute-done.80 = f32[52,128]{1,0:T(8,128)S(1)} collective-permute-done((f32[52,128]{1,0:T(8,128)S(1)}, f32[52,128]{1,0:T(8,128)S(1)}, u32[]{:S(2)}, u32[]{:S(2)}) %collective-permute-start.80) | collective-permute-done | bytes 26656 | tf_op jit(solution)/shard_map/ppermute | solution.py:406
  532.9 4.6 shard_map.329
  537.6 5.3 collective-permute-done.85
  551.0 4.4 shard_map.331
  555.5 4.4 shard_map.332
  (495 shorter events, 257.1 us)
Async XLA Ops:
  21.0 20.0 %collective-permute-start.7 = (bf16[64,4096]{1,0:T(8,128)(2,1)}, bf16[64,4096]{1,0:T(8,128)(2,1)S(1)}, u32[]{:S(2)}, u32[]{:S(2)}) collective-permute-start(bf16[64,4096]{1,0:T(8,128)(2,1)} %collective-permute-done.refs_2_), channel_id=1, source_target_pairs={{0,1},{1,0},{2,3},{3,2},{4,5},{5,4},{6,7},{7,6},{8,9},{9,8},{10,11... | collective-permute-start | bytes 1572872 | tf_op jit(solution)/shard_map/ppermute | solution.py:283
  21.5 25.1 %collective-permute-start.8 = (bf16[64,4096]{1,0:T(8,128)(2,1)}, bf16[64,4096]{1,0:T(8,128)(2,1)S(1)}, u32[]{:S(2)}, u32[]{:S(2)}) collective-permute-start(bf16[64,4096]{1,0:T(8,128)(2,1)} %collective-permute-done.1.refs_3_), channel_id=1, source_target_pairs={{0,1},{1,0},{2,3},{3,2},{4,5},{5,4},{6,7},{7,6},{8,9},{9,8},{10,11... | collective-permute-start | bytes 1572872 | tf_op jit(solution)/shard_map/ppermute | solution.py:283
  58.4 19.5 %collective-permute-start.10 = (bf16[128,2816]{1,0:T(8,128)(2,1)}, bf16[128,2816]{1,0:T(8,128)(2,1)S(1)}, u32[]{:S(2)}, u32[]{:S(2)}) collective-permute-start(bf16[128,2816]{1,0:T(8,128)(2,1)} %dynamic-slice_bitcast_fusion.6.refs_1_), channel_id=1, source_target_pairs={{4,0},{12,4},{20,12},{28,20},{24,28},{16,24},{8,16},{0,8},{5,1},{1... | collective-permute-start | bytes 2162696 | tf_op jit(solution)/shard_map/ppermute | solution.py:154
  102.0 34.3 %collective-permute-start.22 = (bf16[640,1024]{1,0:T(8,128)(2,1)S(1)}, bf16[640,1024]{1,0:T(8,128)(2,1)S(1)}, u32[]{:S(2)}, u32[]{:S(2)}) collective-permute-start(bf16[640,1024]{1,0:T(8,128)(2,1)S(1)} %convolution_convert_fusion.4), channel_id=1, source_target_pairs={{0,2},{1,3},{2,0},{3,1},{4,6},{5,7},{6,4},{7,5},{8,10},{9,11},{10,... | collective-permute-start | bytes 3932168 | tf_op jit(solution)/shard_map/ppermute | solution.py:283
  115.1 21.4 %collective-permute-start.21 = (bf16[320,1024]{1,0:T(8,128)(2,1)S(1)}, bf16[320,1024]{1,0:T(8,128)(2,1)S(1)}, u32[]{:S(2)}, u32[]{:S(2)}) collective-permute-start(bf16[320,1024]{1,0:T(8,128)(2,1)S(1)} %convolution_convert_fusion.7), channel_id=1, source_target_pairs={{0,1},{1,0},{2,3},{3,2},{4,5},{5,4},{6,7},{7,6},{8,9},{9,8},{10,11... | collective-permute-start | bytes 1966088 | tf_op jit(solution)/shard_map/ppermute | solution.py:283
  115.1 21.1 %collective-permute-start.25 = (bf16[128,2816]{1,0:T(8,128)(2,1)S(1)}, bf16[128,2816]{1,0:T(8,128)(2,1)S(1)}, u32[]{:S(2)}, u32[]{:S(2)}) collective-permute-start(bf16[128,2816]{1,0:T(8,128)(2,1)S(1)} %copy-done.18), channel_id=1, source_target_pairs={{0,4},{4,12},{12,20},{20,28},{28,24},{24,16},{16,8},{8,0},{1,5},{5... | collective-permute-start | bytes 2162696 | tf_op jit(solution)/shard_map/ppermute | solution.py:153
  141.4 25.4 %collective-permute-start.30 = (bf16[128,2816]{1,0:T(8,128)(2,1)S(1)}, bf16[128,2816]{1,0:T(8,128)(2,1)}, u32[]{:S(2)}, u32[]{:S(2)}) collective-permute-start(bf16[128,2816]{1,0:T(8,128)(2,1)S(1)} %collective-permute-done.25.refs_2_), channel_id=1, source_target_pairs={{0,4},{4,12},{12,20},{20,28},{28,24},{24,16},{16,8},{8,0},{1,5},{5... | collective-permute-start | bytes 2162696 | tf_op jit(solution)/shard_map/ppermute | solution.py:153
  141.6 25.2 %collective-permute-start.31 = (bf16[128,2816]{1,0:T(8,128)(2,1)S(1)}, bf16[128,2816]{1,0:T(8,128)(2,1)}, u32[]{:S(2)}, u32[]{:S(2)}) collective-permute-start(bf16[128,2816]{1,0:T(8,128)(2,1)S(1)} %collective-permute-done.26.refs_3_), channel_id=1, source_target_pairs={{4,0},{12,4},{20,12},{28,20},{24,28},{16,24},{8,16},{0,8},{5,1},{1... | collective-permute-start | bytes 2162696 | tf_op jit(solution)/shard_map/ppermute | solution.py:154
  143.5 52.8 %collective-permute-start.37 = (bf16[352,1024]{1,0:T(8,128)(2,1)}, bf16[352,1024]{1,0:T(8,128)(2,1)}, u32[]{:S(2)}, u32[]{:S(2)}) collective-permute-start(bf16[352,1024]{1,0:T(8,128)(2,1)} %dynamic-slice_bitcast_fusion.4.refs_1_), channel_id=1, source_target_pairs={{0,4},{4,12},{12,20},{20,28},{28,24},{24,16},{16,8},{8,0},{1,5},{5... | collective-permute-start | bytes 2162696 | tf_op jit(solution)/shard_map/ppermute | solution.py:153
  143.7 52.6 %collective-permute-start.38 = (bf16[352,1024]{1,0:T(8,128)(2,1)}, bf16[352,1024]{1,0:T(8,128)(2,1)}, u32[]{:S(2)}, u32[]{:S(2)}) collective-permute-start(bf16[352,1024]{1,0:T(8,128)(2,1)} %dynamic-slice_bitcast_fusion.4.refs_1_), channel_id=1, source_target_pairs={{4,0},{12,4},{20,12},{28,20},{24,28},{16,24},{8,16},{0,8},{5,1},{1... | collective-permute-start | bytes 2162696 | tf_op jit(solution)/shard_map/ppermute | solution.py:154
  146.4 30.3 %collective-permute-start.33 = (bf16[640,1024]{1,0:T(8,128)(2,1)}, bf16[640,1024]{1,0:T(8,128)(2,1)}, u32[]{:S(2)}, u32[]{:S(2)}) collective-permute-start(bf16[640,1024]{1,0:T(8,128)(2,1)} %convolution_convert_fusion.5), channel_id=1, source_target_pairs={{0,2},{1,3},{2,0},{3,1},{4,6},{5,7},{6,4},{7,5},{8,10},{9,11},{10,... | collective-permute-start | bytes 3932168 | tf_op jit(solution)/shard_map/ppermute | solution.py:283
  166.8 24.0 %collective-permute-start.34 = (bf16[128,2816]{1,0:T(8,128)(2,1)}, bf16[128,2816]{1,0:T(8,128)(2,1)}, u32[]{:S(2)}, u32[]{:S(2)}) collective-permute-start(bf16[128,2816]{1,0:T(8,128)(2,1)} %collective-permute-done.30.refs_4_), channel_id=1, source_target_pairs={{0,4},{4,12},{12,20},{20,28},{28,24},{24,16},{16,8},{8,0},{1,5},{5... | collective-permute-start | bytes 2162696 | tf_op jit(solution)/shard_map/ppermute | solution.py:153
  167.1 23.9 %collective-permute-start.35 = (bf16[128,2816]{1,0:T(8,128)(2,1)}, bf16[128,2816]{1,0:T(8,128)(2,1)}, u32[]{:S(2)}, u32[]{:S(2)}) collective-permute-start(bf16[128,2816]{1,0:T(8,128)(2,1)} %collective-permute-done.31.refs_5_), channel_id=1, source_target_pairs={{4,0},{12,4},{20,12},{28,20},{24,28},{16,24},{8,16},{0,8},{5,1},{1... | collective-permute-start | bytes 2162696 | tf_op jit(solution)/shard_map/ppermute | solution.py:154
  224.5 24.1 %collective-permute-start.43 = (bf16[352,1024]{1,0:T(8,128)(2,1)S(1)}, bf16[352,1024]{1,0:T(8,128)(2,1)S(1)}, u32[]{:S(2)}, u32[]{:S(2)}) collective-permute-start(bf16[352,1024]{1,0:T(8,128)(2,1)S(1)} %collective-permute-done.41.refs_4_), channel_id=1, source_target_pairs={{0,4},{4,12},{12,20},{20,28},{28,24},{24,16},{16,8},{8,0},{1,5},{5... | collective-permute-start | bytes 2162696 | tf_op jit(solution)/shard_map/ppermute | solution.py:153
  226.0 22.6 %collective-permute-start.44 = (bf16[352,1024]{1,0:T(8,128)(2,1)S(1)}, bf16[352,1024]{1,0:T(8,128)(2,1)S(1)}, u32[]{:S(2)}, u32[]{:S(2)}) collective-permute-start(bf16[352,1024]{1,0:T(8,128)(2,1)S(1)} %collective-permute-done.42.refs_5_), channel_id=1, source_target_pairs={{4,0},{12,4},{20,12},{28,20},{24,28},{16,24},{8,16},{0,8},{5,1},{1... | collective-permute-start | bytes 2162696 | tf_op jit(solution)/shard_map/ppermute | solution.py:154
  254.4 19.5 %collective-permute-start.45 = (bf16[1,352,512]{2,1,0:T(8,128)(2,1)S(1)}, bf16[1,352,512]{2,1,0:T(8,128)(2,1)S(1)}, u32[]{:S(2)}, u32[]{:S(2)}) collective-permute-start(bf16[1,352,512]{2,1,0:T(8,128)(2,1)S(1)} %get-tuple-element.226), channel_id=1, source_target_pairs={{0,4},{4,12},{12,20},{20,28},{28,24},{24,16},{16,8},{8,0},{1,5},{5... | collective-permute-start | bytes 1081352 | tf_op jit(solution)/shard_map/ppermute | solution.py:266
  275.8 34.4 %collective-permute-start.49 = (bf16[2,352,512]{2,1,0:T(8,128)(2,1)}, bf16[2,352,512]{2,1,0:T(8,128)(2,1)S(1)}, u32[]{:S(2)}, u32[]{:S(2)}) collective-permute-start(bf16[2,352,512]{2,1,0:T(8,128)(2,1)} %get-tuple-element.231), channel_id=1, source_target_pairs={{0,4},{4,12},{12,20},{20,28},{28,24},{24,16},{16,8},{8,0},{1,5},{5... | collective-permute-start | bytes 2162696 | tf_op jit(solution)/shard_map/ppermute | solution.py:266
  277.3 32.8 %collective-permute-start.50 = (bf16[2,352,512]{2,1,0:T(8,128)(2,1)S(1)}, bf16[2,352,512]{2,1,0:T(8,128)(2,1)S(1)}, u32[]{:S(2)}, u32[]{:S(2)}) collective-permute-start(bf16[2,352,512]{2,1,0:T(8,128)(2,1)S(1)} %get-tuple-element.232), channel_id=1, source_target_pairs={{4,0},{12,4},{20,12},{28,20},{24,28},{16,24},{8,16},{0,8},{5,1},{1... | collective-permute-start | bytes 2162696 | tf_op jit(solution)/shard_map/ppermute | solution.py:267
  277.8 32.4 %collective-permute-start.52 = (bf16[640,1024]{1,0:T(8,128)(2,1)}, bf16[640,1024]{1,0:T(8,128)(2,1)S(1)}, u32[]{:S(2)}, u32[]{:S(2)}) collective-permute-start(bf16[640,1024]{1,0:T(8,128)(2,1)} %slice.148), channel_id=1, source_target_pairs={{0,2},{1,3},{2,0},{3,1},{4,6},{5,7},{6,4},{7,5},{8,10},{9,11},{10,... | collective-permute-start | bytes 3932168 | tf_op jit(solution)/shard_map/ppermute | solution.py:283
  279.3 30.9 %collective-permute-start.51 = (bf16[320,1024]{1,0:T(8,128)(2,1)}, bf16[320,1024]{1,0:T(8,128)(2,1)S(1)}, u32[]{:S(2)}, u32[]{:S(2)}) collective-permute-start(bf16[320,1024]{1,0:T(8,128)(2,1)} %get-tuple-element.235), channel_id=1, source_target_pairs={{0,1},{1,0},{2,3},{3,2},{4,5},{5,4},{6,7},{7,6},{8,9},{9,8},{10,11... | collective-permute-start | bytes 1966088 | tf_op jit(solution)/shard_map/ppermute | solution.py:283
  314.1 29.1 %collective-permute-start.53 = (bf16[1,128,2816]{2,1,0:T(8,128)(2,1)}, bf16[1,128,2816]{2,1,0:T(8,128)(2,1)S(1)}, u32[]{:S(2)}, u32[]{:S(2)}) collective-permute-start(bf16[1,128,2816]{2,1,0:T(8,128)(2,1)} %get-tuple-element.239), channel_id=1, source_target_pairs={{0,4},{4,12},{12,20},{20,28},{28,24},{24,16},{16,8},{8,0},{1,5},{5... | collective-permute-start | bytes 2162696 | tf_op jit(solution)/shard_map/ppermute | solution.py:266
  315.7 27.6 %collective-permute-start.54 = (bf16[1,128,2816]{2,1,0:T(8,128)(2,1)}, bf16[1,128,2816]{2,1,0:T(8,128)(2,1)S(1)}, u32[]{:S(2)}, u32[]{:S(2)}) collective-permute-start(bf16[1,128,2816]{2,1,0:T(8,128)(2,1)} %get-tuple-element.240), channel_id=1, source_target_pairs={{4,0},{12,4},{20,12},{28,20},{24,28},{16,24},{8,16},{0,8},{5,1},{1... | collective-permute-start | bytes 2162696 | tf_op jit(solution)/shard_map/ppermute | solution.py:267
  318.1 29.9 %collective-permute-start.56 = (bf16[2,352,512]{2,1,0:T(8,128)(2,1)}, bf16[2,352,512]{2,1,0:T(8,128)(2,1)S(1)}, u32[]{:S(2)}, u32[]{:S(2)}) collective-permute-start(bf16[2,352,512]{2,1,0:T(8,128)(2,1)} %get-tuple-element.244), channel_id=1, source_target_pairs={{0,4},{4,12},{12,20},{20,28},{28,24},{24,16},{16,8},{8,0},{1,5},{5... | collective-permute-start | bytes 2162696 | tf_op jit(solution)/shard_map/ppermute | solution.py:266
  319.7 29.6 %collective-permute-start.57 = (bf16[2,352,512]{2,1,0:T(8,128)(2,1)}, bf16[2,352,512]{2,1,0:T(8,128)(2,1)S(1)}, u32[]{:S(2)}, u32[]{:S(2)}) collective-permute-start(bf16[2,352,512]{2,1,0:T(8,128)(2,1)} %get-tuple-element.245), channel_id=1, source_target_pairs={{4,0},{12,4},{20,12},{28,20},{24,28},{16,24},{8,16},{0,8},{5,1},{1... | collective-permute-start | bytes 2162696 | tf_op jit(solution)/shard_map/ppermute | solution.py:267
  342.7 29.9 %collective-permute-start.61 = (bf16[640,1024]{1,0:T(8,128)(2,1)}, bf16[640,1024]{1,0:T(8,128)(2,1)S(1)}, u32[]{:S(2)}, u32[]{:S(2)}) collective-permute-start(bf16[640,1024]{1,0:T(8,128)(2,1)} %get-tuple-element.249), channel_id=1, source_target_pairs={{0,2},{1,3},{2,0},{3,1},{4,6},{5,7},{6,4},{7,5},{8,10},{9,11},{10,... | collective-permute-start | bytes 3932168 | tf_op jit(solution)/shard_map/ppermute | solution.py:283
  343.3 43.7 %collective-permute-start.60 = (bf16[320,1024]{1,0:T(8,128)(2,1)}, bf16[320,1024]{1,0:T(8,128)(2,1)S(1)}, u32[]{:S(2)}, u32[]{:S(2)}) collective-permute-start(bf16[320,1024]{1,0:T(8,128)(2,1)} %get-tuple-element.248), channel_id=1, source_target_pairs={{0,1},{1,0},{2,3},{3,2},{4,5},{5,4},{6,7},{7,6},{8,9},{9,8},{10,11... | collective-permute-start | bytes 1966088 | tf_op jit(solution)/shard_map/ppermute | solution.py:283
  346.1 34.0 %collective-permute-start.58 = (bf16[2,128,2816]{2,1,0:T(8,128)(2,1)S(1)}, bf16[2,128,2816]{2,1,0:T(8,128)(2,1)S(1)}, u32[]{:S(2)}, u32[]{:S(2)}) collective-permute-start(bf16[2,128,2816]{2,1,0:T(8,128)(2,1)S(1)} %get-tuple-element.252), channel_id=1, source_target_pairs={{0,4},{4,12},{12,20},{20,28},{28,24},{24,16},{16,8},{8,0},{1,5},{5... | collective-permute-start | bytes 4325384 | tf_op jit(solution)/shard_map/ppermute | solution.py:266
  348.0 33.6 %collective-permute-start.59 = (bf16[2,128,2816]{2,1,0:T(8,128)(2,1)S(1)}, bf16[2,128,2816]{2,1,0:T(8,128)(2,1)S(1)}, u32[]{:S(2)}, u32[]{:S(2)}) collective-permute-start(bf16[2,128,2816]{2,1,0:T(8,128)(2,1)S(1)} %get-tuple-element.253), channel_id=1, source_target_pairs={{4,0},{12,4},{20,12},{28,20},{24,28},{16,24},{8,16},{0,8},{5,1},{1... | collective-permute-start | bytes 4325384 | tf_op jit(solution)/shard_map/ppermute | solution.py:267
  384.9 56.9 %collective-permute-start.63 = (bf16[2,128,2816]{2,1,0:T(8,128)(2,1)S(1)}, bf16[2,128,2816]{2,1,0:T(8,128)(2,1)S(1)}, u32[]{:S(2)}, u32[]{:S(2)}) collective-permute-start(bf16[2,128,2816]{2,1,0:T(8,128)(2,1)S(1)} %get-tuple-element.258), channel_id=1, source_target_pairs={{0,4},{4,12},{12,20},{20,28},{28,24},{24,16},{16,8},{8,0},{1,5},{5... | collective-permute-start | bytes 4325384 | tf_op jit(solution)/shard_map/ppermute | solution.py:266
  386.6 55.2 %collective-permute-start.64 = (bf16[2,128,2816]{2,1,0:T(8,128)(2,1)S(1)}, bf16[2,128,2816]{2,1,0:T(8,128)(2,1)S(1)}, u32[]{:S(2)}, u32[]{:S(2)}) collective-permute-start(bf16[2,128,2816]{2,1,0:T(8,128)(2,1)S(1)} %get-tuple-element.259), channel_id=1, source_target_pairs={{4,0},{12,4},{20,12},{28,20},{24,28},{16,24},{8,16},{0,8},{5,1},{1... | collective-permute-start | bytes 4325384 | tf_op jit(solution)/shard_map/ppermute | solution.py:267
  446.2 34.8 %collective-permute-start.72 = (bf16[2,128,2816]{2,1,0:T(8,128)(2,1)}, bf16[2,128,2816]{2,1,0:T(8,128)(2,1)}, u32[]{:S(2)}, u32[]{:S(2)}) collective-permute-start(bf16[2,128,2816]{2,1,0:T(8,128)(2,1)} %get-tuple-element.273), channel_id=1, source_target_pairs={{0,4},{4,12},{12,20},{20,28},{28,24},{24,16},{16,8},{8,0},{1,5},{5... | collective-permute-start | bytes 4325384 | tf_op jit(solution)/shard_map/ppermute | solution.py:266
  447.1 34.8 %collective-permute-start.73 = (bf16[2,128,2816]{2,1,0:T(8,128)(2,1)}, bf16[2,128,2816]{2,1,0:T(8,128)(2,1)}, u32[]{:S(2)}, u32[]{:S(2)}) collective-permute-start(bf16[2,128,2816]{2,1,0:T(8,128)(2,1)} %get-tuple-element.274), channel_id=1, source_target_pairs={{4,0},{12,4},{20,12},{28,20},{24,28},{16,24},{8,16},{0,8},{5,1},{1... | collective-permute-start | bytes 4325384 | tf_op jit(solution)/shard_map/ppermute | solution.py:267
  (159 other events, 1645.9 us)

commit v2 on v1

--- a/solution.py
+++ b/solution.py
@@ -320,16 +320,10 @@
         self.hop()
 
     @classmethod
-    def pair(cls, both):
-        spreads = cls(both[0]), cls(both[1])
-        for lead, spread in enumerate(spreads):
-            spread.held[0] = (both, lead)
-        return spreads
-
-    @classmethod
     def hop_own(cls, first, second, both, *others):
         swapped = swap(after(both, *others), 1)
         for lead, spread in enumerate((first, second)):
+            spread.held[0] = (both, lead)
             spread.held[1] = (swapped, lead)
             spread.own_last = (swapped,)
 
@@ -903,7 +897,12 @@
     weight_step(inv_one)
     ids, slots, kept = tie((expert_ids, slot_index, slot_kept), weight_ring.sent)
     from_slot, to_slot = routes(ids, slots, kept)
-    weight_step(to_slot, theirs[0])
+    def core_columns(rows):
+        split = rows.reshape(tok_count, dp_count, 2, half_rows)
+        return [pick(split, side, 2).reshape(tok_count, -1) for side in (core, 1 - core)]
+
+    normed_mine, normed_other = core_columns(normed)
+    weight_step(to_slot, theirs[0], normed_mine, normed_other)
     cots, table = tie((cotangent, rel_table), weight_ring.sent)
     cot_blocks = outgoing(cots, to_slot)
     bias = lax.dot_general(
@@ -973,7 +972,8 @@
     cot_exchange.forward(slot_gate, slot_rows_t, *up_ring.arrived())
     slot_cots = cot_exchange.together(seat)
     slot_grads = (slot_gate * slot_cots.astype(jnp.float32)).astype(jnp.bfloat16)
-    up_ring.step(slot_gate, slot_rows_t)
+    context_mine, context_other = core_columns(after(context, *up_ring.sent))
+    up_ring.step(slot_gate, slot_rows_t, context_mine, context_other)
     down_ring.step(*up_ring.arrived())
     up_full = up_ring.finish(*down_ring.sent, slot_grads)
     down_ring.step(up_full, slot_grads)
@@ -1019,7 +1019,8 @@
         router * (grad_router - jnp.sum(router * grad_router, -1, keepdims=True))
     ).astype(jnp.bfloat16)
     returned_grads.forward(grad_logits, *gate_up_sum.arrived())
-    gate_up_sum.step(grad_logits)
+    down_sum.step(grad_logits, *gate_up_sum.arrived())
+    gate_up_sum.step(*down_sum.sent)
     returned_grads = returned_grads.together(seat, *gate_up_sum.sent)
     grad_normed_two = matmul(grad_logits, w_router.T) + matmul(
         from_slot[0] + from_slot[1], returned_grads
@@ -1030,22 +1031,26 @@
     grad_branch = grad_mid.astype(jnp.bfloat16)
     grad_context = dot_dims(grad_branch, full_out, 1, 1).astype(jnp.bfloat16)
 
-    def core_parts(local):
-        split = local.reshape(dp_count, 2, half_rows, -1)
-        return pick(split, core, 1), pick(split, 1 - core, 1)
-
-    out_mine, out_other = core_parts(dot_dims(context, grad_branch, 0, 0).astype(jnp.bfloat16))
+    def half_product(columns, grads):
+        product = dot_dims(columns, grads, 0, 0).astype(jnp.bfloat16)
+        return product.reshape(dp_count, half_rows, -1)
+
+    out_other = half_product(context_other, grad_branch)
+    out_mine = half_product(context_mine, grad_branch)
     (grad_context,) = tie((grad_context,), (out_mine, out_other))
+    out_other = swap(out_other, 1)
     grad_query, grad_key, grad_value, near, away = attend_backward(
         qkv, grad_context, lse, seq_bucket, far, bias
     )
-    down_sum.step(grad_query)
-    out_other = swap(after(out_other, grad_query), 1)
+    grad_query, grad_key, grad_value, near, away = tie(
+        (grad_query, grad_key, grad_value, near, away), (*down_sum.arrived(), out_other)
+    )
     qkv_grads = jnp.concatenate([grad_query, grad_key, grad_value], 1)
-    qkv_mine, qkv_other = core_parts(dot_dims(normed, qkv_grads, 0, 0).astype(jnp.bfloat16))
-    gate_up_sum.step(qkv_other, qkv_mine, *down_sum.arrived())
+    qkv_other = half_product(normed_other, qkv_grads)
+    qkv_mine = half_product(after(normed_mine, qkv_other), qkv_grads)
+    gate_up_sum.step(qkv_other, qkv_mine)
+    qkv_other = swap(after(qkv_other, *gate_up_sum.sent), 1)
     down_share = down_sum.finish(*gate_up_sum.sent, joined=True)
-    qkv_other = swap(after(qkv_other, *gate_up_sum.sent), 1)
     down_blocks = Spread(after(down_share, *gate_up_sum.sent))
     qkv_mine, out_mine = tie((qkv_mine, out_mine), gate_up_sum.sent)
     weight_parts = jnp.concatenate(
@@ -1066,7 +1071,7 @@
     down_blocks.hop(*weight_sum.sent)
 
     gate_up_share = gate_up_sum.finish(input_grad)
-    gate_blocks, up_blocks = Spread.pair(gate_up_share)
+    gate_blocks, up_blocks = Spread(gate_up_share[0]), Spread(gate_up_share[1])
     weight_sum.step(gate_up_share, *down_blocks.arrived())
     (late_rows,) = tie((normed_two,), weight_sum.sent)
     small = SumAll((gain_one_local, table_local, gain_two_local, matmul(late_rows.T, grad_logits)))

time: 581 us -> 582 us (level)
    ppermute x16, waiting for transfers between devices: 16.6 us -> 42.3 us  [step(): self.high = lax.ppermute(high, 'dp', self.behind)]
    ppermute x16, waiting for transfers between devices: 71.9 us -> 47.3 us  [step(): self.low = lax.ppermute(low, 'dp', self.ahead)]
    squeeze x6 -> x4, local copies, waits for them, and re-layouts: 13.5 us -> 4.79 us  [pick(): lax.dynamic_index_in_dim(array, index, axis, keepdims=False, allow_negati...]
    unnamed x201 -> x237, local copies, waits for them, and re-layouts: 26.8 us -> 30.3 us
    dot_general x4 -> x6, matrix products: 11.9 us -> 14.6 us  [dot_dims(): lax.dot_general(left, right, (((left_dim,), (right_dim,)), ((), ())), pre...]
  transfers between devices with their start and end apart: 94 -> 94, of which waited for: 43 -> 41; matrix products, arithmetic and copies ran while one was open for 17% -> 17% of each run, Pallas kernels for 32% -> 31%
where the time goes in v2:
time: 582 us; the launch traced here: 572 us
  Pallas kernels  191 us (33%)
  waiting for transfers between devices  171 us (29%)
  starting transfers between devices  76.6 us (13%)
  local copies, waits for them, and re-layouts  63.4 us (11%)
  matrix products  53 us (9%)
  other arithmetic  13.6 us (2%)
    pallas_call x4, Pallas kernels, kernel_call(): pl.pallas_call(kernel, grid=(steps,), in_specs=in_specs, out_specs=out_sp...  94.5 us
    ppermute x16, waiting for transfers between devices, step(): self.low = lax.ppermute(low, 'dp', self.ahead)  47.3 us
    ppermute x16, waiting for transfers between devices, step(): self.high = lax.ppermute(high, 'dp', self.behind)  42.3 us
    ppermute x33, waiting for transfers between devices, swap(): return lax.ppermute(value, 'expert', [(i, i ^ bit) for i in range(count)])  42 us
    dot_general x16, matrix products, matmul(): return jnp.dot(left, right, preferred_element_type=jnp.float32)  31.8 us
    unnamed x237, local copies, waits for them, and re-layouts  30.3 us
    pallas_call x15, Pallas kernels, call(): pl.pallas_call(lambda seat_ref, *refs: ring_sum_kernel(received, len(own)...  28.6 us
    ppermute x16, starting transfers between devices, step(): self.low = lax.ppermute(low, 'dp', self.ahead)  22.7 us
  transfers between devices with their start and end apart: 94, of which 41 were waited for; matrix products, arithmetic and copies ran while one was open for 17% of the time, Pallas kernels for 31%

profile of v2, /device:TPU:0, one launch (start us, length us, event | category | flops | bytes accessed | tf_op | source)
XLA Modules:
  0.0 572.5 jit_solution(3033166892150734715)
XLA Ops:
  13.9 4.2 collective-permute-done.1.refs_3_
  22.6 11.7 %collective-permute-done.2.refs_4_ = bf16[64,4096]{1,0:T(8,128)(2,1)} collective-permute-done((bf16[64,4096]{1,0:T(8,128)(2,1)}, bf16[64,4096]{1,0:T(8,128)(2,1)}, u32[]{:S(2)}, u32[]{:S(2)}) %collective-permute-start.2) | collective-permute-done | bytes 524320 | tf_op jit(solution)/shard_map/ppermute | solution.py:153
  58.3 5.1 collective-permute-done.12.refs_9_
  69.3 4.7 shard_map.300
  74.0 3.8 shard_map.302
  80.1 3.6 convolution_convert_fusion.2.q_ref.k_ref.v_ref
  83.8 12.3 %shard_map.301 = (bf16[512,1024]{1,0:T(8,128)(2,1)S(1)}, f32[1,8,2,512]{3,2,1,0:T(2,128)S(1)}) custom-call(s32[1]{0:T(128)S(6)} %copy.93.flag_ref, f32[2,16]{1,0:T(2,128)S(1)} %pad_maximum_fusion.3.far_ref, bf16[512,3072]{1,0:T(8,128)(2,1)S(1)} %convolution_convert_fusion.2.q_ref.k_ref.v_ref, ...), custom_call_target="tpu_custom_call" | custom-call | flops 2147483648 | bytes 7340032 | tf_op jit(solution)/shard_map/pallas_call | solution.py:485
  106.5 8.8 %collective-permute-done.23.refs_6_ = bf16[128,2816]{1,0:T(8,128)(2,1)S(1)} collective-permute-done((bf16[128,2816]{1,0:T(8,128)(2,1)S(1)}, bf16[128,2816]{1,0:T(8,128)(2,1)S(1)}, u32[]{:S(2)}, u32[]{:S(2)}) %collective-permute-start.23) | collective-permute-done | bytes 720928 | tf_op jit(solution)/shard_map/ppermute | solution.py:153
  119.2 8.8 %collective-permute-done.28.refs_9_ = bf16[64,2816]{1,0:T(8,128)(2,1)S(1)} collective-permute-done((bf16[64,2816]{1,0:T(8,128)(2,1)S(1)}, bf16[64,2816]{1,0:T(8,128)(2,1)S(1)}, u32[]{:S(2)}, u32[]{:S(2)}) %collective-permute-start.28) | collective-permute-done | bytes 360480 | tf_op jit(solution)/shard_map/ppermute | solution.py:154
  135.2 5.2 collective-permute-done.26.refs_3_
  152.3 18.9 %shard_map.305 = (bf16[1280,2816]{1,0:T(8,128)(2,1)}, bf16[1280,2816]{1,0:T(8,128)(2,1)}) custom-call(bf16[1280,1024]{1,0:T(8,128)(2,1)} %copy-done.8, bf16[1024,2816]{1,0:T(8,128)(2,1)} %bitcast.115), custom_call_target="tpu_custom_call" | custom-call | flops 7381975040 | bytes 22806528 | tf_op jit(solution)/shard_map/pallas_call | solution.py:698
  181.1 14.2 %collective-permute-done.34.refs_6_ = bf16[128,2816]{1,0:T(8,128)(2,1)S(1)} collective-permute-done((bf16[128,2816]{1,0:T(8,128)(2,1)}, bf16[128,2816]{1,0:T(8,128)(2,1)S(1)}, u32[]{:S(2)}, u32[]{:S(2)}) %collective-permute-start.34) | collective-permute-done | bytes 720928 | tf_op jit(solution)/shard_map/ppermute | solution.py:153
  205.4 8.8 %collective-permute-done.40.refs_9_ = bf16[64,2816]{1,0:T(8,128)(2,1)S(1)} collective-permute-done((bf16[64,2816]{1,0:T(8,128)(2,1)S(1)}, bf16[64,2816]{1,0:T(8,128)(2,1)S(1)}, u32[]{:S(2)}, u32[]{:S(2)}) %collective-permute-start.40) | collective-permute-done | bytes 360480 | tf_op jit(solution)/shard_map/ppermute | solution.py:154
  226.7 5.5 collective-permute-done.41.refs_4_
  235.9 22.3 %shard_map.308 = (bf16[1280,2816]{1,0:T(8,128)(2,1)}, bf16[1280,2816]{1,0:T(8,128)(2,1)}, bf16[2816,1024]{1,0:T(8,128)(2,1)}) custom-call(bf16[1280,1024]{1,0:T(8,128)(2,1)} %copy-done.8, bf16[1024,2816]{1,0:T(8,128)(2,1)} %bitcast.117, bf16[1280,2816]{1,0:T(8,128)(2,1)} %get-tuple-element.209.act_ref, bf16[1280,2816]{1,0:T(8,128)(2,1)} %get-tuple-element.225.slope_ref, ...), custom_call_target="tpu_custom_call" | custom-call | flops 14763950080 | bytes 45613056 | tf_op jit(solution)/shard_map/pallas_call | solution.py:698
  272.4 7.8 %convolution_convert_fusion.3 = bf16[1280,1024]{1,0:T(8,128)(2,1)S(1)} fusion(bf16[1280,2816]{1,0:T(8,128)(2,1)S(1)} %bitcast.154, bf16[2816,1024]{1,0:T(8,128)(2,1)S(1)} %bitcast.125), kind=kOutput, calls=%fused_computation.14 | convolution fusion | flops 7383285760 | bytes 15597568 | tf_op jit(solution)/shard_map/dot_general | solution.py:82
  287.6 30.8 %shard_map.312.refs_0_.refs_1_.pre_ref.up_ref = bf16[4,1280,2816]{2,1,0:T(8,128)(2,1)} custom-call(bf16[1280,1024]{1,0:T(8,128)(2,1)} %multiply_convert_fusion.grads_ref, bf16[2816,1024]{1,0:T(8,128)(2,1)} %bitcast.126, bf16[1280,2816]{1,0:T(8,128)(2,1)} %get-tuple-element.241.lift_ref, bf16[1280,2816]{1,0:T(8,128)(2,1)} %get-tuple-element.209.act_ref, ...), custom_call_target="tpu_custom_call" | custom-call | flops 22145925120 | bytes 54263808 | tf_op jit(solution)/shard_map/pallas_call | solution.py:698
  328.3 22.6 %shard_map.315 = (bf16[320,1024]{1,0:T(8,128)(2,1)}, bf16[320,1024]{1,0:T(8,128)(2,1)}, bf16[640,1024]{1,0:T(8,128)(2,1)}) custom-call(bf16[4,1280,2816]{2,1,0:T(8,128)(2,1)} %shard_map.312.refs_0_.refs_1_.pre_ref.up_ref, bf16[4,1280,2816]{2,1,0:T(8,128)(2,1)} %shard_map.312.refs_0_.refs_1_.pre_ref.up_ref, bf16[1024,2816]{1,0:T(8,128)(2,1)} %bitcast.116, ...), custom_call_target="tpu_custom_call" | custom-call | flops 14763950080 | bytes 71827456 | tf_op jit(solution)/shard_map/pallas_call | solution.py:698
  364.2 18.0 %collective-permute-done.61.refs_3_ = bf16[640,1024]{1,0:T(8,128)(2,1)S(1)} collective-permute-done((bf16[640,1024]{1,0:T(8,128)(2,1)}, bf16[640,1024]{1,0:T(8,128)(2,1)S(1)}, u32[]{:S(2)}, u32[]{:S(2)}) %collective-permute-start.61) | collective-permute-done | bytes 1310752 | tf_op jit(solution)/shard_map/ppermute | solution.py:283
  382.3 5.7 collective-permute-done.58.refs_2_
  411.1 21.6 %shard_map.321 = (bf16[512,1024]{1,0:T(8,128)(2,1)S(1)}, bf16[512,1024]{1,0:T(8,128)(2,1)S(1)}, bf16[512,1024]{1,0:T(8,128)(2,1)S(1)}, f32[16,3,128,128]{3,2,1,0:T(8,128)S(1)}, f32[8,2,2,128]{3,2,1,0:T(2,128)S(1)}) custom-call(s32[1]{0:T(128)S(6)} %copy.93.flag_ref, f32[2,16]{1,0:T(2,128)S(1)} %pad_maximum_fusion.3.far_ref, bf16[512,3072]{1,0:T(8,128)(2,1)S(1)} %copy-done.7, ...), custom_call_target="tpu_custom_call" | custom-call | flops 5368709120 | bytes 14680064 | tf_op jit(solution)/shard_map/pallas_call | solution.py:604
  444.1 3.8 shard_map.322
  455.8 4.4 fusion.32
  463.8 6.7 %collective-permute-done.69.refs_2_ = bf16[352,1024]{1,0:T(8,128)(2,1)S(1)} collective-permute-done((bf16[352,1024]{1,0:T(8,128)(2,1)}, bf16[352,1024]{1,0:T(8,128)(2,1)S(1)}, u32[]{:S(2)}, u32[]{:S(2)}) %collective-permute-start.69) | collective-permute-done | bytes 720928 | tf_op jit(solution)/shard_map/ppermute | solution.py:283
  473.2 3.9 fusion.23
  479.1 3.6 collective-permute-done.72.refs_1_
  499.0 8.5 %collective-permute-done.79.refs_2_ = bf16[128,2816]{1,0:T(8,128)(2,1)} collective-permute-done((bf16[128,2816]{1,0:T(8,128)(2,1)}, bf16[128,2816]{1,0:T(8,128)(2,1)}, u32[]{:S(2)}, u32[]{:S(2)}) %collective-permute-start.79) | collective-permute-done | bytes 720928 | tf_op jit(solution)/shard_map/ppermute | solution.py:283
  514.0 12.3 %collective-permute-done.80 = f32[52,128]{1,0:T(8,128)S(1)} collective-permute-done((f32[52,128]{1,0:T(8,128)S(1)}, f32[52,128]{1,0:T(8,128)S(1)}, u32[]{:S(2)}, u32[]{:S(2)}) %collective-permute-start.80) | collective-permute-done | bytes 26656 | tf_op jit(solution)/shard_map/ppermute | solution.py:400
  538.8 3.5 shard_map.329
  542.3 3.9 collective-permute-done.85
  553.6 4.4 shard_map.331
  558.0 4.4 shard_map.332
  (535 shorter events, 265.2 us)
Async XLA Ops:
  19.9 25.0 %collective-permute-start.8 = (bf16[64,4096]{1,0:T(8,128)(2,1)}, bf16[64,4096]{1,0:T(8,128)(2,1)S(1)}, u32[]{:S(2)}, u32[]{:S(2)}) collective-permute-start(bf16[64,4096]{1,0:T(8,128)(2,1)} %collective-permute-done.1.refs_3_), channel_id=1, source_target_pairs={{0,1},{1,0},{2,3},{3,2},{4,5},{5,4},{6,7},{7,6},{8,9},{9,8},{10,11... | collective-permute-start | bytes 1572872 | tf_op jit(solution)/shard_map/ppermute | solution.py:283
  42.0 22.0 %collective-permute-start.14 = (bf16[64,4096]{1,0:T(8,128)(2,1)}, bf16[64,4096]{1,0:T(8,128)(2,1)}, u32[]{:S(2)}, u32[]{:S(2)}) collective-permute-start(bf16[64,4096]{1,0:T(8,128)(2,1)} %collective-permute-done.3.refs_5_), channel_id=1, source_target_pairs={{0,1},{1,0},{2,3},{3,2},{4,5},{5,4},{6,7},{7,6},{8,9},{9,8},{10,11... | collective-permute-start | bytes 1572872 | tf_op jit(solution)/shard_map/ppermute | solution.py:283
  103.9 36.8 %collective-permute-start.22 = (bf16[640,1024]{1,0:T(8,128)(2,1)S(1)}, bf16[640,1024]{1,0:T(8,128)(2,1)S(1)}, u32[]{:S(2)}, u32[]{:S(2)}) collective-permute-start(bf16[640,1024]{1,0:T(8,128)(2,1)S(1)} %convolution_convert_fusion.4), channel_id=1, source_target_pairs={{0,2},{1,3},{2,0},{3,1},{4,6},{5,7},{6,4},{7,5},{8,10},{9,11},{10,... | collective-permute-start | bytes 3932168 | tf_op jit(solution)/shard_map/ppermute | solution.py:283
  118.8 22.1 %collective-permute-start.21 = (bf16[320,1024]{1,0:T(8,128)(2,1)S(1)}, bf16[320,1024]{1,0:T(8,128)(2,1)S(1)}, u32[]{:S(2)}, u32[]{:S(2)}) collective-permute-start(bf16[320,1024]{1,0:T(8,128)(2,1)S(1)} %convolution_convert_fusion.9), channel_id=1, source_target_pairs={{0,1},{1,0},{2,3},{3,2},{4,5},{5,4},{6,7},{7,6},{8,9},{9,8},{10,11... | collective-permute-start | bytes 1966088 | tf_op jit(solution)/shard_map/ppermute | solution.py:283
  145.9 25.3 %collective-permute-start.30 = (bf16[128,2816]{1,0:T(8,128)(2,1)S(1)}, bf16[128,2816]{1,0:T(8,128)(2,1)S(1)}, u32[]{:S(2)}, u32[]{:S(2)}) collective-permute-start(bf16[128,2816]{1,0:T(8,128)(2,1)S(1)} %collective-permute-done.25.refs_2_), channel_id=1, source_target_pairs={{0,4},{4,12},{12,20},{20,28},{28,24},{24,16},{16,8},{8,0},{1,5},{5... | collective-permute-start | bytes 2162696 | tf_op jit(solution)/shard_map/ppermute | solution.py:153
  147.5 23.7 %collective-permute-start.31 = (bf16[128,2816]{1,0:T(8,128)(2,1)S(1)}, bf16[128,2816]{1,0:T(8,128)(2,1)}, u32[]{:S(2)}, u32[]{:S(2)}) collective-permute-start(bf16[128,2816]{1,0:T(8,128)(2,1)S(1)} %collective-permute-done.26.refs_3_), channel_id=1, source_target_pairs={{4,0},{12,4},{20,12},{28,20},{24,28},{16,24},{8,16},{0,8},{5,1},{1... | collective-permute-start | bytes 2162696 | tf_op jit(solution)/shard_map/ppermute | solution.py:154
  147.9 57.5 %collective-permute-start.38 = (bf16[352,1024]{1,0:T(8,128)(2,1)}, bf16[352,1024]{1,0:T(8,128)(2,1)}, u32[]{:S(2)}, u32[]{:S(2)}) collective-permute-start(bf16[352,1024]{1,0:T(8,128)(2,1)} %dynamic-slice_bitcast_fusion.refs_1_), channel_id=1, source_target_pairs={{4,0},{12,4},{20,12},{28,20},{24,28},{16,24},{8,16},{0,8},{5,1},{1... | collective-permute-start | bytes 2162696 | tf_op jit(solution)/shard_map/ppermute | solution.py:154
  148.4 57.0 %collective-permute-start.37 = (bf16[352,1024]{1,0:T(8,128)(2,1)}, bf16[352,1024]{1,0:T(8,128)(2,1)}, u32[]{:S(2)}, u32[]{:S(2)}) collective-permute-start(bf16[352,1024]{1,0:T(8,128)(2,1)} %dynamic-slice_bitcast_fusion.refs_1_), channel_id=1, source_target_pairs={{0,4},{4,12},{12,20},{20,28},{28,24},{24,16},{16,8},{8,0},{1,5},{5... | collective-permute-start | bytes 2162696 | tf_op jit(solution)/shard_map/ppermute | solution.py:153
  150.8 30.2 %collective-permute-start.33 = (bf16[640,1024]{1,0:T(8,128)(2,1)}, bf16[640,1024]{1,0:T(8,128)(2,1)}, u32[]{:S(2)}, u32[]{:S(2)}) collective-permute-start(bf16[640,1024]{1,0:T(8,128)(2,1)} %convolution_convert_fusion.5), channel_id=1, source_target_pairs={{0,2},{1,3},{2,0},{3,1},{4,6},{5,7},{6,4},{7,5},{8,10},{9,11},{10,... | collective-permute-start | bytes 3932168 | tf_op jit(solution)/shard_map/ppermute | solution.py:283
  172.1 23.2 %collective-permute-start.34 = (bf16[128,2816]{1,0:T(8,128)(2,1)}, bf16[128,2816]{1,0:T(8,128)(2,1)S(1)}, u32[]{:S(2)}, u32[]{:S(2)}) collective-permute-start(bf16[128,2816]{1,0:T(8,128)(2,1)} %copy-done.42), channel_id=1, source_target_pairs={{0,4},{4,12},{12,20},{20,28},{28,24},{24,16},{16,8},{8,0},{1,5},{5... | collective-permute-start | bytes 2162696 | tf_op jit(solution)/shard_map/ppermute | solution.py:153
  173.6 23.0 %collective-permute-start.35 = (bf16[128,2816]{1,0:T(8,128)(2,1)}, bf16[128,2816]{1,0:T(8,128)(2,1)}, u32[]{:S(2)}, u32[]{:S(2)}) collective-permute-start(bf16[128,2816]{1,0:T(8,128)(2,1)} %collective-permute-done.31.refs_5_), channel_id=1, source_target_pairs={{4,0},{12,4},{20,12},{28,20},{24,28},{16,24},{8,16},{0,8},{5,1},{1... | collective-permute-start | bytes 2162696 | tf_op jit(solution)/shard_map/ppermute | solution.py:154
  233.9 24.3 %collective-permute-start.43 = (bf16[352,1024]{1,0:T(8,128)(2,1)S(1)}, bf16[352,1024]{1,0:T(8,128)(2,1)S(1)}, u32[]{:S(2)}, u32[]{:S(2)}) collective-permute-start(bf16[352,1024]{1,0:T(8,128)(2,1)S(1)} %collective-permute-done.41.refs_4_), channel_id=1, source_target_pairs={{0,4},{4,12},{12,20},{20,28},{28,24},{24,16},{16,8},{8,0},{1,5},{5... | collective-permute-start | bytes 2162696 | tf_op jit(solution)/shard_map/ppermute | solution.py:153
  235.3 22.9 %collective-permute-start.44 = (bf16[352,1024]{1,0:T(8,128)(2,1)S(1)}, bf16[352,1024]{1,0:T(8,128)(2,1)S(1)}, u32[]{:S(2)}, u32[]{:S(2)}) collective-permute-start(bf16[352,1024]{1,0:T(8,128)(2,1)S(1)} %collective-permute-done.42.refs_5_), channel_id=1, source_target_pairs={{4,0},{12,4},{20,12},{28,20},{24,28},{16,24},{8,16},{0,8},{5,1},{1... | collective-permute-start | bytes 2162696 | tf_op jit(solution)/shard_map/ppermute | solution.py:154
  284.1 34.3 %collective-permute-start.49 = (bf16[2,352,512]{2,1,0:T(8,128)(2,1)}, bf16[2,352,512]{2,1,0:T(8,128)(2,1)S(1)}, u32[]{:S(2)}, u32[]{:S(2)}) collective-permute-start(bf16[2,352,512]{2,1,0:T(8,128)(2,1)} %get-tuple-element.238), channel_id=1, source_target_pairs={{0,4},{4,12},{12,20},{20,28},{28,24},{24,16},{16,8},{8,0},{1,5},{5... | collective-permute-start | bytes 2162696 | tf_op jit(solution)/shard_map/ppermute | solution.py:266
  286.0 32.4 %collective-permute-start.50 = (bf16[2,352,512]{2,1,0:T(8,128)(2,1)S(1)}, bf16[2,352,512]{2,1,0:T(8,128)(2,1)S(1)}, u32[]{:S(2)}, u32[]{:S(2)}) collective-permute-start(bf16[2,352,512]{2,1,0:T(8,128)(2,1)S(1)} %get-tuple-element.239), channel_id=1, source_target_pairs={{4,0},{12,4},{20,12},{28,20},{24,28},{16,24},{8,16},{0,8},{5,1},{1... | collective-permute-start | bytes 2162696 | tf_op jit(solution)/shard_map/ppermute | solution.py:267
  286.1 32.3 %collective-permute-start.51 = (bf16[320,1024]{1,0:T(8,128)(2,1)}, bf16[320,1024]{1,0:T(8,128)(2,1)S(1)}, u32[]{:S(2)}, u32[]{:S(2)}) collective-permute-start(bf16[320,1024]{1,0:T(8,128)(2,1)} %get-tuple-element.242), channel_id=1, source_target_pairs={{0,1},{1,0},{2,3},{3,2},{4,5},{5,4},{6,7},{7,6},{8,9},{9,8},{10,11... | collective-permute-start | bytes 1966088 | tf_op jit(solution)/shard_map/ppermute | solution.py:283
  286.1 32.3 %collective-permute-start.52 = (bf16[640,1024]{1,0:T(8,128)(2,1)}, bf16[640,1024]{1,0:T(8,128)(2,1)S(1)}, u32[]{:S(2)}, u32[]{:S(2)}) collective-permute-start(bf16[640,1024]{1,0:T(8,128)(2,1)} %slice.148), channel_id=1, source_target_pairs={{0,2},{1,3},{2,0},{3,1},{4,6},{5,7},{6,4},{7,5},{8,10},{9,11},{10,... | collective-permute-start | bytes 3932168 | tf_op jit(solution)/shard_map/ppermute | solution.py:283
  322.1 28.8 %collective-permute-start.53 = (bf16[1,128,2816]{2,1,0:T(8,128)(2,1)}, bf16[1,128,2816]{2,1,0:T(8,128)(2,1)S(1)}, u32[]{:S(2)}, u32[]{:S(2)}) collective-permute-start(bf16[1,128,2816]{2,1,0:T(8,128)(2,1)} %get-tuple-element.246), channel_id=1, source_target_pairs={{0,4},{4,12},{12,20},{20,28},{28,24},{24,16},{16,8},{8,0},{1,5},{5... | collective-permute-start | bytes 2162696 | tf_op jit(solution)/shard_map/ppermute | solution.py:266
  324.0 27.5 %collective-permute-start.54 = (bf16[1,128,2816]{2,1,0:T(8,128)(2,1)}, bf16[1,128,2816]{2,1,0:T(8,128)(2,1)S(1)}, u32[]{:S(2)}, u32[]{:S(2)}) collective-permute-start(bf16[1,128,2816]{2,1,0:T(8,128)(2,1)} %get-tuple-element.247), channel_id=1, source_target_pairs={{4,0},{12,4},{20,12},{28,20},{24,28},{16,24},{8,16},{0,8},{5,1},{1... | collective-permute-start | bytes 2162696 | tf_op jit(solution)/shard_map/ppermute | solution.py:267
  326.1 30.2 %collective-permute-start.56 = (bf16[2,352,512]{2,1,0:T(8,128)(2,1)}, bf16[2,352,512]{2,1,0:T(8,128)(2,1)S(1)}, u32[]{:S(2)}, u32[]{:S(2)}) collective-permute-start(bf16[2,352,512]{2,1,0:T(8,128)(2,1)} %get-tuple-element.251), channel_id=1, source_target_pairs={{0,4},{4,12},{12,20},{20,28},{28,24},{24,16},{16,8},{8,0},{1,5},{5... | collective-permute-start | bytes 2162696 | tf_op jit(solution)/shard_map/ppermute | solution.py:266
  328.0 29.7 %collective-permute-start.57 = (bf16[2,352,512]{2,1,0:T(8,128)(2,1)}, bf16[2,352,512]{2,1,0:T(8,128)(2,1)S(1)}, u32[]{:S(2)}, u32[]{:S(2)}) collective-permute-start(bf16[2,352,512]{2,1,0:T(8,128)(2,1)} %get-tuple-element.252), channel_id=1, source_target_pairs={{4,0},{12,4},{20,12},{28,20},{24,28},{16,24},{8,16},{0,8},{5,1},{1... | collective-permute-start | bytes 2162696 | tf_op jit(solution)/shard_map/ppermute | solution.py:267
  350.9 48.9 %collective-permute-start.60 = (bf16[320,1024]{1,0:T(8,128)(2,1)}, bf16[320,1024]{1,0:T(8,128)(2,1)S(1)}, u32[]{:S(2)}, u32[]{:S(2)}) collective-permute-start(bf16[320,1024]{1,0:T(8,128)(2,1)} %get-tuple-element.255), channel_id=1, source_target_pairs={{0,1},{1,0},{2,3},{3,2},{4,5},{5,4},{6,7},{7,6},{8,9},{9,8},{10,11... | collective-permute-start | bytes 1966088 | tf_op jit(solution)/shard_map/ppermute | solution.py:283
  350.9 31.4 %collective-permute-start.61 = (bf16[640,1024]{1,0:T(8,128)(2,1)}, bf16[640,1024]{1,0:T(8,128)(2,1)S(1)}, u32[]{:S(2)}, u32[]{:S(2)}) collective-permute-start(bf16[640,1024]{1,0:T(8,128)(2,1)} %get-tuple-element.256), channel_id=1, source_target_pairs={{0,2},{1,3},{2,0},{3,1},{4,6},{5,7},{6,4},{7,5},{8,10},{9,11},{10,... | collective-permute-start | bytes 3932168 | tf_op jit(solution)/shard_map/ppermute | solution.py:283
  354.3 33.7 %collective-permute-start.58 = (bf16[2,128,2816]{2,1,0:T(8,128)(2,1)S(1)}, bf16[2,128,2816]{2,1,0:T(8,128)(2,1)S(1)}, u32[]{:S(2)}, u32[]{:S(2)}) collective-permute-start(bf16[2,128,2816]{2,1,0:T(8,128)(2,1)S(1)} %get-tuple-element.259), channel_id=1, source_target_pairs={{0,4},{4,12},{12,20},{20,28},{28,24},{24,16},{16,8},{8,0},{1,5},{5... | collective-permute-start | bytes 4325384 | tf_op jit(solution)/shard_map/ppermute | solution.py:266
  356.2 33.4 %collective-permute-start.59 = (bf16[2,128,2816]{2,1,0:T(8,128)(2,1)S(1)}, bf16[2,128,2816]{2,1,0:T(8,128)(2,1)S(1)}, u32[]{:S(2)}, u32[]{:S(2)}) collective-permute-start(bf16[2,128,2816]{2,1,0:T(8,128)(2,1)S(1)} %get-tuple-element.260), channel_id=1, source_target_pairs={{4,0},{12,4},{20,12},{28,20},{24,28},{16,24},{8,16},{0,8},{5,1},{1... | collective-permute-start | bytes 4325384 | tf_op jit(solution)/shard_map/ppermute | solution.py:267
  393.4 39.4 %collective-permute-start.63 = (bf16[2,352,512]{2,1,0:T(8,128)(2,1)S(1)}, bf16[2,352,512]{2,1,0:T(8,128)(2,1)S(1)}, u32[]{:S(2)}, u32[]{:S(2)}) collective-permute-start(bf16[2,352,512]{2,1,0:T(8,128)(2,1)S(1)} %get-tuple-element.265), channel_id=1, source_target_pairs={{0,4},{4,12},{12,20},{20,28},{28,24},{24,16},{16,8},{8,0},{1,5},{5... | collective-permute-start | bytes 2162696 | tf_op jit(solution)/shard_map/ppermute | solution.py:266
  394.9 37.8 %collective-permute-start.64 = (bf16[2,352,512]{2,1,0:T(8,128)(2,1)S(1)}, bf16[2,352,512]{2,1,0:T(8,128)(2,1)S(1)}, u32[]{:S(2)}, u32[]{:S(2)}) collective-permute-start(bf16[2,352,512]{2,1,0:T(8,128)(2,1)S(1)} %get-tuple-element.266), channel_id=1, source_target_pairs={{4,0},{12,4},{20,12},{28,20},{24,28},{16,24},{8,16},{0,8},{5,1},{1... | collective-permute-start | bytes 2162696 | tf_op jit(solution)/shard_map/ppermute | solution.py:267
  398.2 44.7 %collective-permute-start.66 = (bf16[2,128,2816]{2,1,0:T(8,128)(2,1)S(1)}, bf16[2,128,2816]{2,1,0:T(8,128)(2,1)S(1)}, u32[]{:S(2)}, u32[]{:S(2)}) collective-permute-start(bf16[2,128,2816]{2,1,0:T(8,128)(2,1)S(1)} %get-tuple-element.269), channel_id=1, source_target_pairs={{0,4},{4,12},{12,20},{20,28},{28,24},{24,16},{16,8},{8,0},{1,5},{5... | collective-permute-start | bytes 4325384 | tf_op jit(solution)/shard_map/ppermute | solution.py:266
  399.7 44.3 %collective-permute-start.67 = (bf16[2,128,2816]{2,1,0:T(8,128)(2,1)S(1)}, bf16[2,128,2816]{2,1,0:T(8,128)(2,1)S(1)}, u32[]{:S(2)}, u32[]{:S(2)}) collective-permute-start(bf16[2,128,2816]{2,1,0:T(8,128)(2,1)S(1)} %get-tuple-element.270), channel_id=1, source_target_pairs={{4,0},{12,4},{20,12},{28,20},{24,28},{16,24},{8,16},{0,8},{5,1},{1... | collective-permute-start | bytes 4325384 | tf_op jit(solution)/shard_map/ppermute | solution.py:267
  405.7 27.0 %collective-permute-start.65 = (bf16[8,64,1024]{2,1,0:T(8,128)(2,1)S(1)}, bf16[8,64,1024]{2,1,0:T(8,128)(2,1)S(1)}, u32[]{:S(2)}, u32[]{:S(2)}) collective-permute-start(bf16[8,64,1024]{2,1,0:T(8,128)(2,1)S(1)} %bitcast.137), channel_id=1, source_target_pairs={{0,1},{1,0},{2,3},{3,2},{4,5},{5,4},{6,7},{7,6},{8,9},{9,8},{10,11... | collective-permute-start | bytes 3145736 | tf_op jit(solution)/shard_map/ppermute | solution.py:283
  447.9 34.8 %collective-permute-start.72 = (bf16[2,128,2816]{2,1,0:T(8,128)(2,1)}, bf16[2,128,2816]{2,1,0:T(8,128)(2,1)}, u32[]{:S(2)}, u32[]{:S(2)}) collective-permute-start(bf16[2,128,2816]{2,1,0:T(8,128)(2,1)} %get-tuple-element.286), channel_id=1, source_target_pairs={{0,4},{4,12},{12,20},{20,28},{28,24},{24,16},{16,8},{8,0},{1,5},{5... | collective-permute-start | bytes 4325384 | tf_op jit(solution)/shard_map/ppermute | solution.py:266
  449.3 35.0 %collective-permute-start.73 = (bf16[2,128,2816]{2,1,0:T(8,128)(2,1)}, bf16[2,128,2816]{2,1,0:T(8,128)(2,1)}, u32[]{:S(2)}, u32[]{:S(2)}) collective-permute-start(bf16[2,128,2816]{2,1,0:T(8,128)(2,1)} %get-tuple-element.287), channel_id=1, source_target_pairs={{4,0},{12,4},{20,12},{28,20},{24,28},{16,24},{8,16},{0,8},{5,1},{1... | collective-permute-start | bytes 4325384 | tf_op jit(solution)/shard_map/ppermute | solution.py:267
  (177 other events, 1733.6 us)

commit v3 on v2

--- a/solution.py
+++ b/solution.py
@@ -972,8 +972,7 @@
     cot_exchange.forward(slot_gate, slot_rows_t, *up_ring.arrived())
     slot_cots = cot_exchange.together(seat)
     slot_grads = (slot_gate * slot_cots.astype(jnp.float32)).astype(jnp.bfloat16)
-    context_mine, context_other = core_columns(after(context, *up_ring.sent))
-    up_ring.step(slot_gate, slot_rows_t, context_mine, context_other)
+    up_ring.step(slot_gate, slot_rows_t)
     down_ring.step(*up_ring.arrived())
     up_full = up_ring.finish(*down_ring.sent, slot_grads)
     down_ring.step(up_full, slot_grads)
@@ -1018,7 +1017,8 @@
     grad_logits = (
         router * (grad_router - jnp.sum(router * grad_router, -1, keepdims=True))
     ).astype(jnp.bfloat16)
-    returned_grads.forward(grad_logits, *gate_up_sum.arrived())
+    context_mine, context_other = core_columns(after(context, grad_logits))
+    returned_grads.forward(grad_logits, context_mine, context_other, *gate_up_sum.arrived())
     down_sum.step(grad_logits, *gate_up_sum.arrived())
     gate_up_sum.step(*down_sum.sent)
     returned_grads = returned_grads.together(seat, *gate_up_sum.sent)

time: 582 us -> 578 us (level)
  waiting for transfers between devices: 171 us -> 163 us
    ppermute x16, waiting for transfers between devices: 42.3 us -> 15.3 us  [step(): self.high = lax.ppermute(high, 'dp', self.behind)]
    ppermute x16, waiting for transfers between devices: 47.3 us -> 73 us  [step(): self.low = lax.ppermute(low, 'dp', self.ahead)]
    ppermute x33, waiting for transfers between devices: 42 us -> 35.2 us  [swap(): return lax.ppermute(value, 'expert', [(i, i ^ bit) for i in range(count)])]
    unnamed x237 -> x207, local copies, waits for them, and re-layouts: 30.3 us -> 29.5 us
  transfers between devices with their start and end apart: 94 -> 94, of which waited for: 41 -> 42; matrix products, arithmetic and copies ran while one was open for 17% -> 17% of each run, Pallas kernels for 31% -> 33%
where the time goes in v3:
time: 578 us; the launch traced here: 568 us
  Pallas kernels  196 us (34%)
  waiting for transfers between devices  163 us (28%)
  starting transfers between devices  79.6 us (14%)
  local copies, waits for them, and re-layouts  60.9 us (11%)
  matrix products  51.6 us (9%)
  other arithmetic  13.6 us (2%)
    pallas_call x4, Pallas kernels, kernel_call(): pl.pallas_call(kernel, grid=(steps,), in_specs=in_specs, out_specs=out_sp...  94.4 us
    ppermute x16, waiting for transfers between devices, step(): self.low = lax.ppermute(low, 'dp', self.ahead)  73 us
    ppermute x33, waiting for transfers between devices, swap(): return lax.ppermute(value, 'expert', [(i, i ^ bit) for i in range(count)])  35.2 us
    pallas_call x15, Pallas kernels, call(): pl.pallas_call(lambda seat_ref, *refs: ring_sum_kernel(received, len(own)...  31.8 us
    dot_general x16, matrix products, matmul(): return jnp.dot(left, right, preferred_element_type=jnp.float32)  30.5 us
    unnamed x207, local copies, waits for them, and re-layouts  29.5 us
    ppermute x5, waiting for transfers between devices, hop(): self.flat = flat + lax.ppermute(flat, axis, pairs)  23.7 us
    pallas_call x9, Pallas kernels, lay_together(): pl.pallas_call(lambda *refs: lay_kernel(places, *refs), grid_spec=pltpu.P...  22.8 us
  transfers between devices with their start and end apart: 94, of which 42 were waited for; matrix products, arithmetic and copies ran while one was open for 17% of the time, Pallas kernels for 33%

profile of v3, /device:TPU:0, one launch (start us, length us, event | category | flops | bytes accessed | tf_op | source)
XLA Modules:
  0.0 568.3 jit_solution(13531380983353757011)
XLA Ops:
  13.9 4.2 collective-permute-done.refs_2_
  22.5 9.8 %collective-permute-done.2.refs_4_ = bf16[64,4096]{1,0:T(8,128)(2,1)} collective-permute-done((bf16[64,4096]{1,0:T(8,128)(2,1)}, bf16[64,4096]{1,0:T(8,128)(2,1)}, u32[]{:S(2)}, u32[]{:S(2)}) %collective-permute-start.2) | collective-permute-done | bytes 524320 | tf_op jit(solution)/shard_map/ppermute | solution.py:153
  70.1 4.7 shard_map.300
  74.8 3.8 shard_map.302
  81.0 3.6 convolution_convert_fusion.2.q_ref.k_ref.v_ref
  84.7 12.3 %shard_map.301 = (bf16[512,1024]{1,0:T(8,128)(2,1)S(1)}, f32[1,8,2,512]{3,2,1,0:T(2,128)S(1)}) custom-call(s32[1]{0:T(128)S(6)} %copy.93.flag_ref, f32[2,16]{1,0:T(2,128)S(1)} %pad_maximum_fusion.3.far_ref, bf16[512,3072]{1,0:T(8,128)(2,1)S(1)} %convolution_convert_fusion.2.q_ref.k_ref.v_ref, ...), custom_call_target="tpu_custom_call" | custom-call | flops 2147483648 | bytes 7340032 | tf_op jit(solution)/shard_map/pallas_call | solution.py:485
  106.3 8.8 %collective-permute-done.23.refs_6_ = bf16[128,2816]{1,0:T(8,128)(2,1)S(1)} collective-permute-done((bf16[128,2816]{1,0:T(8,128)(2,1)S(1)}, bf16[128,2816]{1,0:T(8,128)(2,1)S(1)}, u32[]{:S(2)}, u32[]{:S(2)}) %collective-permute-start.23) | collective-permute-done | bytes 720928 | tf_op jit(solution)/shard_map/ppermute | solution.py:153
  117.9 8.8 %collective-permute-done.27.refs_8_ = bf16[64,2816]{1,0:T(8,128)(2,1)S(1)} collective-permute-done((bf16[64,2816]{1,0:T(8,128)(2,1)S(1)}, bf16[64,2816]{1,0:T(8,128)(2,1)S(1)}, u32[]{:S(2)}, u32[]{:S(2)}) %collective-permute-start.27) | collective-permute-done | bytes 360480 | tf_op jit(solution)/shard_map/ppermute | solution.py:153
  133.9 5.4 collective-permute-done.25.refs_2_
  151.0 18.8 %shard_map.305 = (bf16[1280,2816]{1,0:T(8,128)(2,1)}, bf16[1280,2816]{1,0:T(8,128)(2,1)}) custom-call(bf16[1280,1024]{1,0:T(8,128)(2,1)} %copy-done.9, bf16[1024,2816]{1,0:T(8,128)(2,1)} %bitcast.115), custom_call_target="tpu_custom_call" | custom-call | flops 7381975040 | bytes 22806528 | tf_op jit(solution)/shard_map/pallas_call | solution.py:698
  179.8 14.1 %collective-permute-done.34.refs_6_ = bf16[128,2816]{1,0:T(8,128)(2,1)S(1)} collective-permute-done((bf16[128,2816]{1,0:T(8,128)(2,1)}, bf16[128,2816]{1,0:T(8,128)(2,1)S(1)}, u32[]{:S(2)}, u32[]{:S(2)}) %collective-permute-start.34) | collective-permute-done | bytes 720928 | tf_op jit(solution)/shard_map/ppermute | solution.py:153
  198.6 7.7 %collective-permute-done.39.refs_8_ = bf16[64,2816]{1,0:T(8,128)(2,1)S(1)} collective-permute-done((bf16[64,2816]{1,0:T(8,128)(2,1)S(1)}, bf16[64,2816]{1,0:T(8,128)(2,1)S(1)}, u32[]{:S(2)}, u32[]{:S(2)}) %collective-permute-start.39) | collective-permute-done | bytes 360480 | tf_op jit(solution)/shard_map/ppermute | solution.py:153
  220.8 5.3 collective-permute-done.41.refs_4_
  229.9 22.1 %shard_map.308 = (bf16[1280,2816]{1,0:T(8,128)(2,1)}, bf16[1280,2816]{1,0:T(8,128)(2,1)}, bf16[2816,1024]{1,0:T(8,128)(2,1)}) custom-call(bf16[1280,1024]{1,0:T(8,128)(2,1)} %copy-done.9, bf16[1024,2816]{1,0:T(8,128)(2,1)} %bitcast.117, bf16[1280,2816]{1,0:T(8,128)(2,1)} %get-tuple-element.209.act_ref, bf16[1280,2816]{1,0:T(8,128)(2,1)} %get-tuple-element.224.slope_ref, ...), custom_call_target="tpu_custom_call" | custom-call | flops 14763950080 | bytes 45613056 | tf_op jit(solution)/shard_map/pallas_call | solution.py:698
  267.1 7.8 %convolution_convert_fusion.3 = bf16[1280,1024]{1,0:T(8,128)(2,1)S(1)} fusion(bf16[1280,2816]{1,0:T(8,128)(2,1)S(1)} %bitcast.154, bf16[2816,1024]{1,0:T(8,128)(2,1)S(1)} %bitcast.125), kind=kOutput, calls=%fused_computation.14 | convolution fusion | flops 7383285760 | bytes 15597568 | tf_op jit(solution)/shard_map/dot_general | solution.py:82
  282.4 30.9 %shard_map.312.refs_0_.refs_1_.pre_ref.up_ref = bf16[4,1280,2816]{2,1,0:T(8,128)(2,1)} custom-call(bf16[1280,1024]{1,0:T(8,128)(2,1)} %multiply_convert_fusion.grads_ref, bf16[2816,1024]{1,0:T(8,128)(2,1)} %bitcast.126, bf16[1280,2816]{1,0:T(8,128)(2,1)} %get-tuple-element.240.lift_ref, bf16[1280,2816]{1,0:T(8,128)(2,1)} %get-tuple-element.209.act_ref, ...), custom_call_target="tpu_custom_call" | custom-call | flops 22145925120 | bytes 54263808 | tf_op jit(solution)/shard_map/pallas_call | solution.py:698
  323.4 22.6 %shard_map.315 = (bf16[320,1024]{1,0:T(8,128)(2,1)}, bf16[320,1024]{1,0:T(8,128)(2,1)}, bf16[640,1024]{1,0:T(8,128)(2,1)}) custom-call(bf16[4,1280,2816]{2,1,0:T(8,128)(2,1)} %shard_map.312.refs_0_.refs_1_.pre_ref.up_ref, bf16[4,1280,2816]{2,1,0:T(8,128)(2,1)} %shard_map.312.refs_0_.refs_1_.pre_ref.up_ref, bf16[1024,2816]{1,0:T(8,128)(2,1)} %bitcast.116, ...), custom_call_target="tpu_custom_call" | custom-call | flops 14763950080 | bytes 71827456 | tf_op jit(solution)/shard_map/pallas_call | solution.py:698
  346.6 3.7 shard_map.316
  362.5 13.4 %collective-permute-done.61.refs_3_ = bf16[640,1024]{1,0:T(8,128)(2,1)S(1)} collective-permute-done((bf16[640,1024]{1,0:T(8,128)(2,1)}, bf16[640,1024]{1,0:T(8,128)(2,1)S(1)}, u32[]{:S(2)}, u32[]{:S(2)}) %collective-permute-start.61) | collective-permute-done | bytes 1310752 | tf_op jit(solution)/shard_map/ppermute | solution.py:283
  375.9 8.5 %collective-permute-done.58.refs_2_ = bf16[2,128,2816]{2,1,0:T(8,128)(2,1)S(1)} collective-permute-done((bf16[2,128,2816]{2,1,0:T(8,128)(2,1)}, bf16[2,128,2816]{2,1,0:T(8,128)(2,1)S(1)}, u32[]{:S(2)}, u32[]{:S(2)}) %collective-permute-start.58) | collective-permute-done | bytes 1441824 | tf_op jit(solution)/shard_map/ppermute | solution.py:266
  409.7 21.7 %shard_map.321 = (bf16[512,1024]{1,0:T(8,128)(2,1)S(1)}, bf16[512,1024]{1,0:T(8,128)(2,1)S(1)}, bf16[512,1024]{1,0:T(8,128)(2,1)S(1)}, f32[16,3,128,128]{3,2,1,0:T(8,128)S(1)}, f32[8,2,2,128]{3,2,1,0:T(2,128)S(1)}) custom-call(s32[1]{0:T(128)S(6)} %copy.93.flag_ref, f32[2,16]{1,0:T(2,128)S(1)} %pad_maximum_fusion.3.far_ref, bf16[512,3072]{1,0:T(8,128)(2,1)S(1)} %copy-done.8, ...), custom_call_target="tpu_custom_call" | custom-call | flops 5368709120 | bytes 14680064 | tf_op jit(solution)/shard_map/pallas_call | solution.py:604
  441.0 4.0 shard_map.322
  452.7 4.4 fusion.32
  460.7 6.6 %collective-permute-done.69.refs_2_ = bf16[352,1024]{1,0:T(8,128)(2,1)} collective-permute-done((bf16[352,1024]{1,0:T(8,128)(2,1)}, bf16[352,1024]{1,0:T(8,128)(2,1)}, u32[]{:S(2)}, u32[]{:S(2)}) %collective-permute-start.69) | collective-permute-done | bytes 720928 | tf_op jit(solution)/shard_map/ppermute | solution.py:283
  470.0 3.9 fusion.23
  475.9 3.8 collective-permute-done.72.refs_1_
  495.7 7.2 %collective-permute-done.79.refs_2_ = bf16[128,2816]{1,0:T(8,128)(2,1)} collective-permute-done((bf16[128,2816]{1,0:T(8,128)(2,1)}, bf16[128,2816]{1,0:T(8,128)(2,1)}, u32[]{:S(2)}, u32[]{:S(2)}) %collective-permute-start.79) | collective-permute-done | bytes 720928 | tf_op jit(solution)/shard_map/ppermute | solution.py:283
  510.2 12.3 %collective-permute-done.80 = f32[52,128]{1,0:T(8,128)S(1)} collective-permute-done((f32[52,128]{1,0:T(8,128)S(1)}, f32[52,128]{1,0:T(8,128)S(1)}, u32[]{:S(2)}, u32[]{:S(2)}) %collective-permute-start.80) | collective-permute-done | bytes 26656 | tf_op jit(solution)/shard_map/ppermute | solution.py:400
  532.8 4.6 shard_map.329
  537.4 4.2 collective-permute-done.85
  549.8 4.4 shard_map.331
  554.2 4.4 shard_map.332
  (505 shorter events, 267.3 us)
Async XLA Ops:
  21.6 25.1 %collective-permute-start.8 = (bf16[64,4096]{1,0:T(8,128)(2,1)}, bf16[64,4096]{1,0:T(8,128)(2,1)S(1)}, u32[]{:S(2)}, u32[]{:S(2)}) collective-permute-start(bf16[64,4096]{1,0:T(8,128)(2,1)} %collective-permute-done.1.refs_3_), channel_id=1, source_target_pairs={{0,1},{1,0},{2,3},{3,2},{4,5},{5,4},{6,7},{7,6},{8,9},{9,8},{10,11... | collective-permute-start | bytes 1572872 | tf_op jit(solution)/shard_map/ppermute | solution.py:283
  56.5 22.1 %collective-permute-start.10 = (bf16[128,2816]{1,0:T(8,128)(2,1)}, bf16[128,2816]{1,0:T(8,128)(2,1)}, u32[]{:S(2)}, u32[]{:S(2)}) collective-permute-start(bf16[128,2816]{1,0:T(8,128)(2,1)} %dynamic-slice_bitcast_fusion.2.refs_1_), channel_id=1, source_target_pairs={{4,0},{12,4},{20,12},{28,20},{24,28},{16,24},{8,16},{0,8},{5,1},{1... | collective-permute-start | bytes 2162696 | tf_op jit(solution)/shard_map/ppermute | solution.py:154
  103.7 35.8 %collective-permute-start.22 = (bf16[640,1024]{1,0:T(8,128)(2,1)S(1)}, bf16[640,1024]{1,0:T(8,128)(2,1)S(1)}, u32[]{:S(2)}, u32[]{:S(2)}) collective-permute-start(bf16[640,1024]{1,0:T(8,128)(2,1)S(1)} %convolution_convert_fusion.4), channel_id=1, source_target_pairs={{0,2},{1,3},{2,0},{3,1},{4,6},{5,7},{6,4},{7,5},{8,10},{9,11},{10,... | collective-permute-start | bytes 3932168 | tf_op jit(solution)/shard_map/ppermute | solution.py:283
  117.4 22.2 %collective-permute-start.21 = (bf16[320,1024]{1,0:T(8,128)(2,1)S(1)}, bf16[320,1024]{1,0:T(8,128)(2,1)S(1)}, u32[]{:S(2)}, u32[]{:S(2)}) collective-permute-start(bf16[320,1024]{1,0:T(8,128)(2,1)S(1)} %convolution_convert_fusion.9), channel_id=1, source_target_pairs={{0,1},{1,0},{2,3},{3,2},{4,5},{5,4},{6,7},{7,6},{8,9},{9,8},{10,11... | collective-permute-start | bytes 1966088 | tf_op jit(solution)/shard_map/ppermute | solution.py:283
  144.6 25.2 %collective-permute-start.30 = (bf16[128,2816]{1,0:T(8,128)(2,1)S(1)}, bf16[128,2816]{1,0:T(8,128)(2,1)S(1)}, u32[]{:S(2)}, u32[]{:S(2)}) collective-permute-start(bf16[128,2816]{1,0:T(8,128)(2,1)S(1)} %collective-permute-done.25.refs_2_), channel_id=1, source_target_pairs={{0,4},{4,12},{12,20},{20,28},{28,24},{24,16},{16,8},{8,0},{1,5},{5... | collective-permute-start | bytes 2162696 | tf_op jit(solution)/shard_map/ppermute | solution.py:153
  145.1 24.8 %collective-permute-start.31 = (bf16[128,2816]{1,0:T(8,128)(2,1)S(1)}, bf16[128,2816]{1,0:T(8,128)(2,1)}, u32[]{:S(2)}, u32[]{:S(2)}) collective-permute-start(bf16[128,2816]{1,0:T(8,128)(2,1)S(1)} %collective-permute-done.26.refs_3_), channel_id=1, source_target_pairs={{4,0},{12,4},{20,12},{28,20},{24,28},{16,24},{8,16},{0,8},{5,1},{1... | collective-permute-start | bytes 2162696 | tf_op jit(solution)/shard_map/ppermute | solution.py:154
  146.7 51.9 %collective-permute-start.37 = (bf16[352,1024]{1,0:T(8,128)(2,1)}, bf16[352,1024]{1,0:T(8,128)(2,1)}, u32[]{:S(2)}, u32[]{:S(2)}) collective-permute-start(bf16[352,1024]{1,0:T(8,128)(2,1)} %dynamic-slice_bitcast_fusion.refs_1_), channel_id=1, source_target_pairs={{0,4},{4,12},{12,20},{20,28},{28,24},{24,16},{16,8},{8,0},{1,5},{5... | collective-permute-start | bytes 2162696 | tf_op jit(solution)/shard_map/ppermute | solution.py:153
  147.1 51.5 %collective-permute-start.38 = (bf16[352,1024]{1,0:T(8,128)(2,1)}, bf16[352,1024]{1,0:T(8,128)(2,1)}, u32[]{:S(2)}, u32[]{:S(2)}) collective-permute-start(bf16[352,1024]{1,0:T(8,128)(2,1)} %dynamic-slice_bitcast_fusion.refs_1_), channel_id=1, source_target_pairs={{4,0},{12,4},{20,12},{28,20},{24,28},{16,24},{8,16},{0,8},{5,1},{1... | collective-permute-start | bytes 2162696 | tf_op jit(solution)/shard_map/ppermute | solution.py:154
  149.5 30.2 %collective-permute-start.33 = (bf16[640,1024]{1,0:T(8,128)(2,1)}, bf16[640,1024]{1,0:T(8,128)(2,1)}, u32[]{:S(2)}, u32[]{:S(2)}) collective-permute-start(bf16[640,1024]{1,0:T(8,128)(2,1)} %convolution_convert_fusion.5), channel_id=1, source_target_pairs={{0,2},{1,3},{2,0},{3,1},{4,6},{5,7},{6,4},{7,5},{8,10},{9,11},{10,... | collective-permute-start | bytes 3932168 | tf_op jit(solution)/shard_map/ppermute | solution.py:283
  170.8 23.2 %collective-permute-start.34 = (bf16[128,2816]{1,0:T(8,128)(2,1)}, bf16[128,2816]{1,0:T(8,128)(2,1)S(1)}, u32[]{:S(2)}, u32[]{:S(2)}) collective-permute-start(bf16[128,2816]{1,0:T(8,128)(2,1)} %copy-done.37), channel_id=1, source_target_pairs={{0,4},{4,12},{12,20},{20,28},{28,24},{24,16},{16,8},{8,0},{1,5},{5... | collective-permute-start | bytes 2162696 | tf_op jit(solution)/shard_map/ppermute | solution.py:153
  171.2 23.0 %collective-permute-start.35 = (bf16[128,2816]{1,0:T(8,128)(2,1)}, bf16[128,2816]{1,0:T(8,128)(2,1)}, u32[]{:S(2)}, u32[]{:S(2)}) collective-permute-start(bf16[128,2816]{1,0:T(8,128)(2,1)} %collective-permute-done.31.refs_5_), channel_id=1, source_target_pairs={{4,0},{12,4},{20,12},{28,20},{24,28},{16,24},{8,16},{0,8},{5,1},{1... | collective-permute-start | bytes 2162696 | tf_op jit(solution)/shard_map/ppermute | solution.py:154
  227.9 24.1 %collective-permute-start.43 = (bf16[352,1024]{1,0:T(8,128)(2,1)S(1)}, bf16[352,1024]{1,0:T(8,128)(2,1)S(1)}, u32[]{:S(2)}, u32[]{:S(2)}) collective-permute-start(bf16[352,1024]{1,0:T(8,128)(2,1)S(1)} %collective-permute-done.41.refs_4_), channel_id=1, source_target_pairs={{0,4},{4,12},{12,20},{20,28},{28,24},{24,16},{16,8},{8,0},{1,5},{5... | collective-permute-start | bytes 2162696 | tf_op jit(solution)/shard_map/ppermute | solution.py:153
  229.5 22.6 %collective-permute-start.44 = (bf16[352,1024]{1,0:T(8,128)(2,1)S(1)}, bf16[352,1024]{1,0:T(8,128)(2,1)S(1)}, u32[]{:S(2)}, u32[]{:S(2)}) collective-permute-start(bf16[352,1024]{1,0:T(8,128)(2,1)S(1)} %collective-permute-done.42.refs_5_), channel_id=1, source_target_pairs={{4,0},{12,4},{20,12},{28,20},{24,28},{16,24},{8,16},{0,8},{5,1},{1... | collective-permute-start | bytes 2162696 | tf_op jit(solution)/shard_map/ppermute | solution.py:154
  278.9 34.4 %collective-permute-start.49 = (bf16[2,352,512]{2,1,0:T(8,128)(2,1)}, bf16[2,352,512]{2,1,0:T(8,128)(2,1)S(1)}, u32[]{:S(2)}, u32[]{:S(2)}) collective-permute-start(bf16[2,352,512]{2,1,0:T(8,128)(2,1)} %get-tuple-element.237), channel_id=1, source_target_pairs={{0,4},{4,12},{12,20},{20,28},{28,24},{24,16},{16,8},{8,0},{1,5},{5... | collective-permute-start | bytes 2162696 | tf_op jit(solution)/shard_map/ppermute | solution.py:266
  280.4 32.8 %collective-permute-start.50 = (bf16[2,352,512]{2,1,0:T(8,128)(2,1)S(1)}, bf16[2,352,512]{2,1,0:T(8,128)(2,1)S(1)}, u32[]{:S(2)}, u32[]{:S(2)}) collective-permute-start(bf16[2,352,512]{2,1,0:T(8,128)(2,1)S(1)} %get-tuple-element.238), channel_id=1, source_target_pairs={{4,0},{12,4},{20,12},{28,20},{24,28},{16,24},{8,16},{0,8},{5,1},{1... | collective-permute-start | bytes 2162696 | tf_op jit(solution)/shard_map/ppermute | solution.py:267
  280.9 32.4 %collective-permute-start.52 = (bf16[640,1024]{1,0:T(8,128)(2,1)}, bf16[640,1024]{1,0:T(8,128)(2,1)S(1)}, u32[]{:S(2)}, u32[]{:S(2)}) collective-permute-start(bf16[640,1024]{1,0:T(8,128)(2,1)} %slice.148), channel_id=1, source_target_pairs={{0,2},{1,3},{2,0},{3,1},{4,6},{5,7},{6,4},{7,5},{8,10},{9,11},{10,... | collective-permute-start | bytes 3932168 | tf_op jit(solution)/shard_map/ppermute | solution.py:283
  282.4 30.9 %collective-permute-start.51 = (bf16[320,1024]{1,0:T(8,128)(2,1)}, bf16[320,1024]{1,0:T(8,128)(2,1)S(1)}, u32[]{:S(2)}, u32[]{:S(2)}) collective-permute-start(bf16[320,1024]{1,0:T(8,128)(2,1)} %get-tuple-element.241), channel_id=1, source_target_pairs={{0,1},{1,0},{2,3},{3,2},{4,5},{5,4},{6,7},{7,6},{8,9},{9,8},{10,11... | collective-permute-start | bytes 1966088 | tf_op jit(solution)/shard_map/ppermute | solution.py:283
  317.2 29.3 %collective-permute-start.53 = (bf16[1,128,2816]{2,1,0:T(8,128)(2,1)}, bf16[1,128,2816]{2,1,0:T(8,128)(2,1)S(1)}, u32[]{:S(2)}, u32[]{:S(2)}) collective-permute-start(bf16[1,128,2816]{2,1,0:T(8,128)(2,1)} %get-tuple-element.245), channel_id=1, source_target_pairs={{0,4},{4,12},{12,20},{20,28},{28,24},{24,16},{16,8},{8,0},{1,5},{5... | collective-permute-start | bytes 2162696 | tf_op jit(solution)/shard_map/ppermute | solution.py:266
  318.8 27.7 %collective-permute-start.54 = (bf16[1,128,2816]{2,1,0:T(8,128)(2,1)}, bf16[1,128,2816]{2,1,0:T(8,128)(2,1)S(1)}, u32[]{:S(2)}, u32[]{:S(2)}) collective-permute-start(bf16[1,128,2816]{2,1,0:T(8,128)(2,1)} %get-tuple-element.246), channel_id=1, source_target_pairs={{4,0},{12,4},{20,12},{28,20},{24,28},{16,24},{8,16},{0,8},{5,1},{1... | collective-permute-start | bytes 2162696 | tf_op jit(solution)/shard_map/ppermute | solution.py:267
  321.2 30.6 %collective-permute-start.56 = (bf16[2,352,512]{2,1,0:T(8,128)(2,1)}, bf16[2,352,512]{2,1,0:T(8,128)(2,1)}, u32[]{:S(2)}, u32[]{:S(2)}) collective-permute-start(bf16[2,352,512]{2,1,0:T(8,128)(2,1)} %get-tuple-element.250), channel_id=1, source_target_pairs={{0,4},{4,12},{12,20},{20,28},{28,24},{24,16},{16,8},{8,0},{1,5},{5... | collective-permute-start | bytes 2162696 | tf_op jit(solution)/shard_map/ppermute | solution.py:266
  322.8 29.7 %collective-permute-start.57 = (bf16[2,352,512]{2,1,0:T(8,128)(2,1)}, bf16[2,352,512]{2,1,0:T(8,128)(2,1)}, u32[]{:S(2)}, u32[]{:S(2)}) collective-permute-start(bf16[2,352,512]{2,1,0:T(8,128)(2,1)} %get-tuple-element.251), channel_id=1, source_target_pairs={{4,0},{12,4},{20,12},{28,20},{24,28},{16,24},{8,16},{0,8},{5,1},{1... | collective-permute-start | bytes 2162696 | tf_op jit(solution)/shard_map/ppermute | solution.py:267
  346.0 29.9 %collective-permute-start.61 = (bf16[640,1024]{1,0:T(8,128)(2,1)}, bf16[640,1024]{1,0:T(8,128)(2,1)S(1)}, u32[]{:S(2)}, u32[]{:S(2)}) collective-permute-start(bf16[640,1024]{1,0:T(8,128)(2,1)} %get-tuple-element.255), channel_id=1, source_target_pairs={{0,2},{1,3},{2,0},{3,1},{4,6},{5,7},{6,4},{7,5},{8,10},{9,11},{10,... | collective-permute-start | bytes 3932168 | tf_op jit(solution)/shard_map/ppermute | solution.py:283
  346.5 50.5 %collective-permute-start.60 = (bf16[320,1024]{1,0:T(8,128)(2,1)}, bf16[320,1024]{1,0:T(8,128)(2,1)}, u32[]{:S(2)}, u32[]{:S(2)}) collective-permute-start(bf16[320,1024]{1,0:T(8,128)(2,1)} %get-tuple-element.254), channel_id=1, source_target_pairs={{0,1},{1,0},{2,3},{3,2},{4,5},{5,4},{6,7},{7,6},{8,9},{9,8},{10,11... | collective-permute-start | bytes 1966088 | tf_op jit(solution)/shard_map/ppermute | solution.py:283
  350.2 34.2 %collective-permute-start.58 = (bf16[2,128,2816]{2,1,0:T(8,128)(2,1)}, bf16[2,128,2816]{2,1,0:T(8,128)(2,1)S(1)}, u32[]{:S(2)}, u32[]{:S(2)}) collective-permute-start(bf16[2,128,2816]{2,1,0:T(8,128)(2,1)} %get-tuple-element.258), channel_id=1, source_target_pairs={{0,4},{4,12},{12,20},{20,28},{28,24},{24,16},{16,8},{8,0},{1,5},{5... | collective-permute-start | bytes 4325384 | tf_op jit(solution)/shard_map/ppermute | solution.py:266
  351.8 34.0 %collective-permute-start.59 = (bf16[2,128,2816]{2,1,0:T(8,128)(2,1)}, bf16[2,128,2816]{2,1,0:T(8,128)(2,1)}, u32[]{:S(2)}, u32[]{:S(2)}) collective-permute-start(bf16[2,128,2816]{2,1,0:T(8,128)(2,1)} %get-tuple-element.259), channel_id=1, source_target_pairs={{4,0},{12,4},{20,12},{28,20},{24,28},{16,24},{8,16},{0,8},{5,1},{1... | collective-permute-start | bytes 4325384 | tf_op jit(solution)/shard_map/ppermute | solution.py:267
  391.2 40.2 %collective-permute-start.63 = (bf16[2,352,512]{2,1,0:T(8,128)(2,1)S(1)}, bf16[2,352,512]{2,1,0:T(8,128)(2,1)S(1)}, u32[]{:S(2)}, u32[]{:S(2)}) collective-permute-start(bf16[2,352,512]{2,1,0:T(8,128)(2,1)S(1)} %get-tuple-element.264), channel_id=1, source_target_pairs={{0,4},{4,12},{12,20},{20,28},{28,24},{24,16},{16,8},{8,0},{1,5},{5... | collective-permute-start | bytes 2162696 | tf_op jit(solution)/shard_map/ppermute | solution.py:266
  391.8 39.6 %collective-permute-start.64 = (bf16[2,352,512]{2,1,0:T(8,128)(2,1)S(1)}, bf16[2,352,512]{2,1,0:T(8,128)(2,1)S(1)}, u32[]{:S(2)}, u32[]{:S(2)}) collective-permute-start(bf16[2,352,512]{2,1,0:T(8,128)(2,1)S(1)} %get-tuple-element.265), channel_id=1, source_target_pairs={{4,0},{12,4},{20,12},{28,20},{24,28},{16,24},{8,16},{0,8},{5,1},{1... | collective-permute-start | bytes 2162696 | tf_op jit(solution)/shard_map/ppermute | solution.py:267
  396.4 44.3 %collective-permute-start.66 = (bf16[2,128,2816]{2,1,0:T(8,128)(2,1)S(1)}, bf16[2,128,2816]{2,1,0:T(8,128)(2,1)S(1)}, u32[]{:S(2)}, u32[]{:S(2)}) collective-permute-start(bf16[2,128,2816]{2,1,0:T(8,128)(2,1)S(1)} %get-tuple-element.268), channel_id=1, source_target_pairs={{0,4},{4,12},{12,20},{20,28},{28,24},{24,16},{16,8},{8,0},{1,5},{5... | collective-permute-start | bytes 4325384 | tf_op jit(solution)/shard_map/ppermute | solution.py:266
  397.0 43.9 %collective-permute-start.67 = (bf16[2,128,2816]{2,1,0:T(8,128)(2,1)S(1)}, bf16[2,128,2816]{2,1,0:T(8,128)(2,1)S(1)}, u32[]{:S(2)}, u32[]{:S(2)}) collective-permute-start(bf16[2,128,2816]{2,1,0:T(8,128)(2,1)S(1)} %get-tuple-element.269), channel_id=1, source_target_pairs={{4,0},{12,4},{20,12},{28,20},{24,28},{16,24},{8,16},{0,8},{5,1},{1... | collective-permute-start | bytes 4325384 | tf_op jit(solution)/shard_map/ppermute | solution.py:267
  404.4 27.1 %collective-permute-start.65 = (bf16[8,64,1024]{2,1,0:T(8,128)(2,1)S(1)}, bf16[8,64,1024]{2,1,0:T(8,128)(2,1)S(1)}, u32[]{:S(2)}, u32[]{:S(2)}) collective-permute-start(bf16[8,64,1024]{2,1,0:T(8,128)(2,1)S(1)} %bitcast.137), channel_id=1, source_target_pairs={{0,1},{1,0},{2,3},{3,2},{4,5},{5,4},{6,7},{7,6},{8,9},{9,8},{10,11... | collective-permute-start | bytes 3145736 | tf_op jit(solution)/shard_map/ppermute | solution.py:283
  445.0 34.8 %collective-permute-start.72 = (bf16[2,128,2816]{2,1,0:T(8,128)(2,1)}, bf16[2,128,2816]{2,1,0:T(8,128)(2,1)}, u32[]{:S(2)}, u32[]{:S(2)}) collective-permute-start(bf16[2,128,2816]{2,1,0:T(8,128)(2,1)} %get-tuple-element.286), channel_id=1, source_target_pairs={{0,4},{4,12},{12,20},{20,28},{28,24},{24,16},{16,8},{8,0},{1,5},{5... | collective-permute-start | bytes 4325384 | tf_op jit(solution)/shard_map/ppermute | solution.py:266
  445.5 35.0 %collective-permute-start.73 = (bf16[2,128,2816]{2,1,0:T(8,128)(2,1)}, bf16[2,128,2816]{2,1,0:T(8,128)(2,1)}, u32[]{:S(2)}, u32[]{:S(2)}) collective-permute-start(bf16[2,128,2816]{2,1,0:T(8,128)(2,1)} %get-tuple-element.287), channel_id=1, source_target_pairs={{4,0},{12,4},{20,12},{28,20},{24,28},{16,24},{8,16},{0,8},{5,1},{1... | collective-permute-start | bytes 4325384 | tf_op jit(solution)/shard_map/ppermute | solution.py:267
  (162 other events, 1655.3 us)

commit v4 on v3

--- a/solution.py
+++ b/solution.py
@@ -1018,7 +1018,7 @@
         router * (grad_router - jnp.sum(router * grad_router, -1, keepdims=True))
     ).astype(jnp.bfloat16)
     context_mine, context_other = core_columns(after(context, grad_logits))
-    returned_grads.forward(grad_logits, context_mine, context_other, *gate_up_sum.arrived())
+    returned_grads.forward(grad_logits, context_mine, context_other)
     down_sum.step(grad_logits, *gate_up_sum.arrived())
     gate_up_sum.step(*down_sum.sent)
     returned_grads = returned_grads.together(seat, *gate_up_sum.sent)

time: 578 us -> 576 us (level)
  transfers between devices with their start and end apart: 94 -> 94, of which waited for: 42 -> 41; matrix products, arithmetic and copies ran while one was open for 17% -> 17% of each run, Pallas kernels for 33% -> 33%
where the time goes in v4:
time: 576 us; the launch traced here: 567 us
  Pallas kernels  196 us (34%)
  waiting for transfers between devices  162 us (28%)
  starting transfers between devices  79.5 us (14%)
  local copies, waits for them, and re-layouts  60.9 us (11%)
  matrix products  51.6 us (9%)
  other arithmetic  13.6 us (2%)
    pallas_call x4, Pallas kernels, kernel_call(): pl.pallas_call(kernel, grid=(steps,), in_specs=in_specs, out_specs=out_sp...  94.4 us
    ppermute x16, waiting for transfers between devices, step(): self.low = lax.ppermute(low, 'dp', self.ahead)  73 us
    ppermute x33, waiting for transfers between devices, swap(): return lax.ppermute(value, 'expert', [(i, i ^ bit) for i in range(count)])  35.1 us
    pallas_call x15, Pallas kernels, call(): pl.pallas_call(lambda seat_ref, *refs: ring_sum_kernel(received, len(own)...  31.8 us
    dot_general x16, matrix products, matmul(): return jnp.dot(left, right, preferred_element_type=jnp.float32)  30.5 us
    unnamed x207, local copies, waits for them, and re-layouts  29.5 us
    ppermute x5, waiting for transfers between devices, hop(): self.flat = flat + lax.ppermute(flat, axis, pairs)  23.8 us
    pallas_call x9, Pallas kernels, lay_together(): pl.pallas_call(lambda *refs: lay_kernel(places, *refs), grid_spec=pltpu.P...  22.8 us
  transfers between devices with their start and end apart: 94, of which 41 were waited for; matrix products, arithmetic and copies ran while one was open for 17% of the time, Pallas kernels for 33%

profile of v4, /device:TPU:0, one launch (start us, length us, event | category | flops | bytes accessed | tf_op | source)
XLA Modules:
  0.0 566.6 jit_solution(16486564605723663244)
XLA Ops:
  13.9 4.2 collective-permute-done.refs_2_
  22.5 9.8 %collective-permute-done.2.refs_4_ = bf16[64,4096]{1,0:T(8,128)(2,1)} collective-permute-done((bf16[64,4096]{1,0:T(8,128)(2,1)}, bf16[64,4096]{1,0:T(8,128)(2,1)}, u32[]{:S(2)}, u32[]{:S(2)}) %collective-permute-start.2) | collective-permute-done | bytes 524320 | tf_op jit(solution)/shard_map/ppermute | solution.py:153
  70.1 4.7 shard_map.300
  74.8 3.8 shard_map.302
  81.0 3.6 convolution_convert_fusion.2.q_ref.k_ref.v_ref
  84.7 12.3 %shard_map.301 = (bf16[512,1024]{1,0:T(8,128)(2,1)S(1)}, f32[1,8,2,512]{3,2,1,0:T(2,128)S(1)}) custom-call(s32[1]{0:T(128)S(6)} %copy.93.flag_ref, f32[2,16]{1,0:T(2,128)S(1)} %pad_maximum_fusion.3.far_ref, bf16[512,3072]{1,0:T(8,128)(2,1)S(1)} %convolution_convert_fusion.2.q_ref.k_ref.v_ref, ...), custom_call_target="tpu_custom_call" | custom-call | flops 2147483648 | bytes 7340032 | tf_op jit(solution)/shard_map/pallas_call | solution.py:485
  106.3 8.8 %collective-permute-done.23.refs_6_ = bf16[128,2816]{1,0:T(8,128)(2,1)S(1)} collective-permute-done((bf16[128,2816]{1,0:T(8,128)(2,1)S(1)}, bf16[128,2816]{1,0:T(8,128)(2,1)S(1)}, u32[]{:S(2)}, u32[]{:S(2)}) %collective-permute-start.23) | collective-permute-done | bytes 720928 | tf_op jit(solution)/shard_map/ppermute | solution.py:153
  117.9 8.8 %collective-permute-done.27.refs_8_ = bf16[64,2816]{1,0:T(8,128)(2,1)S(1)} collective-permute-done((bf16[64,2816]{1,0:T(8,128)(2,1)S(1)}, bf16[64,2816]{1,0:T(8,128)(2,1)S(1)}, u32[]{:S(2)}, u32[]{:S(2)}) %collective-permute-start.27) | collective-permute-done | bytes 360480 | tf_op jit(solution)/shard_map/ppermute | solution.py:153
  133.9 5.4 collective-permute-done.25.refs_2_
  151.0 18.8 %shard_map.305 = (bf16[1280,2816]{1,0:T(8,128)(2,1)}, bf16[1280,2816]{1,0:T(8,128)(2,1)}) custom-call(bf16[1280,1024]{1,0:T(8,128)(2,1)} %copy-done.9, bf16[1024,2816]{1,0:T(8,128)(2,1)} %bitcast.115), custom_call_target="tpu_custom_call" | custom-call | flops 7381975040 | bytes 22806528 | tf_op jit(solution)/shard_map/pallas_call | solution.py:698
  179.8 14.1 %collective-permute-done.34.refs_6_ = bf16[128,2816]{1,0:T(8,128)(2,1)S(1)} collective-permute-done((bf16[128,2816]{1,0:T(8,128)(2,1)}, bf16[128,2816]{1,0:T(8,128)(2,1)S(1)}, u32[]{:S(2)}, u32[]{:S(2)}) %collective-permute-start.34) | collective-permute-done | bytes 720928 | tf_op jit(solution)/shard_map/ppermute | solution.py:153
  198.6 7.7 %collective-permute-done.39.refs_8_ = bf16[64,2816]{1,0:T(8,128)(2,1)S(1)} collective-permute-done((bf16[64,2816]{1,0:T(8,128)(2,1)S(1)}, bf16[64,2816]{1,0:T(8,128)(2,1)S(1)}, u32[]{:S(2)}, u32[]{:S(2)}) %collective-permute-start.39) | collective-permute-done | bytes 360480 | tf_op jit(solution)/shard_map/ppermute | solution.py:153
  220.8 5.3 collective-permute-done.41.refs_4_
  229.9 22.1 %shard_map.308 = (bf16[1280,2816]{1,0:T(8,128)(2,1)}, bf16[1280,2816]{1,0:T(8,128)(2,1)}, bf16[2816,1024]{1,0:T(8,128)(2,1)}) custom-call(bf16[1280,1024]{1,0:T(8,128)(2,1)} %copy-done.9, bf16[1024,2816]{1,0:T(8,128)(2,1)} %bitcast.117, bf16[1280,2816]{1,0:T(8,128)(2,1)} %get-tuple-element.209.act_ref, bf16[1280,2816]{1,0:T(8,128)(2,1)} %get-tuple-element.224.slope_ref, ...), custom_call_target="tpu_custom_call" | custom-call | flops 14763950080 | bytes 45613056 | tf_op jit(solution)/shard_map/pallas_call | solution.py:698
  267.1 7.8 %convolution_convert_fusion.3 = bf16[1280,1024]{1,0:T(8,128)(2,1)S(1)} fusion(bf16[1280,2816]{1,0:T(8,128)(2,1)S(1)} %bitcast.154, bf16[2816,1024]{1,0:T(8,128)(2,1)S(1)} %bitcast.125), kind=kOutput, calls=%fused_computation.14 | convolution fusion | flops 7383285760 | bytes 15597568 | tf_op jit(solution)/shard_map/dot_general | solution.py:82
  282.4 30.9 %shard_map.312.refs_0_.refs_1_.pre_ref.up_ref = bf16[4,1280,2816]{2,1,0:T(8,128)(2,1)} custom-call(bf16[1280,1024]{1,0:T(8,128)(2,1)} %multiply_convert_fusion.grads_ref, bf16[2816,1024]{1,0:T(8,128)(2,1)} %bitcast.126, bf16[1280,2816]{1,0:T(8,128)(2,1)} %get-tuple-element.240.lift_ref, bf16[1280,2816]{1,0:T(8,128)(2,1)} %get-tuple-element.209.act_ref, ...), custom_call_target="tpu_custom_call" | custom-call | flops 22145925120 | bytes 54263808 | tf_op jit(solution)/shard_map/pallas_call | solution.py:698
  323.4 22.6 %shard_map.315 = (bf16[320,1024]{1,0:T(8,128)(2,1)}, bf16[320,1024]{1,0:T(8,128)(2,1)}, bf16[640,1024]{1,0:T(8,128)(2,1)}) custom-call(bf16[4,1280,2816]{2,1,0:T(8,128)(2,1)} %shard_map.312.refs_0_.refs_1_.pre_ref.up_ref, bf16[4,1280,2816]{2,1,0:T(8,128)(2,1)} %shard_map.312.refs_0_.refs_1_.pre_ref.up_ref, bf16[1024,2816]{1,0:T(8,128)(2,1)} %bitcast.116, ...), custom_call_target="tpu_custom_call" | custom-call | flops 14763950080 | bytes 71827456 | tf_op jit(solution)/shard_map/pallas_call | solution.py:698
  346.6 3.7 shard_map.316
  362.5 13.4 %collective-permute-done.61.refs_3_ = bf16[640,1024]{1,0:T(8,128)(2,1)S(1)} collective-permute-done((bf16[640,1024]{1,0:T(8,128)(2,1)}, bf16[640,1024]{1,0:T(8,128)(2,1)S(1)}, u32[]{:S(2)}, u32[]{:S(2)}) %collective-permute-start.61) | collective-permute-done | bytes 1310752 | tf_op jit(solution)/shard_map/ppermute | solution.py:283
  376.5 7.9 %collective-permute-done.58.refs_2_ = bf16[2,128,2816]{2,1,0:T(8,128)(2,1)S(1)} collective-permute-done((bf16[2,128,2816]{2,1,0:T(8,128)(2,1)}, bf16[2,128,2816]{2,1,0:T(8,128)(2,1)S(1)}, u32[]{:S(2)}, u32[]{:S(2)}) %collective-permute-start.58) | collective-permute-done | bytes 1441824 | tf_op jit(solution)/shard_map/ppermute | solution.py:266
  409.1 21.7 %shard_map.321 = (bf16[512,1024]{1,0:T(8,128)(2,1)S(1)}, bf16[512,1024]{1,0:T(8,128)(2,1)S(1)}, bf16[512,1024]{1,0:T(8,128)(2,1)S(1)}, f32[16,3,128,128]{3,2,1,0:T(8,128)S(1)}, f32[8,2,2,128]{3,2,1,0:T(2,128)S(1)}) custom-call(s32[1]{0:T(128)S(6)} %copy.93.flag_ref, f32[2,16]{1,0:T(2,128)S(1)} %pad_maximum_fusion.3.far_ref, bf16[512,3072]{1,0:T(8,128)(2,1)S(1)} %copy-done.8, ...), custom_call_target="tpu_custom_call" | custom-call | flops 5368709120 | bytes 14680064 | tf_op jit(solution)/shard_map/pallas_call | solution.py:604
  439.3 4.0 shard_map.322
  451.1 4.4 fusion.32
  459.0 6.6 %collective-permute-done.69.refs_2_ = bf16[352,1024]{1,0:T(8,128)(2,1)} collective-permute-done((bf16[352,1024]{1,0:T(8,128)(2,1)}, bf16[352,1024]{1,0:T(8,128)(2,1)}, u32[]{:S(2)}, u32[]{:S(2)}) %collective-permute-start.69) | collective-permute-done | bytes 720928 | tf_op jit(solution)/shard_map/ppermute | solution.py:283
  468.3 3.9 fusion.23
  474.2 3.8 collective-permute-done.72.refs_1_
  494.0 7.1 %collective-permute-done.79.refs_2_ = bf16[128,2816]{1,0:T(8,128)(2,1)} collective-permute-done((bf16[128,2816]{1,0:T(8,128)(2,1)}, bf16[128,2816]{1,0:T(8,128)(2,1)}, u32[]{:S(2)}, u32[]{:S(2)}) %collective-permute-start.79) | collective-permute-done | bytes 720928 | tf_op jit(solution)/shard_map/ppermute | solution.py:283
  508.6 12.3 %collective-permute-done.80 = f32[52,128]{1,0:T(8,128)S(1)} collective-permute-done((f32[52,128]{1,0:T(8,128)S(1)}, f32[52,128]{1,0:T(8,128)S(1)}, u32[]{:S(2)}, u32[]{:S(2)}) %collective-permute-start.80) | collective-permute-done | bytes 26656 | tf_op jit(solution)/shard_map/ppermute | solution.py:400
  531.0 4.6 shard_map.329
  535.7 4.3 collective-permute-done.85
  548.1 4.4 shard_map.331
  552.5 4.4 shard_map.332
  (505 shorter events, 266.3 us)
Async XLA Ops:
  21.6 25.1 %collective-permute-start.8 = (bf16[64,4096]{1,0:T(8,128)(2,1)}, bf16[64,4096]{1,0:T(8,128)(2,1)S(1)}, u32[]{:S(2)}, u32[]{:S(2)}) collective-permute-start(bf16[64,4096]{1,0:T(8,128)(2,1)} %collective-permute-done.1.refs_3_), channel_id=1, source_target_pairs={{0,1},{1,0},{2,3},{3,2},{4,5},{5,4},{6,7},{7,6},{8,9},{9,8},{10,11... | collective-permute-start | bytes 1572872 | tf_op jit(solution)/shard_map/ppermute | solution.py:283
  103.7 35.8 %collective-permute-start.22 = (bf16[640,1024]{1,0:T(8,128)(2,1)S(1)}, bf16[640,1024]{1,0:T(8,128)(2,1)S(1)}, u32[]{:S(2)}, u32[]{:S(2)}) collective-permute-start(bf16[640,1024]{1,0:T(8,128)(2,1)S(1)} %convolution_convert_fusion.4), channel_id=1, source_target_pairs={{0,2},{1,3},{2,0},{3,1},{4,6},{5,7},{6,4},{7,5},{8,10},{9,11},{10,... | collective-permute-start | bytes 3932168 | tf_op jit(solution)/shard_map/ppermute | solution.py:283
  117.4 22.2 %collective-permute-start.21 = (bf16[320,1024]{1,0:T(8,128)(2,1)S(1)}, bf16[320,1024]{1,0:T(8,128)(2,1)S(1)}, u32[]{:S(2)}, u32[]{:S(2)}) collective-permute-start(bf16[320,1024]{1,0:T(8,128)(2,1)S(1)} %convolution_convert_fusion.9), channel_id=1, source_target_pairs={{0,1},{1,0},{2,3},{3,2},{4,5},{5,4},{6,7},{7,6},{8,9},{9,8},{10,11... | collective-permute-start | bytes 1966088 | tf_op jit(solution)/shard_map/ppermute | solution.py:283
  144.6 25.2 %collective-permute-start.30 = (bf16[128,2816]{1,0:T(8,128)(2,1)S(1)}, bf16[128,2816]{1,0:T(8,128)(2,1)S(1)}, u32[]{:S(2)}, u32[]{:S(2)}) collective-permute-start(bf16[128,2816]{1,0:T(8,128)(2,1)S(1)} %collective-permute-done.25.refs_2_), channel_id=1, source_target_pairs={{0,4},{4,12},{12,20},{20,28},{28,24},{24,16},{16,8},{8,0},{1,5},{5... | collective-permute-start | bytes 2162696 | tf_op jit(solution)/shard_map/ppermute | solution.py:153
  145.1 24.8 %collective-permute-start.31 = (bf16[128,2816]{1,0:T(8,128)(2,1)S(1)}, bf16[128,2816]{1,0:T(8,128)(2,1)}, u32[]{:S(2)}, u32[]{:S(2)}) collective-permute-start(bf16[128,2816]{1,0:T(8,128)(2,1)S(1)} %collective-permute-done.26.refs_3_), channel_id=1, source_target_pairs={{4,0},{12,4},{20,12},{28,20},{24,28},{16,24},{8,16},{0,8},{5,1},{1... | collective-permute-start | bytes 2162696 | tf_op jit(solution)/shard_map/ppermute | solution.py:154
  146.7 51.9 %collective-permute-start.37 = (bf16[352,1024]{1,0:T(8,128)(2,1)}, bf16[352,1024]{1,0:T(8,128)(2,1)}, u32[]{:S(2)}, u32[]{:S(2)}) collective-permute-start(bf16[352,1024]{1,0:T(8,128)(2,1)} %dynamic-slice_bitcast_fusion.refs_1_), channel_id=1, source_target_pairs={{0,4},{4,12},{12,20},{20,28},{28,24},{24,16},{16,8},{8,0},{1,5},{5... | collective-permute-start | bytes 2162696 | tf_op jit(solution)/shard_map/ppermute | solution.py:153
  147.1 51.5 %collective-permute-start.38 = (bf16[352,1024]{1,0:T(8,128)(2,1)}, bf16[352,1024]{1,0:T(8,128)(2,1)}, u32[]{:S(2)}, u32[]{:S(2)}) collective-permute-start(bf16[352,1024]{1,0:T(8,128)(2,1)} %dynamic-slice_bitcast_fusion.refs_1_), channel_id=1, source_target_pairs={{4,0},{12,4},{20,12},{28,20},{24,28},{16,24},{8,16},{0,8},{5,1},{1... | collective-permute-start | bytes 2162696 | tf_op jit(solution)/shard_map/ppermute | solution.py:154
  149.5 30.2 %collective-permute-start.33 = (bf16[640,1024]{1,0:T(8,128)(2,1)}, bf16[640,1024]{1,0:T(8,128)(2,1)}, u32[]{:S(2)}, u32[]{:S(2)}) collective-permute-start(bf16[640,1024]{1,0:T(8,128)(2,1)} %convolution_convert_fusion.5), channel_id=1, source_target_pairs={{0,2},{1,3},{2,0},{3,1},{4,6},{5,7},{6,4},{7,5},{8,10},{9,11},{10,... | collective-permute-start | bytes 3932168 | tf_op jit(solution)/shard_map/ppermute | solution.py:283
  170.8 23.2 %collective-permute-start.34 = (bf16[128,2816]{1,0:T(8,128)(2,1)}, bf16[128,2816]{1,0:T(8,128)(2,1)S(1)}, u32[]{:S(2)}, u32[]{:S(2)}) collective-permute-start(bf16[128,2816]{1,0:T(8,128)(2,1)} %copy-done.37), channel_id=1, source_target_pairs={{0,4},{4,12},{12,20},{20,28},{28,24},{24,16},{16,8},{8,0},{1,5},{5... | collective-permute-start | bytes 2162696 | tf_op jit(solution)/shard_map/ppermute | solution.py:153
  171.2 23.0 %collective-permute-start.35 = (bf16[128,2816]{1,0:T(8,128)(2,1)}, bf16[128,2816]{1,0:T(8,128)(2,1)}, u32[]{:S(2)}, u32[]{:S(2)}) collective-permute-start(bf16[128,2816]{1,0:T(8,128)(2,1)} %collective-permute-done.31.refs_5_), channel_id=1, source_target_pairs={{4,0},{12,4},{20,12},{28,20},{24,28},{16,24},{8,16},{0,8},{5,1},{1... | collective-permute-start | bytes 2162696 | tf_op jit(solution)/shard_map/ppermute | solution.py:154
  227.9 24.1 %collective-permute-start.43 = (bf16[352,1024]{1,0:T(8,128)(2,1)S(1)}, bf16[352,1024]{1,0:T(8,128)(2,1)S(1)}, u32[]{:S(2)}, u32[]{:S(2)}) collective-permute-start(bf16[352,1024]{1,0:T(8,128)(2,1)S(1)} %collective-permute-done.41.refs_4_), channel_id=1, source_target_pairs={{0,4},{4,12},{12,20},{20,28},{28,24},{24,16},{16,8},{8,0},{1,5},{5... | collective-permute-start | bytes 2162696 | tf_op jit(solution)/shard_map/ppermute | solution.py:153
  229.5 22.6 %collective-permute-start.44 = (bf16[352,1024]{1,0:T(8,128)(2,1)S(1)}, bf16[352,1024]{1,0:T(8,128)(2,1)S(1)}, u32[]{:S(2)}, u32[]{:S(2)}) collective-permute-start(bf16[352,1024]{1,0:T(8,128)(2,1)S(1)} %collective-permute-done.42.refs_5_), channel_id=1, source_target_pairs={{4,0},{12,4},{20,12},{28,20},{24,28},{16,24},{8,16},{0,8},{5,1},{1... | collective-permute-start | bytes 2162696 | tf_op jit(solution)/shard_map/ppermute | solution.py:154
  278.9 34.4 %collective-permute-start.49 = (bf16[2,352,512]{2,1,0:T(8,128)(2,1)}, bf16[2,352,512]{2,1,0:T(8,128)(2,1)S(1)}, u32[]{:S(2)}, u32[]{:S(2)}) collective-permute-start(bf16[2,352,512]{2,1,0:T(8,128)(2,1)} %get-tuple-element.237), channel_id=1, source_target_pairs={{0,4},{4,12},{12,20},{20,28},{28,24},{24,16},{16,8},{8,0},{1,5},{5... | collective-permute-start | bytes 2162696 | tf_op jit(solution)/shard_map/ppermute | solution.py:266
  280.4 32.8 %collective-permute-start.50 = (bf16[2,352,512]{2,1,0:T(8,128)(2,1)S(1)}, bf16[2,352,512]{2,1,0:T(8,128)(2,1)S(1)}, u32[]{:S(2)}, u32[]{:S(2)}) collective-permute-start(bf16[2,352,512]{2,1,0:T(8,128)(2,1)S(1)} %get-tuple-element.238), channel_id=1, source_target_pairs={{4,0},{12,4},{20,12},{28,20},{24,28},{16,24},{8,16},{0,8},{5,1},{1... | collective-permute-start | bytes 2162696 | tf_op jit(solution)/shard_map/ppermute | solution.py:267
  280.9 32.4 %collective-permute-start.52 = (bf16[640,1024]{1,0:T(8,128)(2,1)}, bf16[640,1024]{1,0:T(8,128)(2,1)S(1)}, u32[]{:S(2)}, u32[]{:S(2)}) collective-permute-start(bf16[640,1024]{1,0:T(8,128)(2,1)} %slice.148), channel_id=1, source_target_pairs={{0,2},{1,3},{2,0},{3,1},{4,6},{5,7},{6,4},{7,5},{8,10},{9,11},{10,... | collective-permute-start | bytes 3932168 | tf_op jit(solution)/shard_map/ppermute | solution.py:283
  282.4 30.9 %collective-permute-start.51 = (bf16[320,1024]{1,0:T(8,128)(2,1)}, bf16[320,1024]{1,0:T(8,128)(2,1)S(1)}, u32[]{:S(2)}, u32[]{:S(2)}) collective-permute-start(bf16[320,1024]{1,0:T(8,128)(2,1)} %get-tuple-element.241), channel_id=1, source_target_pairs={{0,1},{1,0},{2,3},{3,2},{4,5},{5,4},{6,7},{7,6},{8,9},{9,8},{10,11... | collective-permute-start | bytes 1966088 | tf_op jit(solution)/shard_map/ppermute | solution.py:283
  317.2 29.3 %collective-permute-start.53 = (bf16[1,128,2816]{2,1,0:T(8,128)(2,1)}, bf16[1,128,2816]{2,1,0:T(8,128)(2,1)S(1)}, u32[]{:S(2)}, u32[]{:S(2)}) collective-permute-start(bf16[1,128,2816]{2,1,0:T(8,128)(2,1)} %get-tuple-element.245), channel_id=1, source_target_pairs={{0,4},{4,12},{12,20},{20,28},{28,24},{24,16},{16,8},{8,0},{1,5},{5... | collective-permute-start | bytes 2162696 | tf_op jit(solution)/shard_map/ppermute | solution.py:266
  318.8 27.7 %collective-permute-start.54 = (bf16[1,128,2816]{2,1,0:T(8,128)(2,1)}, bf16[1,128,2816]{2,1,0:T(8,128)(2,1)S(1)}, u32[]{:S(2)}, u32[]{:S(2)}) collective-permute-start(bf16[1,128,2816]{2,1,0:T(8,128)(2,1)} %get-tuple-element.246), channel_id=1, source_target_pairs={{4,0},{12,4},{20,12},{28,20},{24,28},{16,24},{8,16},{0,8},{5,1},{1... | collective-permute-start | bytes 2162696 | tf_op jit(solution)/shard_map/ppermute | solution.py:267
  321.2 30.6 %collective-permute-start.56 = (bf16[2,352,512]{2,1,0:T(8,128)(2,1)}, bf16[2,352,512]{2,1,0:T(8,128)(2,1)}, u32[]{:S(2)}, u32[]{:S(2)}) collective-permute-start(bf16[2,352,512]{2,1,0:T(8,128)(2,1)} %get-tuple-element.250), channel_id=1, source_target_pairs={{0,4},{4,12},{12,20},{20,28},{28,24},{24,16},{16,8},{8,0},{1,5},{5... | collective-permute-start | bytes 2162696 | tf_op jit(solution)/shard_map/ppermute | solution.py:266
  322.8 29.7 %collective-permute-start.57 = (bf16[2,352,512]{2,1,0:T(8,128)(2,1)}, bf16[2,352,512]{2,1,0:T(8,128)(2,1)}, u32[]{:S(2)}, u32[]{:S(2)}) collective-permute-start(bf16[2,352,512]{2,1,0:T(8,128)(2,1)} %get-tuple-element.251), channel_id=1, source_target_pairs={{4,0},{12,4},{20,12},{28,20},{24,28},{16,24},{8,16},{0,8},{5,1},{1... | collective-permute-start | bytes 2162696 | tf_op jit(solution)/shard_map/ppermute | solution.py:267
  346.0 29.9 %collective-permute-start.61 = (bf16[640,1024]{1,0:T(8,128)(2,1)}, bf16[640,1024]{1,0:T(8,128)(2,1)S(1)}, u32[]{:S(2)}, u32[]{:S(2)}) collective-permute-start(bf16[640,1024]{1,0:T(8,128)(2,1)} %get-tuple-element.255), channel_id=1, source_target_pairs={{0,2},{1,3},{2,0},{3,1},{4,6},{5,7},{6,4},{7,5},{8,10},{9,11},{10,... | collective-permute-start | bytes 3932168 | tf_op jit(solution)/shard_map/ppermute | solution.py:283
  346.5 49.9 %collective-permute-start.60 = (bf16[320,1024]{1,0:T(8,128)(2,1)}, bf16[320,1024]{1,0:T(8,128)(2,1)}, u32[]{:S(2)}, u32[]{:S(2)}) collective-permute-start(bf16[320,1024]{1,0:T(8,128)(2,1)} %get-tuple-element.254), channel_id=1, source_target_pairs={{0,1},{1,0},{2,3},{3,2},{4,5},{5,4},{6,7},{7,6},{8,9},{9,8},{10,11... | collective-permute-start | bytes 1966088 | tf_op jit(solution)/shard_map/ppermute | solution.py:283
  350.2 34.2 %collective-permute-start.58 = (bf16[2,128,2816]{2,1,0:T(8,128)(2,1)}, bf16[2,128,2816]{2,1,0:T(8,128)(2,1)S(1)}, u32[]{:S(2)}, u32[]{:S(2)}) collective-permute-start(bf16[2,128,2816]{2,1,0:T(8,128)(2,1)} %get-tuple-element.258), channel_id=1, source_target_pairs={{0,4},{4,12},{12,20},{20,28},{28,24},{24,16},{16,8},{8,0},{1,5},{5... | collective-permute-start | bytes 4325384 | tf_op jit(solution)/shard_map/ppermute | solution.py:266
  351.8 34.0 %collective-permute-start.59 = (bf16[2,128,2816]{2,1,0:T(8,128)(2,1)}, bf16[2,128,2816]{2,1,0:T(8,128)(2,1)}, u32[]{:S(2)}, u32[]{:S(2)}) collective-permute-start(bf16[2,128,2816]{2,1,0:T(8,128)(2,1)} %get-tuple-element.259), channel_id=1, source_target_pairs={{4,0},{12,4},{20,12},{28,20},{24,28},{16,24},{8,16},{0,8},{5,1},{1... | collective-permute-start | bytes 4325384 | tf_op jit(solution)/shard_map/ppermute | solution.py:267
  375.9 22.2 %collective-permute-start.62 = (bf16[320,1024]{1,0:T(8,128)(2,1)S(1)}, bf16[320,1024]{1,0:T(8,128)(2,1)S(1)}, u32[]{:S(2)}, u32[]{:S(2)}) collective-permute-start(bf16[320,1024]{1,0:T(8,128)(2,1)S(1)} %slice.130), channel_id=1, source_target_pairs={{0,1},{1,0},{2,3},{3,2},{4,5},{5,4},{6,7},{7,6},{8,9},{9,8},{10,11... | collective-permute-start | bytes 1966088 | tf_op jit(solution)/shard_map/ppermute | solution.py:283
  390.6 40.2 %collective-permute-start.63 = (bf16[2,352,512]{2,1,0:T(8,128)(2,1)S(1)}, bf16[2,352,512]{2,1,0:T(8,128)(2,1)S(1)}, u32[]{:S(2)}, u32[]{:S(2)}) collective-permute-start(bf16[2,352,512]{2,1,0:T(8,128)(2,1)S(1)} %get-tuple-element.264), channel_id=1, source_target_pairs={{0,4},{4,12},{12,20},{20,28},{28,24},{24,16},{16,8},{8,0},{1,5},{5... | collective-permute-start | bytes 2162696 | tf_op jit(solution)/shard_map/ppermute | solution.py:266
  391.2 39.6 %collective-permute-start.64 = (bf16[2,352,512]{2,1,0:T(8,128)(2,1)S(1)}, bf16[2,352,512]{2,1,0:T(8,128)(2,1)S(1)}, u32[]{:S(2)}, u32[]{:S(2)}) collective-permute-start(bf16[2,352,512]{2,1,0:T(8,128)(2,1)S(1)} %get-tuple-element.265), channel_id=1, source_target_pairs={{4,0},{12,4},{20,12},{28,20},{24,28},{16,24},{8,16},{0,8},{5,1},{1... | collective-permute-start | bytes 2162696 | tf_op jit(solution)/shard_map/ppermute | solution.py:267
  395.8 43.4 %collective-permute-start.66 = (bf16[2,128,2816]{2,1,0:T(8,128)(2,1)S(1)}, bf16[2,128,2816]{2,1,0:T(8,128)(2,1)S(1)}, u32[]{:S(2)}, u32[]{:S(2)}) collective-permute-start(bf16[2,128,2816]{2,1,0:T(8,128)(2,1)S(1)} %get-tuple-element.268), channel_id=1, source_target_pairs={{0,4},{4,12},{12,20},{20,28},{28,24},{24,16},{16,8},{8,0},{1,5},{5... | collective-permute-start | bytes 4325384 | tf_op jit(solution)/shard_map/ppermute | solution.py:266
  396.4 42.9 %collective-permute-start.67 = (bf16[2,128,2816]{2,1,0:T(8,128)(2,1)S(1)}, bf16[2,128,2816]{2,1,0:T(8,128)(2,1)S(1)}, u32[]{:S(2)}, u32[]{:S(2)}) collective-permute-start(bf16[2,128,2816]{2,1,0:T(8,128)(2,1)S(1)} %get-tuple-element.269), channel_id=1, source_target_pairs={{4,0},{12,4},{20,12},{28,20},{24,28},{16,24},{8,16},{0,8},{5,1},{1... | collective-permute-start | bytes 4325384 | tf_op jit(solution)/shard_map/ppermute | solution.py:267
  403.7 27.1 %collective-permute-start.65 = (bf16[8,64,1024]{2,1,0:T(8,128)(2,1)S(1)}, bf16[8,64,1024]{2,1,0:T(8,128)(2,1)S(1)}, u32[]{:S(2)}, u32[]{:S(2)}) collective-permute-start(bf16[8,64,1024]{2,1,0:T(8,128)(2,1)S(1)} %bitcast.137), channel_id=1, source_target_pairs={{0,1},{1,0},{2,3},{3,2},{4,5},{5,4},{6,7},{7,6},{8,9},{9,8},{10,11... | collective-permute-start | bytes 3145736 | tf_op jit(solution)/shard_map/ppermute | solution.py:283
  443.3 34.8 %collective-permute-start.72 = (bf16[2,128,2816]{2,1,0:T(8,128)(2,1)}, bf16[2,128,2816]{2,1,0:T(8,128)(2,1)}, u32[]{:S(2)}, u32[]{:S(2)}) collective-permute-start(bf16[2,128,2816]{2,1,0:T(8,128)(2,1)} %get-tuple-element.286), channel_id=1, source_target_pairs={{0,4},{4,12},{12,20},{20,28},{28,24},{24,16},{16,8},{8,0},{1,5},{5... | collective-permute-start | bytes 4325384 | tf_op jit(solution)/shard_map/ppermute | solution.py:266
  443.9 35.0 %collective-permute-start.73 = (bf16[2,128,2816]{2,1,0:T(8,128)(2,1)}, bf16[2,128,2816]{2,1,0:T(8,128)(2,1)}, u32[]{:S(2)}, u32[]{:S(2)}) collective-permute-start(bf16[2,128,2816]{2,1,0:T(8,128)(2,1)} %get-tuple-element.287), channel_id=1, source_target_pairs={{4,0},{12,4},{20,12},{28,20},{24,28},{16,24},{8,16},{0,8},{5,1},{1... | collective-permute-start | bytes 4325384 | tf_op jit(solution)/shard_map/ppermute | solution.py:267
  (162 other events, 1664.2 us)
